TPU v7x, 32 devices: a whole 2x2x4 slice. The times are simulated.
32 devices in a mesh: groups: 2 (over y), patch: 8 (over z, x), head: 2 (over core).
Axes of the slice: x: 2, y: 2, z: 4, core: 2. Of those that a mesh axis runs over, the one named last changes fastest.
Arguments:
- queries: bfloat16 [2, 256, 1536], P(None, ('groups', 'patch'), 'head'), parts along dimension 1, may hold values from -15 to 15
- stale_pairs: bfloat16 [2, 320, 1536], P(None, ('groups', 'patch'), 'head'), parts along dimension 1, may hold values from -6 to 6
- step_pairs: bfloat16 [2, 2, 320, 1536], P(None, None, ('groups', 'patch'), 'head'), parts along dimension 2, may hold values from -6 to 6
- hidden: bfloat16 [256, 3072], P(('groups', 'patch'), 'head'), parts along dimension 0, may hold values from -3 to 3
- out_weight: bfloat16 [1536, 3072], P('head'), may hold values from -0.15625 to 0.15625
- gate_table: bfloat16 [28, 3072], replicated, may hold values from -4 to 4
- t_index: int32 [4], P('groups'), parts along dimension 0, may hold values from 0 to 27
- text_len: int32 [2], P('groups'), parts along dimension 0, may hold values from 1 to 32
Outputs:
- final_latents: bfloat16 [256, 3072], P(('groups', 'patch', 'head')), parts along dimension 0
There are 2 independent parts, one for each index of `groups`. A program takes and returns all parts, laid end to end along the dimension named above; an argument that names none is the same for every part. Nothing has to cross between parts.
All inputs are finite; a program needn't handle non-finite values.
Results may differ from a plain program's by a relative error of at most 0.0065.
Values may be sent and summed in bfloat16 or wider, within the bound.
No kernel may reach another device: no remote copies, remote signals or barrier semaphores. Data moves between devices by JAX's collectives and lax.ppermute only.
A program may use at most 128 MiB of HBM per device.

v0:
```python
import jax
import jax.numpy as jnp
from jax import lax
from jax.sharding import PartitionSpec as P

HDIM = 128


def attend(query_rows, key_rows, value_rows, usable):
    count = query_rows.shape[0]
    total = key_rows.shape[0]
    heads_here = query_rows.shape[1] // HDIM
    qs = query_rows.reshape(count, heads_here, HDIM)
    ks = key_rows.reshape(total, heads_here, HDIM)
    vs = value_rows.reshape(total, heads_here, HDIM)
    scores = jnp.einsum("qhd,khd->hqk", qs, ks, preferred_element_type=jnp.float32) * (
        1.0 / HDIM**0.5
    )
    scores = jnp.where(usable[None, None, :], scores, jnp.float32(-1e30))
    top = jnp.max(scores, axis=2, keepdims=True)
    expo = jnp.exp(scores - top)
    weights = (expo / jnp.sum(expo, axis=2, keepdims=True)).astype(jnp.bfloat16)
    mixed = jnp.einsum("hqk,khd->qhd", weights, vs, preferred_element_type=jnp.float32)
    return mixed.reshape(count, heads_here * HDIM).astype(jnp.bfloat16)


def per_device(queries, stale_pairs, step_pairs, hidden, out_weight, gate_table, t_index, text_len):
    strip_rows = stale_pairs.shape[1]
    lat_rows = queries.shape[1]
    text_rows = strip_rows - lat_rows
    strip_count = lax.axis_size("patch")
    strip_index = lax.axis_index("patch")
    head_index = lax.axis_index("head")
    head_count = lax.axis_size("head")
    total = strip_rows * strip_count
    positions = jnp.arange(total, dtype=jnp.int32)
    within = positions % strip_rows
    holder = positions // strip_rows
    usable = (within < lat_rows) | (holder * text_rows + within - lat_rows < text_len[0])
    old_sets = lax.all_gather(stale_pairs, "patch", axis=1, tiled=True)
    first_sets = lax.all_gather(step_pairs[0], "patch", axis=1, tiled=True)
    remote_sets = (old_sets, first_sets)
    model_width = out_weight.shape[1]
    col_width = model_width // head_count

    def project(section):
        pairs = lax.dynamic_update_slice_in_dim(
            remote_sets[section], step_pairs[section], strip_index * strip_rows, axis=1
        )
        attended = attend(queries[section], pairs[0], pairs[1], usable)
        return jnp.dot(attended, out_weight, preferred_element_type=jnp.float32)

    state = hidden.astype(jnp.float32)
    first_proj = lax.psum_scatter(
        project(0).astype(jnp.bfloat16), "head", scatter_dimension=1, tiled=True
    ).astype(jnp.float32)
    gate_row = gate_table[t_index[0]].astype(jnp.float32)
    state = (
        state
        + lax.dynamic_slice_in_dim(gate_row, head_index * col_width, col_width, 0)[None, :]
        * first_proj
    )
    moved = lax.all_to_all(state, "head", split_axis=0, concat_axis=1, tiled=True)
    last_proj = lax.psum_scatter(project(1), "head", scatter_dimension=0, tiled=True)
    gate_full = gate_table[t_index[1]].astype(jnp.float32)
    return (moved + gate_full[None, :] * last_proj).astype(jnp.bfloat16)


def solution(mesh):
    return jax.shard_map(
        per_device,
        mesh=mesh,
        in_specs=(
            P(None, ("groups", "patch"), "head"),
            P(None, ("groups", "patch"), "head"),
            P(None, None, ("groups", "patch"), "head"),
            P(("groups", "patch"), "head"),
            P("head", None),
            P(),
            P("groups"),
            P("groups"),
        ),
        out_specs=P(("groups", "patch", "head"), None),
        check_vma=False,
    )
```

profile of v0, /device:TPU:0, one launch (start us, length us, event | category | flops | bytes accessed | tf_op | source)
XLA Modules:
  0.0 112.1 jit_solution(2523433137556579357)
XLA Ops:
  6.5 0.9 slice_bitcast_fusion
  7.4 32.9 %all-gather = bf16[1,2,160,768]{3,1,0,2:T(2,128)(2,1)S(1)} all-gather(bf16[1,2,20,768]{3,1,0,2:T(2,128)(2,1)S(1)} %slice_bitcast_fusion), channel_id=2, replica_groups=mesh['groups'=2,'patch'=8,'head'=2] {'patch'}, dimensions={2}, use_global_device_ids=true | all-gather | bytes 552960 | tf_op jit(solution)/shard_map/all_gather | solution.py:41
  40.3 31.4 %all_gather.6 = bf16[2,160,768]{2,0,1:T(2,128)(2,1)S(1)} all-gather(bf16[2,20,768]{2,0,1:T(2,128)(2,1)} %param.9), channel_id=1, replica_groups=mesh['groups'=2,'patch'=8,'head'=2] {'patch'}, dimensions={1}, use_global_device_ids=true | all-gather | bytes 552960 | tf_op jit(solution)/shard_map/all_gather | solution.py:40
  71.8 0.8 fusion.33
  72.5 0.1 reshape_squeeze.20
  73.3 1.0 bitcast_dynamic-update-slice_fusion
  74.2 5.2 %slice_reduce_fusion.1 = (bf16[160,768]{1,0:T(8,128)(2,1)S(1)}, bf16[160,768]{1,0:T(8,128)(2,1)S(1)}, bf16[160,768]{1,0:T(8,128)(2,1)S(1)}, bf16[160,768]{1,0:T(8,128)(2,1)S(1)}) fusion(bf16[2,160,768]{2,0,1:T(2,128)(2,1)S(1)} %get-tuple-element.9, bf16[2,160,768]{2,0,1:T(2,128)(2,1)S(1)} %get-tuple-element.10), kind=kLoop, calls=%fused_computation.18 | loop fusion | bytes 1966080 | tf_op jit(solution)/shard_map/slice | solution.py:50
  79.4 0.4 fusion.35
  79.8 0.2 fusion.10
  80.0 3.7 %convolution_convert_fusion = bf16[16,3072]{1,0:T(8,128)(2,1)} fusion(bf16[768,3072]{1,0:T(8,128)(2,1)} %param.12, bf16[6,2,8,128]{3,2,1,0:T(8,128)(2,1)S(1)} %fusion.10), kind=kOutput, calls=%fused_computation.2 | convolution fusion | flops 75546624 | bytes 4841472 | tf_op jit(solution)/shard_map/dot_general | solution.py:51
  83.8 0.0 reduce-scatter.3.cloned.1.call-update
  83.8 0.0 reduce-scatter.5.cloned.1.call-start
  83.9 0.1 reshape_squeeze.23
  83.9 0.4 fusion.36
  84.3 0.2 fusion.11
  84.6 3.7 %fusion.22 = f32[16,3072]{1,0:T(8,128)} fusion(bf16[768,3072]{1,0:T(8,128)(2,1)} %param.12, bf16[6,2,8,128]{3,2,1,0:T(8,128)(2,1)S(1)} %fusion.11), kind=kOutput, calls=%fused_computation.38 | convolution fusion | flops 75497472 | bytes 4939776 | tf_op jit(solution)/shard_map/dot_general | solution.py:51
  88.3 0.6 fusion.34
  92.6 0.8 dynamic-slice_convert_fusion
  93.4 0.8 fusion.29
  94.3 0.0 reduce-scatter.3.cloned.1.call-done
  94.3 0.8 add_bitcast_fusion
  95.1 3.8 %all_to_all.19 = f32[2,8,1536]{2,1,0:T(8,128)S(1)} all-to-all(f32[2,8,1536]{2,1,0:T(8,128)S(1)} %add_bitcast_fusion), channel_id=1, replica_groups=mesh['groups'=2,'patch'=8,'head'=2] {'head'}, dimensions={0} | all-to-all | bytes 196608 | tf_op jit(solution)/shard_map/all_to_all | solution.py:63
  98.9 4.8 %reduce-scatter.5.cloned.1.call-done = f32[8,3072]{1,0:T(8,128)} async-done(((f32[16,3072]{1,0:T(8,128)}), f32[8,3072]{1,0:T(8,128)}) %reduce-scatter.5.cloned.1.call-update) | async-done | bytes 98320 | tf_op jit(solution)/shard_map/reduce_scatter | solution.py:64
  103.7 1.5 %add_convert_fusion = bf16[8,3072]{1,0:T(8,128)(2,1)} fusion(f32[8,3072]{1,0:T(8,128)S(1)} %bitcast.74, f32[8,3072]{1,0:T(8,128)} %reduce-scatter.5.cloned.1.call-done, f32[3072]{0:T(1024)S(1)} %bitcast.75), kind=kLoop, calls=%fused_computation.29 | loop fusion | flops 73728 | bytes 258048 | tf_op jit(solution)/shard_map/convert_element_type | solution.py:66
  (7 shorter events, 0.0 us)
Async XLA Ops:
  6.5 87.7 %reduce-scatter.3.cloned.1.call-start = ((), (), s32[]{:S(2)}) async-start(), calls=%async_computation.3 | async-start | bytes 147456 | tf_op jit(solution)/shard_map/reduce_scatter | solution.py:54
  80.0 8.3 %copy-start.1 = (s32[2]{0:T(128)S(1)}, s32[2]{0:T(128)}, u32[]{:S(2)}) copy-start(s32[2]{0:T(128)} %param.14) | copy-start | bytes 28
  80.0 14.2 %copy-start = (bf16[16,1536]{1,0:T(8,128)(2,1)S(1)}, bf16[16,1536]{1,0:T(8,128)(2,1)}, u32[]{:S(2)}) copy-start(bf16[16,1536]{1,0:T(8,128)(2,1)} %param.11) | copy-start | bytes 147460
  83.8 19.9 %reduce-scatter.5.cloned.1.call-start = ((), (), s32[]{:S(2)}) async-start(), calls=%async_computation.4 | async-start | bytes 294912 | tf_op jit(solution)/shard_map/reduce_scatter | solution.py:64
Sparse Core Ops, SparseCore 0:
  83.9 8.7 reduce-scatter.2
  94.9 8.7 reduce-scatter.4
where the time goes:
time: 113 us; the launch traced here: 112 us
  blocking collectives  68.2 us (60%)
  between operations  17.8 us (16%)
  matrix products  8.77 us (8%)
  local copies, waits for them, and re-layouts  8.44 us (7%)
  waiting for transfers between devices  4.83 us (4%)
  other arithmetic  4.01 us (4%)
    all_gather x1, blocking collectives, per_device(): first_sets = lax.all_gather(step_pairs[0], 'patch', axis=1, tiled=True)  32.9 us
    all_gather x1, blocking collectives, per_device(): old_sets = lax.all_gather(stale_pairs, 'patch', axis=1, tiled=True)  31.4 us
    dot_general x2, matrix products, project(): return jnp.dot(attended, out_weight, preferred_element_type=jnp.float32)  7.5 us
    slice x2, local copies, waits for them, and re-layouts, project(): attended = attend(queries[section], pairs[0], pairs[1], usable)  5.91 us
    reduce_scatter x1, waiting for transfers between devices, per_device(): lax.psum_scatter(project(1), 'head', scatter_dimension=0, tiled=True)  4.78 us
    all_to_all x1, blocking collectives, per_device(): lax.all_to_all(state, 'head', split_axis=0, concat_axis=1, tiled=True)  3.79 us
  transfers between devices with their start and end apart: 2, of which 1 were waited for; matrix products, arithmetic and copies ran while one was open for 7% of the time, Pallas kernels for 0%

commit v1 on v0

v1 whole, which is shorter than its diff:
```python
import functools

import jax
import jax.numpy as jnp
import numpy as np
from jax import lax
from jax.experimental import pallas as pl
from jax.experimental.pallas import tpu as pltpu
from jax.sharding import PartitionSpec as P

HDIM = 128
LANES = 128
TILE = 16
MASKED = -1e30
VMEM_LIMIT = 24 * 1024 * 1024


def round_up(value, step):
    return (value + step - 1) // step * step


def attention_kernel(sizes, bias_ref, own_ref, local_ref, pair_ref, *refs):
    set_rows, query_rows, columns = sizes
    others, (mine_ref, back_ref) = refs[:-2], refs[-2:]
    pair_rows = 2 * set_rows
    fresh_at = query_rows
    heads = own_ref.shape[1] // HDIM
    scale = 1.0 / HDIM**0.5
    per_class = query_rows // 2
    bias = jnp.concatenate(
        [jnp.broadcast_to(bias_ref[c : c + 1, :], (per_class, columns)) for c in range(4)], axis=0
    )
    for head in range(heads):
        lanes = slice(head * HDIM, (head + 1) * HDIM)
        rows = [own_ref[:, lanes], pair_ref[:pair_rows, lanes]]
        rows += [ref[:, lanes] for ref in others]
        rows += [local_ref[fresh_at:, lanes], pair_ref[pair_rows + fresh_at :, lanes]]
        filled = sum(r.shape[0] for r in rows)
        if filled < columns:
            rows.append(jnp.zeros((columns - filled, HDIM), jnp.bfloat16))
        keys = jnp.concatenate(rows, axis=0)
        queries = jnp.concatenate(
            [local_ref[:fresh_at, lanes], pair_ref[pair_rows : pair_rows + fresh_at, lanes]], axis=0
        )
        scores = lax.dot_general(
            queries, keys, (((1,), (1,)), ((), ())), preferred_element_type=jnp.float32
        )
        scores = scores * scale + bias
        top = jnp.max(scores, axis=1, keepdims=True)
        expo = jnp.exp(scores - top)
        weights = expo / jnp.sum(expo, axis=1, keepdims=True)
        weights = pltpu.roll(weights, 1, 1).astype(jnp.bfloat16)
        mixed = jnp.dot(weights, keys, preferred_element_type=jnp.float32).astype(jnp.bfloat16)
        mine_ref[:, lanes] = mixed[:query_rows]
        back_ref[:, lanes] = mixed[query_rows:]


def gated(attended, weight, gates):
    strip = attended.shape[0] // 2
    projected = jnp.dot(attended, weight, preferred_element_type=jnp.float32)
    return gates[0:1, :] * projected[:strip] + gates[1:2, :] * projected[strip:]


def first_half_kernel(place_ref, attended_ref, weight_ref, gates_ref, hidden_ref, out_ref):
    depth = attended_ref.shape[1]
    width = hidden_ref.shape[1]
    rows = pl.ds(pl.multiple_of(place_ref[0] * depth, depth), depth)
    out_ref[...] = gated(attended_ref[...], weight_ref[rows, :], gates_ref[...])
    lanes = pl.ds(pl.multiple_of(place_ref[1] * width, LANES), width)
    out_ref[:, lanes] += hidden_ref[...].astype(jnp.float32)


def second_half_kernel(place_ref, attended_ref, weight_ref, gates_ref, sum_ref, keep_ref, send_ref, total):
    depth = attended_ref.shape[1]
    half = keep_ref.shape[0]
    rows = pl.ds(pl.multiple_of((1 - place_ref[0]) * depth, depth), depth)
    total[...] = sum_ref[...] + gated(attended_ref[...], weight_ref[rows, :], gates_ref[...])
    core = place_ref[1]
    keep_ref[...] = total[pl.ds(pl.multiple_of(core * half, half), half), :]
    send_ref[...] = total[pl.ds(pl.multiple_of((1 - core) * half, half), half), :].astype(jnp.bfloat16)


def per_device(queries, stale_pairs, step_pairs, hidden, out_weight, gate_table, t_index, text_len):
    strips = lax.axis_size("patch")
    strip = lax.axis_index("patch")
    core = lax.axis_index("head")
    strip_rows = stale_pairs.shape[1]
    lat_rows = queries.shape[1]
    text_rows = strip_rows - lat_rows
    width = queries.shape[2]
    half = width // 2
    side = strip % 2
    set_rows = 2 * strip_rows
    query_rows = 2 * lat_rows

    def interleaved(pairs):
        return pairs.transpose(1, 0, 2).reshape(set_rows, width)

    def near(rows):
        return jnp.where(side == 0, rows[:, :half], rows[:, half:])

    def far(rows):
        return jnp.where(side == 0, rows[:, half:], rows[:, :half])

    remote = jnp.concatenate([interleaved(stale_pairs), interleaved(step_pairs[0])], axis=0)
    extra = jnp.concatenate([queries.reshape(query_rows, width), interleaved(step_pairs[1])], axis=0)

    def to(rows, flip):
        return lax.ppermute(rows, "patch", [(i, i ^ flip) for i in range(strips)])

    own, other = near(remote), far(remote)
    local = near(extra)
    held = {0: own}
    bit = strips // 2
    pair = None
    while bit > 1:
        arrived = {bit: to(own, bit), bit + 1: to(other, bit + 1)}
        if pair is None:
            pair = to(jnp.concatenate([other, far(extra)], axis=0), 1)
        for flip, block in held.items():
            if flip > 1:
                arrived[flip + bit] = to(block, bit)
        held.update(arrived)
        bit //= 2
    flips = sorted(flip for flip in held if flip > 1)
    blocks = [0, 1] + flips

    filled = 2 * set_rows * len(blocks) + 2 * set_rows
    columns = round_up(filled, LANES)
    column = np.arange(columns)
    in_blocks = column < 2 * set_rows * len(blocks)
    block = np.minimum(column // (2 * set_rows), len(blocks) - 1)
    within = column % (2 * set_rows)
    flip = np.where(in_blocks, np.asarray(blocks)[block], within // set_rows)
    kind = np.where(in_blocks, within // set_rows, np.where(column < filled, 2, 3))
    token = (within % set_rows) // 2
    whose, step = np.asarray([0, 0, 1, 1])[:, None], np.asarray([0, 1, 0, 1])[:, None]
    wanted = np.where(flip == whose, step + 1, step)
    chosen = (within % 2 == 0) & (kind == wanted)
    holder = strip ^ jnp.asarray(flip, jnp.int32)
    live = (token < lat_rows) | (holder * text_rows + (token - lat_rows) < text_len[0])
    bias = jnp.where(chosen & live[None, :], jnp.float32(0.0), jnp.float32(MASKED))

    attended_shape = jax.ShapeDtypeStruct((query_rows, half), jnp.bfloat16)
    mine, back = pl.pallas_call(
        functools.partial(attention_kernel, (set_rows, query_rows, columns)),
        out_shape=(attended_shape, attended_shape),
        compiler_params=pltpu.CompilerParams(vmem_limit_bytes=VMEM_LIMIT),
    )(bias, own, local, pair, *[held[flip] for flip in flips])
    returned = to(back, 1)

    model = out_weight.shape[1]
    place = jnp.stack([side, core]).astype(jnp.int32)
    gates = gate_table[t_index].astype(jnp.float32)
    smem = pl.BlockSpec(memory_space=pltpu.SMEM)
    vmem = pl.BlockSpec(memory_space=pltpu.VMEM)
    partial_sum = pl.pallas_call(
        first_half_kernel,
        out_shape=jax.ShapeDtypeStruct((lat_rows, model), jnp.float32),
        in_specs=[smem, vmem, vmem, vmem, vmem],
        out_specs=vmem,
        compiler_params=pltpu.CompilerParams(vmem_limit_bytes=VMEM_LIMIT),
    )(place, mine, out_weight, gates, hidden)
    keep, send = pl.pallas_call(
        second_half_kernel,
        out_shape=(
            jax.ShapeDtypeStruct((lat_rows // 2, model), jnp.float32),
            jax.ShapeDtypeStruct((lat_rows // 2, model), jnp.bfloat16),
        ),
        in_specs=[smem, vmem, vmem, vmem, vmem],
        out_specs=(vmem, vmem),
        scratch_shapes=[pltpu.VMEM((lat_rows, model), jnp.float32)],
        compiler_params=pltpu.CompilerParams(vmem_limit_bytes=VMEM_LIMIT),
    )(place, returned, out_weight, gates, partial_sum)
    received = lax.ppermute(send, "head", [(0, 1), (1, 0)])
    return (keep + received.astype(jnp.float32)).astype(jnp.bfloat16)


def solution(mesh):
    return jax.shard_map(
        per_device,
        mesh=mesh,
        in_specs=(
            P(None, ("groups", "patch"), "head"),
            P(None, ("groups", "patch"), "head"),
            P(None, None, ("groups", "patch"), "head"),
            P(("groups", "patch"), "head"),
            P("head", None),
            P(),
            P("groups"),
            P("groups"),
        ),
        out_specs=P(("groups", "patch", "head"), None),
        check_vma=False,
    )
```

time: 113 us -> 32.1 us (0.28)
  blocking collectives: 68.2 us -> 0 us
  between operations: 17.8 us -> 0.78 us
  starting transfers between devices: 0.04 us -> 11.8 us
  matrix products: 8.77 us -> 0 us
  Pallas kernels: 0 us -> 3.72 us
  local copies, waits for them, and re-layouts: 8.44 us -> 6.86 us
    all_gather x2 -> x0, blocking collectives: 64.4 us -> none  [the longest x1 32.9 us: per_device(): first_sets = lax.all_gather(step_pairs[0], 'patch', axis=1, tiled=True)]
    ppermute x0 -> x9, starting transfers between devices: none -> 11.8 us  [the longest x8 11.7 us: to(): return lax.ppermute(rows, 'patch', [(i, i ^ flip) for i in range(strips)])]
    dot_general x4 -> x0, matrix products: 7.96 us -> none  [the longest x2 7.5 us: project(): return jnp.dot(attended, out_weight, preferred_element_type=jnp.float32)]
    slice x4 -> x0, local copies, waits for them, and re-layouts: 7.37 us -> none  [the longest x2 5.91 us: project(): attended = attend(queries[section], pairs[0], pairs[1], usable)]
    reduce_scatter x2 -> x0, waiting for transfers between devices: 4.8 us -> none  [the longest x1 4.78 us: per_device(): lax.psum_scatter(project(1), 'head', scatter_dimension=0, tiled=True)]
    ppermute x0 -> x9, waiting for transfers between devices: none -> 4.8 us  [the longest x8 3.58 us: to(): return lax.ppermute(rows, 'patch', [(i, i ^ flip) for i in range(strips)])]
    unnamed x4 -> x9, local copies, waits for them, and re-layouts: 0.01 us -> 4.38 us
    all_to_all x1 -> x0, blocking collectives: 3.79 us -> none  [per_device(): lax.all_to_all(state, 'head', split_axis=0, concat_axis=1, tiled=True)]
  transfers between devices with their start and end apart: 2 -> 9, of which waited for: 1 -> 3; matrix products, arithmetic and copies ran while one was open for 7% -> 11% of each run, Pallas kernels for 0% -> 3%
where the time goes in v1:
time: 32.1 us; the launch traced here: 31.6 us
  starting transfers between devices  11.8 us (37%)
  local copies, waits for them, and re-layouts  6.86 us (21%)
  waiting for transfers between devices  4.8 us (15%)
  Pallas kernels  3.72 us (12%)
  other arithmetic  3.68 us (11%)
  between operations  0.78 us (2%)
    ppermute x8, starting transfers between devices, to(): return lax.ppermute(rows, 'patch', [(i, i ^ flip) for i in range(strips)])  11.7 us
    unnamed x9, local copies, waits for them, and re-layouts  4.38 us
    ppermute x8, waiting for transfers between devices, to(): return lax.ppermute(rows, 'patch', [(i, i ^ flip) for i in range(strips)])  3.58 us
    pallas_call x1, Pallas kernels, per_device(): pl.pallas_call(functools.partial(attention_kernel, (set_rows, query_rows,...  1.57 us
    ppermute x1, waiting for transfers between devices, per_device(): received = lax.ppermute(send, 'head', [(0, 1), (1, 0)])  1.22 us
    pallas_call x1, Pallas kernels, per_device(): pl.pallas_call(second_half_kernel, out_shape=(jax.ShapeDtypeStruct((lat_r...  1.08 us
    pallas_call x1, Pallas kernels, per_device(): pl.pallas_call(first_half_kernel, out_shape=jax.ShapeDtypeStruct((lat_row...  1.08 us
    reshape x3, local copies, waits for them, and re-layouts, interleaved(): return pairs.transpose(1, 0, 2).reshape(set_rows, width)  0.95 us
  transfers between devices with their start and end apart: 9, of which 3 were waited for; matrix products, arithmetic and copies ran while one was open for 11% of the time, Pallas kernels for 3%

profile of v1, /device:TPU:0, one launch (start us, length us, event | category | flops | bytes accessed | tf_op | source)
XLA Modules:
  0.0 31.6 jit_solution(2593536031308780898)
XLA Ops:
  0.0 0.9 %reshape.13 = bf16[40,768]{1,0:T(8,128)(2,1)S(1)} reshape(bf16[20,2,768]{2,1,0:T(2,128)(2,1)} %bitcast.14) | data formatting | bytes 122880 | tf_op jit(solution)/shard_map/reshape | solution.py:97
  0.9 0.9 %slice_bitcast_fusion = (bf16[20,2,768]{2,1,0:T(2,128)(2,1)S(1)}, bf16[20,2,768]{2,1,0:T(2,128)(2,1)S(1)}) fusion(bf16[2,2,20,768]{3,1,2,0:T(2,128)(2,1)} %param.14), kind=kLoop, calls=%fused_computation.5 | loop fusion | bytes 245760 | tf_op jit(solution)/shard_map/transpose | solution.py:97
  1.9 3.1 %collective-permute-start.1 = (bf16[80,384]{1,0:T(8,128)(2,1)S(1)}, bf16[80,384]{1,0:T(8,128)(2,1)S(1)}, u32[]{:S(2)}, u32[]{:S(2)}) collective-permute-start(bf16[80,384]{1,0:T(8,128)(2,1)S(1)} %get-tuple-element.14.own_ref), channel_id=1, source_target_pairs={{0,4},{2,6},{4,0},{6,2},{8,12},{10,14},{12,8},{14,10},{1,5},{3,7},... | collective-permute-start | bytes 184328 | tf_op jit(solution)/shard_map/ppermute | solution.py:109
  5.0 2.6 %collective-permute-start.3 = (bf16[80,384]{1,0:T(8,128)(2,1)S(1)}, bf16[80,384]{1,0:T(8,128)(2,1)S(1)}, u32[]{:S(2)}, u32[]{:S(2)}) collective-permute-start(bf16[80,384]{1,0:T(8,128)(2,1)S(1)} %get-tuple-element.14.own_ref), channel_id=1, source_target_pairs={{0,8},{2,10},{4,12},{6,14},{8,0},{10,2},{12,4},{14,6},{1,9},{3,11}... | collective-permute-start | bytes 184328 | tf_op jit(solution)/shard_map/ppermute | solution.py:109
  7.6 1.4 %collective-permute-start.2 = (bf16[80,384]{1,0:T(8,128)(2,1)S(1)}, bf16[80,384]{1,0:T(8,128)(2,1)S(1)}, u32[]{:S(2)}, u32[]{:S(2)}) collective-permute-start(bf16[80,384]{1,0:T(8,128)(2,1)S(1)} %get-tuple-element.13), channel_id=1, source_target_pairs={{0,6},{2,4},{4,2},{6,0},{8,14},{10,12},{12,10},{14,8},{1,7},{3,5},... | collective-permute-start | bytes 184328 | tf_op jit(solution)/shard_map/ppermute | solution.py:109
  9.0 0.8 %broadcast_select_fusion.2 = (bf16[72,384]{1,0:T(8,128)(2,1)S(1)}, bf16[72,384]{1,0:T(8,128)(2,1)S(1)}) fusion(pred[]{:T(512)S(6)} %eq.4, bf16[40,768]{1,0:T(8,128)(2,1)S(1)} %reshape.16, bf16[32,768]{1,0:T(8,128)(2,1)} %bitcast.15), kind=kLoop, calls=%fused_computation.11 | loop fusion | flops 387072 | bytes 221185 | tf_op jit(solution)/shard_map/jit(_where)/select_n | solution.py:103
  9.9 1.9 %collective-permute-start = (bf16[152,384]{1,0:T(8,128)(2,1)S(1)}, bf16[152,384]{1,0:T(8,128)(2,1)S(1)}, u32[]{:S(2)}, u32[]{:S(2)}) collective-permute-start(bf16[152,384]{1,0:T(8,128)(2,1)S(1)} %pad_maximum_fusion), channel_id=1, source_target_pairs={{0,2},{2,0},{4,6},{6,4},{8,10},{10,8},{12,14},{14,12},{1,3},{3,1},... | collective-permute-start | bytes 350216 | tf_op jit(solution)/shard_map/ppermute | solution.py:109
  12.4 0.7 %fusion.1 = pred[768]{0:T(1024)(128)(4,1)S(1)} fusion(pred[768]{0:T(1024)(128)(4,1)} %constant.41.clone, s32[768]{0:T(1024)} %constant.40.clone, s32[768]{0:T(1024)} %constant.39.clone, s32[]{:T(128)} %bitcast.13, s32[]{:T(128)S(6)} %axis_index.23), kind=kLoop, calls=%fused_computation.18 | loop fusion | flops 3840 | bytes 7688 | tf_op jit(solution)/shard_map/or | solution.py:141
  13.1 0.7 %and_select_fusion.bias_ref = f32[4,768]{1,0:T(4,128)S(1)} fusion(pred[4,768]{1,0:T(4,128)(4,1)} %constant.42.clone, pred[768]{0:T(1024)(128)(4,1)S(1)} %fusion.1), kind=kLoop, calls=%fused_computation.13 | loop fusion | flops 6144 | bytes 16128 | tf_op jit(solution)/shard_map/jit(_where)/select_n | solution.py:142
  13.8 0.7 %compare_select_fusion = s32[2]{0:T(128)S(1)} fusion(s32[2]{0:T(128)} %param.18), kind=kLoop, calls=%fused_computation.19 | loop fusion | flops 6 | bytes 16 | tf_op jit(solution)/shard_map/select_n | solution.py:154
  14.5 1.6 %collective-permute-start.5 = (bf16[80,384]{1,0:T(8,128)(2,1)S(1)}, bf16[80,384]{1,0:T(8,128)(2,1)S(1)}, u32[]{:S(2)}, u32[]{:S(2)}) collective-permute-start(bf16[80,384]{1,0:T(8,128)(2,1)S(1)} %collective-permute-done.3.refs_2_), channel_id=1, source_target_pairs={{0,4},{2,6},{4,0},{6,2},{8,12},{10,14},{12,8},{14,10},{1,5},{3,7},... | collective-permute-start | bytes 184328 | tf_op jit(solution)/shard_map/ppermute | solution.py:109
  16.1 0.6 %collective-permute-start.6 = (bf16[80,384]{1,0:T(8,128)(2,1)S(1)}, bf16[80,384]{1,0:T(8,128)(2,1)S(1)}, u32[]{:S(2)}, u32[]{:S(2)}) collective-permute-start(bf16[80,384]{1,0:T(8,128)(2,1)S(1)} %collective-permute-done.4.refs_3_), channel_id=1, source_target_pairs={{0,4},{2,6},{4,0},{6,2},{8,12},{10,14},{12,8},{14,10},{1,5},{3,7},... | collective-permute-start | bytes 184328 | tf_op jit(solution)/shard_map/ppermute | solution.py:109
  16.7 2.0 %collective-permute-done.5.refs_4_ = bf16[80,384]{1,0:T(8,128)(2,1)S(1)} collective-permute-done((bf16[80,384]{1,0:T(8,128)(2,1)S(1)}, bf16[80,384]{1,0:T(8,128)(2,1)S(1)}, u32[]{:S(2)}, u32[]{:S(2)}) %collective-permute-start.5) | collective-permute-done | bytes 61472 | tf_op jit(solution)/shard_map/ppermute | solution.py:109
  18.7 1.6 %collective-permute-done.6.refs_5_ = bf16[80,384]{1,0:T(8,128)(2,1)S(1)} collective-permute-done((bf16[80,384]{1,0:T(8,128)(2,1)S(1)}, bf16[80,384]{1,0:T(8,128)(2,1)S(1)}, u32[]{:S(2)}, u32[]{:S(2)}) %collective-permute-start.6) | collective-permute-done | bytes 61472 | tf_op jit(solution)/shard_map/ppermute | solution.py:109
  20.3 1.6 %shard_map.118 = (bf16[32,384]{1,0:T(8,128)(2,1)S(1)}, bf16[32,384]{1,0:T(8,128)(2,1)S(1)}) custom-call(f32[4,768]{1,0:T(4,128)S(1)} %and_select_fusion.bias_ref, bf16[80,384]{1,0:T(8,128)(2,1)S(1)} %get-tuple-element.14.own_ref, bf16[72,384]{1,0:T(8,128)(2,1)S(1)} %get-tuple-element.18.local_ref, bf16[152,384]{1,0:T(8,128)(2,1)S(1)} %collective-permute-done.pair_ref, ...), custom_call_target="tpu_custom_call" | custom-call | tf_op jit(solution)/shard_map/pallas_call | solution.py:145
  21.9 0.6 %collective-permute-start.7 = (bf16[32,384]{1,0:T(8,128)(2,1)S(1)}, bf16[32,384]{1,0:T(8,128)(2,1)S(1)}, u32[]{:S(2)}, u32[]{:S(2)}) collective-permute-start(bf16[32,384]{1,0:T(8,128)(2,1)S(1)} %get-tuple-element.9), channel_id=1, source_target_pairs={{0,2},{2,0},{4,6},{6,4},{8,10},{10,8},{12,14},{14,12},{1,3},{3,1},... | collective-permute-start | bytes 73736 | tf_op jit(solution)/shard_map/ppermute | solution.py:109
  22.6 0.6 %gather_fusion = bf16[2,3072]{1,0:T(2,128)(2,1)S(1)} fusion(bf16[28,3072]{1,0:T(8,128)(2,1)S(1)} %copy-done, s32[1024]{0:T(1024)S(1)} %pad_clamp_fusion), kind=kCustom, calls=%fused_computation | custom fusion | bytes 24584 | tf_op jit(solution)/shard_map/gather | solution.py:154
  23.2 2.3 %copy-done.1 = bf16[768,3072]{1,0:T(8,128)(2,1)S(1)} copy-done((bf16[768,3072]{1,0:T(8,128)(2,1)S(1)}, bf16[768,3072]{1,0:T(8,128)(2,1)}, u32[]{:S(2)}) %copy-start.1) | copy-done | bytes 4718616
  25.5 0.8 %copy-done.3 = bf16[16,1536]{1,0:T(8,128)(2,1)S(1)} copy-done((bf16[16,1536]{1,0:T(8,128)(2,1)S(1)}, bf16[16,1536]{1,0:T(8,128)(2,1)}, u32[]{:S(2)}) %copy-start.3) | copy-done | bytes 49176
  26.3 1.1 %shard_map.119.sum_ref = f32[16,3072]{1,0:T(8,128)S(1)} custom-call(s32[2]{0:T(128)S(1)} %pad_add_fusion.place_ref, bf16[32,384]{1,0:T(8,128)(2,1)S(1)} %get-tuple-element.10.attended_ref, bf16[768,3072]{1,0:T(8,128)(2,1)S(1)} %copy-done.1, f32[2,3072]{1,0:T(2,128)S(1)} %convert_element_type.9.gates_ref, bf16[16,1536]{1,0:T(8,128)(2,1)S(1)} %copy-done.3), custom_call_target="tpu_custom_call" | custom-call | tf_op jit(solution)/shard_map/pallas_call | solution.py:157
  27.4 1.2 %copy-done.2 = bf16[768,3072]{1,0:T(8,128)(2,1)S(1)} copy-done((bf16[768,3072]{1,0:T(8,128)(2,1)S(1)}, bf16[768,3072]{1,0:T(8,128)(2,1)}, u32[]{:S(2)}) %copy-start.2) | copy-done | bytes 4718616
  28.6 1.1 %shard_map.120 = (f32[8,3072]{1,0:T(8,128)S(1)}, bf16[8,3072]{1,0:T(8,128)(2,1)S(1)}) custom-call(s32[2]{0:T(128)S(1)} %pad_add_fusion.place_ref, bf16[32,384]{1,0:T(8,128)(2,1)S(1)} %collective-permute-done.7.attended_ref, bf16[768,3072]{1,0:T(8,128)(2,1)S(1)} %copy-done.2, f32[2,3072]{1,0:T(2,128)S(1)} %convert_element_type.9.gates_ref, ...), custom_call_target="tpu_custom_call" | custom-call | tf_op jit(solution)/shard_map/pallas_call | solution.py:164
  29.8 1.2 %collective-permute-done.8 = bf16[8,3072]{1,0:T(8,128)(2,1)S(1)} collective-permute-done((bf16[8,3072]{1,0:T(8,128)(2,1)S(1)}, bf16[8,3072]{1,0:T(8,128)(2,1)S(1)}, u32[]{:S(2)}, u32[]{:S(2)}) %collective-permute-start.8) | collective-permute-done | bytes 49184 | tf_op jit(solution)/shard_map/ppermute | solution.py:175
  31.0 0.6 %add_convert_fusion = bf16[8,3072]{1,0:T(8,128)(2,1)} fusion(f32[8,3072]{1,0:T(8,128)S(1)} %get-tuple-element.11, bf16[8,3072]{1,0:T(8,128)(2,1)S(1)} %collective-permute-done.8), kind=kLoop, calls=%fused_computation.4 | loop fusion | flops 73728 | bytes 196608 | tf_op jit(solution)/shard_map/convert_element_type | solution.py:176
  (22 shorter events, 0.3 us)
Async XLA Ops:
  0.0 22.5 %copy-start = (bf16[28,3072]{1,0:T(8,128)(2,1)S(1)}, bf16[28,3072]{1,0:T(8,128)(2,1)}, u32[]{:S(2)}) copy-start(bf16[28,3072]{1,0:T(8,128)(2,1)} %param.17) | copy-start | bytes 516100
  1.9 14.8 %collective-permute-start.1 = (bf16[80,384]{1,0:T(8,128)(2,1)S(1)}, bf16[80,384]{1,0:T(8,128)(2,1)S(1)}, u32[]{:S(2)}, u32[]{:S(2)}) collective-permute-start(bf16[80,384]{1,0:T(8,128)(2,1)S(1)} %get-tuple-element.14.own_ref), channel_id=1, source_target_pairs={{0,4},{2,6},{4,0},{6,2},{8,12},{10,14},{12,8},{14,10},{1,5},{3,7},... | collective-permute-start | bytes 184328 | tf_op jit(solution)/shard_map/ppermute | solution.py:109
  5.0 9.5 %collective-permute-start.3 = (bf16[80,384]{1,0:T(8,128)(2,1)S(1)}, bf16[80,384]{1,0:T(8,128)(2,1)S(1)}, u32[]{:S(2)}, u32[]{:S(2)}) collective-permute-start(bf16[80,384]{1,0:T(8,128)(2,1)S(1)} %get-tuple-element.14.own_ref), channel_id=1, source_target_pairs={{0,8},{2,10},{4,12},{6,14},{8,0},{10,2},{12,4},{14,6},{1,9},{3,11}... | collective-permute-start | bytes 184328 | tf_op jit(solution)/shard_map/ppermute | solution.py:109
  7.6 9.1 %collective-permute-start.2 = (bf16[80,384]{1,0:T(8,128)(2,1)S(1)}, bf16[80,384]{1,0:T(8,128)(2,1)S(1)}, u32[]{:S(2)}, u32[]{:S(2)}) collective-permute-start(bf16[80,384]{1,0:T(8,128)(2,1)S(1)} %get-tuple-element.13), channel_id=1, source_target_pairs={{0,6},{2,4},{4,2},{6,0},{8,14},{10,12},{12,10},{14,8},{1,7},{3,5},... | collective-permute-start | bytes 184328 | tf_op jit(solution)/shard_map/ppermute | solution.py:109
  9.0 7.1 %collective-permute-start.4 = (bf16[80,384]{1,0:T(8,128)(2,1)S(1)}, bf16[80,384]{1,0:T(8,128)(2,1)S(1)}, u32[]{:S(2)}, u32[]{:S(2)}) collective-permute-start(bf16[80,384]{1,0:T(8,128)(2,1)S(1)} %get-tuple-element.13), channel_id=1, source_target_pairs={{0,10},{2,8},{4,14},{6,12},{8,2},{10,0},{12,6},{14,4},{1,11},{3,9}... | collective-permute-start | bytes 184328 | tf_op jit(solution)/shard_map/ppermute | solution.py:109
  9.9 6.8 %collective-permute-start = (bf16[152,384]{1,0:T(8,128)(2,1)S(1)}, bf16[152,384]{1,0:T(8,128)(2,1)S(1)}, u32[]{:S(2)}, u32[]{:S(2)}) collective-permute-start(bf16[152,384]{1,0:T(8,128)(2,1)S(1)} %pad_maximum_fusion), channel_id=1, source_target_pairs={{0,2},{2,0},{4,6},{6,4},{8,10},{10,8},{12,14},{14,12},{1,3},{3,1},... | collective-permute-start | bytes 350216 | tf_op jit(solution)/shard_map/ppermute | solution.py:109
  14.5 4.2 %collective-permute-start.5 = (bf16[80,384]{1,0:T(8,128)(2,1)S(1)}, bf16[80,384]{1,0:T(8,128)(2,1)S(1)}, u32[]{:S(2)}, u32[]{:S(2)}) collective-permute-start(bf16[80,384]{1,0:T(8,128)(2,1)S(1)} %collective-permute-done.3.refs_2_), channel_id=1, source_target_pairs={{0,4},{2,6},{4,0},{6,2},{8,12},{10,14},{12,8},{14,10},{1,5},{3,7},... | collective-permute-start | bytes 184328 | tf_op jit(solution)/shard_map/ppermute | solution.py:109
  16.1 4.2 %collective-permute-start.6 = (bf16[80,384]{1,0:T(8,128)(2,1)S(1)}, bf16[80,384]{1,0:T(8,128)(2,1)S(1)}, u32[]{:S(2)}, u32[]{:S(2)}) collective-permute-start(bf16[80,384]{1,0:T(8,128)(2,1)S(1)} %collective-permute-done.4.refs_3_), channel_id=1, source_target_pairs={{0,4},{2,6},{4,0},{6,2},{8,12},{10,14},{12,8},{14,10},{1,5},{3,7},... | collective-permute-start | bytes 184328 | tf_op jit(solution)/shard_map/ppermute | solution.py:109
  21.9 5.5 %collective-permute-start.7 = (bf16[32,384]{1,0:T(8,128)(2,1)S(1)}, bf16[32,384]{1,0:T(8,128)(2,1)S(1)}, u32[]{:S(2)}, u32[]{:S(2)}) collective-permute-start(bf16[32,384]{1,0:T(8,128)(2,1)S(1)} %get-tuple-element.9), channel_id=1, source_target_pairs={{0,2},{2,0},{4,6},{6,4},{8,10},{10,8},{12,14},{14,12},{1,3},{3,1},... | collective-permute-start | bytes 73736 | tf_op jit(solution)/shard_map/ppermute | solution.py:109
  23.1 2.3 %copy-start.1 = (bf16[768,3072]{1,0:T(8,128)(2,1)S(1)}, bf16[768,3072]{1,0:T(8,128)(2,1)}, u32[]{:S(2)}) copy-start(bf16[768,3072]{1,0:T(8,128)(2,1)} %weight_ref.3) | copy-start | bytes 14155780
  25.5 0.8 %copy-start.3 = (bf16[16,1536]{1,0:T(8,128)(2,1)S(1)}, bf16[16,1536]{1,0:T(8,128)(2,1)}, u32[]{:S(2)}) copy-start(bf16[16,1536]{1,0:T(8,128)(2,1)} %hidden_ref.1) | copy-start | bytes 147460
  26.3 2.3 %copy-start.2 = (bf16[768,3072]{1,0:T(8,128)(2,1)S(1)}, bf16[768,3072]{1,0:T(8,128)(2,1)}, u32[]{:S(2)}) copy-start(bf16[768,3072]{1,0:T(8,128)(2,1)} %weight_ref.3) | copy-start | bytes 14155780
  29.7 1.3 %collective-permute-start.8 = (bf16[8,3072]{1,0:T(8,128)(2,1)S(1)}, bf16[8,3072]{1,0:T(8,128)(2,1)S(1)}, u32[]{:S(2)}, u32[]{:S(2)}) collective-permute-start(bf16[8,3072]{1,0:T(8,128)(2,1)S(1)} %get-tuple-element.12), channel_id=1, source_target_pairs={{0,1},{1,0},{2,3},{3,2},{4,5},{5,4},{6,7},{7,6},{8,9},{9,8},{10,11... | collective-permute-start | bytes 147464 | tf_op jit(solution)/shard_map/ppermute | solution.py:175

commit v2 on v1

v2 whole, which is shorter than its diff:
```python
import functools

import jax
import jax.numpy as jnp
import numpy as np
from jax import lax
from jax.experimental import pallas as pl
from jax.experimental.pallas import tpu as pltpu
from jax.sharding import PartitionSpec as P

HDIM = 128
LANES = 128
MASKED = -1e30
VMEM_LIMIT = 24 * 1024 * 1024


def round_up(value, step):
    return (value + step - 1) // step * step


def pack_kernel(sizes, text_hbm, table_hbm, stale_hbm, step_hbm, query_hbm, own_ref, other_ref, local_ref, pair_ref, bias_ref,
                text_ref, table_ref, stale, step, query, sems):
    strips, lat_rows, text_rows = sizes
    copies = [
        pltpu.make_async_copy(stale_hbm, stale, sems.at[0]),
        pltpu.make_async_copy(step_hbm, step, sems.at[1]),
        pltpu.make_async_copy(query_hbm, query, sems.at[2]),
        pltpu.make_async_copy(text_hbm, text_ref, sems.at[3]),
        pltpu.make_async_copy(table_hbm, table_ref, sems.at[4]),
    ]
    for copy in copies:
        copy.start()
    strip = lax.axis_index("patch")
    side = lax.rem(strip, 2)
    half = own_ref.shape[1]
    for copy in copies:
        copy.wait()
    early = table_ref[5:6, :]
    live = (early < 0) | ((strip ^ table_ref[4:5, :]) * text_rows + early < text_ref[0])
    for c in range(4):
        bias_ref[c : c + 1, :] = jnp.where((table_ref[c : c + 1, :] > 0) & live, 0.0, MASKED)

    def pick(ref, lead, which):
        lanes = pl.ds(pl.multiple_of(which * half, LANES), half)
        rows = ref[lead + (slice(None),) * (len(ref.shape) - len(lead) - 1) + (lanes,)]
        return rows.reshape(-1, half)

    for which, block_ref, rest_ref in ((side, own_ref, local_ref), (1 - side, other_ref, pair_ref)):
        block = jnp.concatenate([pick(stale, (), which), pick(step, (0,), which)], axis=0)
        rest = jnp.concatenate([pick(query, (), which), pick(step, (1,), which)], axis=0)
        block_ref[...] = block
        if rest_ref is pair_ref:
            rest = jnp.concatenate([block, rest], axis=0)
        spare = rest_ref.shape[0] - rest.shape[0]
        rest_ref[...] = jnp.concatenate([rest, jnp.zeros((spare, half), rest.dtype)], axis=0) if spare else rest


def attention_kernel(sizes, bias_ref, own_ref, local_ref, pair_ref, *refs):
    set_rows, query_rows, columns = sizes
    others, (mine_ref, back_ref) = refs[:-2], refs[-2:]
    pair_rows = 2 * set_rows
    per_class = query_rows // 2
    scale = 1.0 / HDIM**0.5
    bias = jnp.concatenate(
        [jnp.broadcast_to(bias_ref[c : c + 1, :], (per_class, columns)) for c in range(4)], axis=0
    )
    for head in range(own_ref.shape[1] // HDIM):
        lanes = slice(head * HDIM, (head + 1) * HDIM)
        rows = [own_ref[:, lanes], pair_ref[:pair_rows, lanes]]
        rows += [ref[:, lanes] for ref in others]
        rows += [local_ref[query_rows:, lanes], pair_ref[pair_rows + query_rows :, lanes]]
        filled = sum(r.shape[0] for r in rows)
        if filled < columns:
            rows.append(jnp.zeros((columns - filled, HDIM), jnp.bfloat16))
        keys = jnp.concatenate(rows, axis=0)
        queries = jnp.concatenate(
            [local_ref[:query_rows, lanes], pair_ref[pair_rows : pair_rows + query_rows, lanes]], axis=0
        )
        scores = lax.dot_general(
            queries, keys, (((1,), (1,)), ((), ())), preferred_element_type=jnp.float32
        )
        scores = scores * scale + bias
        top = jnp.max(scores, axis=1, keepdims=True)
        expo = jnp.exp(scores - top)
        weights = expo / jnp.sum(expo, axis=1, keepdims=True)
        weights = pltpu.roll(weights, 1, 1).astype(jnp.bfloat16)
        mixed = jnp.dot(weights, keys, preferred_element_type=jnp.float32).astype(jnp.bfloat16)
        mine_ref[:, lanes] = mixed[:query_rows]
        back_ref[:, lanes] = mixed[query_rows:]


def gated(attended, weight, gates):
    strip = attended.shape[0] // 2
    projected = jnp.dot(attended, weight, preferred_element_type=jnp.float32)
    return gates[0:1, :] * projected[:strip] + gates[1:2, :] * projected[strip:]


def first_half_kernel(attended_ref, plan_hbm, table_hbm, hidden_hbm, weight_hbm, sum_ref, gates_ref, far_ref,
                      plan_ref, table_ref, hidden_ref, near, sems):
    depth = attended_ref.shape[1]
    width = hidden_ref.shape[1]
    side = lax.rem(lax.axis_index("patch"), 2)
    rows = pl.ds(pl.multiple_of(side * depth, depth), depth)
    far_rows = pl.ds(pl.multiple_of((1 - side) * depth, depth), depth)
    near_copy = pltpu.make_async_copy(weight_hbm.at[rows, :], near, sems.at[0])
    far_copy = pltpu.make_async_copy(weight_hbm.at[far_rows, :], far_ref, sems.at[1])
    small = [
        pltpu.make_async_copy(plan_hbm, plan_ref, sems.at[2]),
        pltpu.make_async_copy(table_hbm, table_ref, sems.at[3]),
        pltpu.make_async_copy(hidden_hbm, hidden_ref, sems.at[4]),
    ]
    for copy in small + [near_copy, far_copy]:
        copy.start()
    for copy in small:
        copy.wait()
    table = table_ref[...].astype(jnp.float32)
    entry = lax.broadcasted_iota(jnp.int32, table.shape, 0)
    for step in range(2):
        row = jnp.sum(jnp.where(entry == plan_ref[step], table, 0.0), axis=0, keepdims=True)
        gates_ref[step : step + 1, :] = row
    near_copy.wait()
    sum_ref[...] = gated(attended_ref[...], near[...], gates_ref[...])
    lanes = pl.ds(pl.multiple_of(lax.axis_index("head") * width, LANES), width)
    sum_ref[:, lanes] += hidden_ref[...].astype(jnp.float32)
    far_copy.wait()


def second_half_kernel(attended_ref, weight_ref, gates_ref, sum_ref, keep_ref, send_ref, total):
    half = keep_ref.shape[0]
    total[...] = sum_ref[...] + gated(attended_ref[...], weight_ref[...], gates_ref[...])
    core = lax.axis_index("head")
    keep_ref[...] = total[pl.ds(pl.multiple_of(core * half, half), half), :]
    send_ref[...] = total[pl.ds(pl.multiple_of((1 - core) * half, half), half), :].astype(jnp.bfloat16)


def per_device(queries, stale_pairs, step_pairs, hidden, out_weight, gate_table, t_index, text_len):
    strips = lax.axis_size("patch")
    strip_rows = stale_pairs.shape[1]
    lat_rows = queries.shape[1]
    text_rows = strip_rows - lat_rows
    width = queries.shape[2]
    half = width // 2
    set_rows = 2 * strip_rows
    query_rows = 2 * lat_rows
    block_rows = 2 * set_rows
    vmem = pl.BlockSpec(memory_space=pltpu.VMEM)
    hbm = pl.BlockSpec(memory_space=pltpu.HBM)
    params = pltpu.CompilerParams(vmem_limit_bytes=VMEM_LIMIT)

    def in_hbm(*arrays):
        return [pltpu.with_memory_space_constraint(array, pltpu.HBM) for array in arrays]

    flips = list(range(2, strips))
    blocks = [0, 1] + flips
    filled = block_rows * len(blocks) + 2 * set_rows
    columns = round_up(filled, LANES)
    column = np.arange(columns)
    in_blocks = column < block_rows * len(blocks)
    block = np.minimum(column // block_rows, len(blocks) - 1)
    within = column % block_rows
    flip = np.where(in_blocks, np.asarray(blocks)[block], within // set_rows)
    kind = np.where(in_blocks, within // set_rows, np.where(column < filled, 2, 3))
    token = (within % set_rows) // 2
    whose, step = np.asarray([0, 0, 1, 1])[:, None], np.asarray([0, 1, 0, 1])[:, None]
    chosen = (within % 2 == 0) & (kind == np.where(flip == whose, step + 1, step))
    unused = np.zeros((2, columns))
    table = np.concatenate([chosen, flip[None], (token - lat_rows)[None], unused], axis=0).astype(np.int32)

    bf16 = functools.partial(jax.ShapeDtypeStruct, dtype=jnp.bfloat16)
    f32 = functools.partial(jax.ShapeDtypeStruct, dtype=jnp.float32)
    local_rows = query_rows + set_rows
    own, other, local, pair, bias = pl.pallas_call(
        functools.partial(pack_kernel, (strips, lat_rows, text_rows)),
        out_shape=(
            bf16((block_rows, half)),
            bf16((block_rows, half)),
            bf16((local_rows, half)),
            bf16((block_rows + local_rows, half)),
            f32((4, columns)),
        ),
        in_specs=[hbm] * 5,
        out_specs=(vmem,) * 5,
        scratch_shapes=[
            pltpu.SMEM(text_len.shape, jnp.int32),
            pltpu.VMEM(table.shape, jnp.int32),
            pltpu.VMEM((strip_rows, 2, width), jnp.bfloat16),
            pltpu.VMEM((2, strip_rows, 2, width), jnp.bfloat16),
            pltpu.VMEM((2, lat_rows, width), jnp.bfloat16),
            pltpu.SemaphoreType.DMA((5,)),
        ],
        compiler_params=params,
    )(text_len, *in_hbm(jnp.asarray(table), stale_pairs.transpose(1, 0, 2), step_pairs.transpose(0, 2, 1, 3), queries))

    def to(rows, flip):
        return lax.ppermute(rows, "patch", [(i, i ^ flip) for i in range(strips)])

    held = {0: own}
    bit = strips // 2
    pair_rows = None
    while bit > 1:
        arrived = {bit: to(own, bit), bit + 1: to(other, bit + 1)}
        if pair_rows is None:
            pair_rows = to(pair, 1)
        for flip, rows in held.items():
            if flip > 1:
                arrived[flip + bit] = to(rows, bit)
        held.update(arrived)
        bit //= 2

    mine, back = pl.pallas_call(
        functools.partial(attention_kernel, (set_rows, query_rows, columns)),
        out_shape=(bf16((query_rows, half)),) * 2,
        compiler_params=params,
    )(bias, own, local, pair_rows, *[held[flip] for flip in flips])
    returned = to(back, 1)

    model = out_weight.shape[1]
    total, gates, far_weight = pl.pallas_call(
        first_half_kernel,
        out_shape=(f32((lat_rows, model)), f32((2, model)), bf16((half, model))),
        in_specs=[vmem] + [hbm] * 4,
        out_specs=(vmem,) * 3,
        scratch_shapes=[
            pltpu.SMEM(t_index.shape, jnp.int32),
            pltpu.VMEM(gate_table.shape, jnp.bfloat16),
            pltpu.VMEM(hidden.shape, jnp.bfloat16),
            pltpu.VMEM((half, model), jnp.bfloat16),
            pltpu.SemaphoreType.DMA((5,)),
        ],
        compiler_params=params,
    )(mine, *in_hbm(t_index, gate_table, hidden, out_weight))
    keep, send = pl.pallas_call(
        second_half_kernel,
        out_shape=(f32((lat_rows // 2, model)), bf16((lat_rows // 2, model))),
        in_specs=[vmem] * 4,
        out_specs=(vmem, vmem),
        scratch_shapes=[pltpu.VMEM((lat_rows, model), jnp.float32)],
        compiler_params=params,
    )(returned, far_weight, gates, total)
    received = lax.ppermute(send, "head", [(0, 1), (1, 0)])
    return (keep + received.astype(jnp.float32)).astype(jnp.bfloat16)


def solution(mesh):
    return jax.shard_map(
        per_device,
        mesh=mesh,
        in_specs=(
            P(None, ("groups", "patch"), "head"),
            P(None, ("groups", "patch"), "head"),
            P(None, None, ("groups", "patch"), "head"),
            P(("groups", "patch"), "head"),
            P("head", None),
            P(),
            P("groups"),
            P("groups"),
        ),
        out_specs=P(("groups", "patch", "head"), None),
        check_vma=False,
    )
```

time: 32.1 us -> 25 us (0.78)
  local copies, waits for them, and re-layouts: 6.86 us -> 0 us
  other arithmetic: 3.68 us -> 0.63 us
  Pallas kernels: 3.72 us -> 5.71 us
  waiting for transfers between devices: 4.8 us -> 5.42 us
  starting transfers between devices: 11.8 us -> 12.4 us
    unnamed x9 -> x0, local copies, waits for them, and re-layouts: 4.38 us -> none
    select_n x4 -> x0, other arithmetic: 2.21 us -> none  [the longest x2 0.86 us: far(): return jnp.where(side == 0, rows[:, half:], rows[:, :half])]
    pallas_call x2 -> x3, Pallas kernels: 2.15 us -> 4.13 us  [the longest x1 2.56 us: per_device(): pl.pallas_call(first_half_kernel, out_shape=(f32((lat_rows, model)), f32(...]
    reshape x3 -> x0, local copies, waits for them, and re-layouts: 0.95 us -> none  [interleaved(): return pairs.transpose(1, 0, 2).reshape(set_rows, width)]
    transpose x1 -> x0, local copies, waits for them, and re-layouts: 0.95 us -> none  [interleaved(): return pairs.transpose(1, 0, 2).reshape(set_rows, width)]
    or x1 -> x0, other arithmetic: 0.73 us -> none  [per_device(): (token < lat_rows) | (holder * text_rows + (token - lat_rows) < text_len[0])]
    ppermute x8, waiting for transfers between devices: 3.58 us -> 4.2 us  [to(): return lax.ppermute(rows, 'patch', [(i, i ^ flip) for i in range(strips)])]
    ppermute x8, starting transfers between devices: 11.7 us -> 12.3 us  [to(): return lax.ppermute(rows, 'patch', [(i, i ^ flip) for i in range(strips)])]
  transfers between devices with their start and end apart: 9 -> 9, of which waited for: 3 -> 6; matrix products, arithmetic and copies ran while one was open for 11% -> 0% of each run, Pallas kernels for 3% -> 10%
where the time goes in v2:
time: 25 us; the launch traced here: 24.8 us
  starting transfers between devices  12.4 us (50%)
  Pallas kernels  5.71 us (23%)
  waiting for transfers between devices  5.42 us (22%)
  between operations  0.69 us (3%)
  other arithmetic  0.63 us (3%)
    ppermute x8, starting transfers between devices, to(): return lax.ppermute(rows, 'patch', [(i, i ^ flip) for i in range(strips)])  12.3 us
    ppermute x8, waiting for transfers between devices, to(): return lax.ppermute(rows, 'patch', [(i, i ^ flip) for i in range(strips)])  4.2 us
    pallas_call x1, Pallas kernels, per_device(): pl.pallas_call(first_half_kernel, out_shape=(f32((lat_rows, model)), f32(...  2.56 us
    pallas_call x1, Pallas kernels, per_device(): pl.pallas_call(functools.partial(attention_kernel, (set_rows, query_rows,...  1.57 us
    ppermute x1, waiting for transfers between devices, per_device(): received = lax.ppermute(send, 'head', [(0, 1), (1, 0)])  1.22 us
    pallas_call x1, Pallas kernels, per_device(): pl.pallas_call(functools.partial(pack_kernel, (strips, lat_rows, text_row...  1.05 us
    convert_element_type x1, other arithmetic, per_device(): return (keep + received.astype(jnp.float32)).astype(jnp.bfloat16)  0.63 us
    pallas_call x1, Pallas kernels, per_device(): pl.pallas_call(second_half_kernel, out_shape=(f32((lat_rows // 2, model))...  0.52 us
  transfers between devices with their start and end apart: 9, of which 6 were waited for; matrix products, arithmetic and copies ran while one was open for 0% of the time, Pallas kernels for 10%

profile of v2, /device:TPU:0, one launch (start us, length us, event | category | flops | bytes accessed | tf_op | source)
XLA Modules:
  0.0 24.8 jit_solution(11830213860211378218)
XLA Ops:
  0.7 1.0 %shard_map.91 = (bf16[80,384]{1,0:T(8,128)(2,1)S(1)}, bf16[80,384]{1,0:T(8,128)(2,1)S(1)}, bf16[72,384]{1,0:T(8,128)(2,1)S(1)}, bf16[152,384]{1,0:T(8,128)(2,1)S(1)}, f32[4,768]{1,0:T(4,128)S(1)}) custom-call(s32[1]{0:T(128)S(6)} %copy.10.text_hbm, s32[8,768]{1,0:T(8,128)} %constant.2.clone.table_hbm, bf16[20,2,768]{2,1,0:T(2,128)(2,1)} %bitcast.3, ...), custom_call_target="tpu_custom_call" | custom-call | tf_op jit(solution)/shard_map/pallas_call | solution.py:172
  1.7 5.0 %collective-permute-start.4 = (bf16[80,384]{1,0:T(8,128)(2,1)S(1)}, bf16[80,384]{1,0:T(8,128)(2,1)S(1)}, u32[]{:S(2)}, u32[]{:S(2)}) collective-permute-start(bf16[80,384]{1,0:T(8,128)(2,1)S(1)} %get-tuple-element.21), channel_id=1, source_target_pairs={{0,10},{2,8},{4,14},{6,12},{8,2},{10,0},{12,6},{14,4},{1,11},{3,9}... | collective-permute-start | bytes 184328 | tf_op jit(solution)/shard_map/ppermute | solution.py:195
  6.7 0.3 %collective-permute-start.3 = (bf16[80,384]{1,0:T(8,128)(2,1)S(1)}, bf16[80,384]{1,0:T(8,128)(2,1)S(1)}, u32[]{:S(2)}, u32[]{:S(2)}) collective-permute-start(bf16[80,384]{1,0:T(8,128)(2,1)S(1)} %get-tuple-element.18.own_ref), channel_id=1, source_target_pairs={{0,8},{2,10},{4,12},{6,14},{8,0},{10,2},{12,4},{14,6},{1,9},{3,11}... | collective-permute-start | bytes 184328 | tf_op jit(solution)/shard_map/ppermute | solution.py:195
  7.1 0.3 %collective-permute-start = (bf16[152,384]{1,0:T(8,128)(2,1)S(1)}, bf16[152,384]{1,0:T(8,128)(2,1)S(1)}, u32[]{:S(2)}, u32[]{:S(2)}) collective-permute-start(bf16[152,384]{1,0:T(8,128)(2,1)S(1)} %get-tuple-element.20), channel_id=1, source_target_pairs={{0,2},{2,0},{4,6},{6,4},{8,10},{10,8},{12,14},{14,12},{1,3},{3,1},... | collective-permute-start | bytes 350216 | tf_op jit(solution)/shard_map/ppermute | solution.py:195
  7.4 2.7 %collective-permute-start.2 = (bf16[80,384]{1,0:T(8,128)(2,1)S(1)}, bf16[80,384]{1,0:T(8,128)(2,1)S(1)}, u32[]{:S(2)}, u32[]{:S(2)}) collective-permute-start(bf16[80,384]{1,0:T(8,128)(2,1)S(1)} %get-tuple-element.21), channel_id=1, source_target_pairs={{0,6},{2,4},{4,2},{6,0},{8,14},{10,12},{12,10},{14,8},{1,7},{3,5},... | collective-permute-start | bytes 184328 | tf_op jit(solution)/shard_map/ppermute | solution.py:195
  10.1 0.4 %collective-permute-start.1 = (bf16[80,384]{1,0:T(8,128)(2,1)S(1)}, bf16[80,384]{1,0:T(8,128)(2,1)S(1)}, u32[]{:S(2)}, u32[]{:S(2)}) collective-permute-start(bf16[80,384]{1,0:T(8,128)(2,1)S(1)} %get-tuple-element.18.own_ref), channel_id=1, source_target_pairs={{0,4},{2,6},{4,0},{6,2},{8,12},{10,14},{12,8},{14,10},{1,5},{3,7},... | collective-permute-start | bytes 184328 | tf_op jit(solution)/shard_map/ppermute | solution.py:195
  10.6 0.0 collective-permute-done.4.refs_3_
  10.6 1.6 %collective-permute-start.6 = (bf16[80,384]{1,0:T(8,128)(2,1)S(1)}, bf16[80,384]{1,0:T(8,128)(2,1)S(1)}, u32[]{:S(2)}, u32[]{:S(2)}) collective-permute-start(bf16[80,384]{1,0:T(8,128)(2,1)S(1)} %collective-permute-done.4.refs_3_), channel_id=1, source_target_pairs={{0,4},{2,6},{4,0},{6,2},{8,12},{10,14},{12,8},{14,10},{1,5},{3,7},... | collective-permute-start | bytes 184328 | tf_op jit(solution)/shard_map/ppermute | solution.py:195
  12.2 0.5 %collective-permute-done.3.refs_2_ = bf16[80,384]{1,0:T(8,128)(2,1)S(1)} collective-permute-done((bf16[80,384]{1,0:T(8,128)(2,1)S(1)}, bf16[80,384]{1,0:T(8,128)(2,1)S(1)}, u32[]{:S(2)}, u32[]{:S(2)}) %collective-permute-start.3) | collective-permute-done | bytes 61472 | tf_op jit(solution)/shard_map/ppermute | solution.py:195
  12.7 1.4 %collective-permute-start.5 = (bf16[80,384]{1,0:T(8,128)(2,1)S(1)}, bf16[80,384]{1,0:T(8,128)(2,1)S(1)}, u32[]{:S(2)}, u32[]{:S(2)}) collective-permute-start(bf16[80,384]{1,0:T(8,128)(2,1)S(1)} %collective-permute-done.3.refs_2_), channel_id=1, source_target_pairs={{0,4},{2,6},{4,0},{6,2},{8,12},{10,14},{12,8},{14,10},{1,5},{3,7},... | collective-permute-start | bytes 184328 | tf_op jit(solution)/shard_map/ppermute | solution.py:195
  14.0 0.0 collective-permute-done.2.refs_1_
  14.0 1.1 %collective-permute-done.1.refs_0_ = bf16[80,384]{1,0:T(8,128)(2,1)S(1)} collective-permute-done((bf16[80,384]{1,0:T(8,128)(2,1)S(1)}, bf16[80,384]{1,0:T(8,128)(2,1)S(1)}, u32[]{:S(2)}, u32[]{:S(2)}) %collective-permute-start.1) | collective-permute-done | bytes 61472 | tf_op jit(solution)/shard_map/ppermute | solution.py:195
  15.2 0.0 collective-permute-done.pair_ref
  15.2 1.1 %collective-permute-done.6.refs_5_ = bf16[80,384]{1,0:T(8,128)(2,1)S(1)} collective-permute-done((bf16[80,384]{1,0:T(8,128)(2,1)S(1)}, bf16[80,384]{1,0:T(8,128)(2,1)S(1)}, u32[]{:S(2)}, u32[]{:S(2)}) %collective-permute-start.6) | collective-permute-done | bytes 61472 | tf_op jit(solution)/shard_map/ppermute | solution.py:195
  16.3 0.7 %collective-permute-done.5.refs_4_ = bf16[80,384]{1,0:T(8,128)(2,1)S(1)} collective-permute-done((bf16[80,384]{1,0:T(8,128)(2,1)S(1)}, bf16[80,384]{1,0:T(8,128)(2,1)S(1)}, u32[]{:S(2)}, u32[]{:S(2)}) %collective-permute-start.5) | collective-permute-done | bytes 61472 | tf_op jit(solution)/shard_map/ppermute | solution.py:195
  16.9 1.6 %shard_map.92 = (bf16[32,384]{1,0:T(8,128)(2,1)S(1)}, bf16[32,384]{1,0:T(8,128)(2,1)S(1)}) custom-call(f32[4,768]{1,0:T(4,128)S(1)} %get-tuple-element.17.bias_ref, bf16[80,384]{1,0:T(8,128)(2,1)S(1)} %get-tuple-element.18.own_ref, bf16[72,384]{1,0:T(8,128)(2,1)S(1)} %get-tuple-element.19.local_ref, bf16[152,384]{1,0:T(8,128)(2,1)S(1)} %collective-permute-done.pair_ref, ...), custom_call_target="tpu_custom_call" | custom-call | tf_op jit(solution)/shard_map/pallas_call | solution.py:210
  18.5 0.5 %collective-permute-start.7 = (bf16[32,384]{1,0:T(8,128)(2,1)S(1)}, bf16[32,384]{1,0:T(8,128)(2,1)S(1)}, u32[]{:S(2)}, u32[]{:S(2)}) collective-permute-start(bf16[32,384]{1,0:T(8,128)(2,1)S(1)} %get-tuple-element.22), channel_id=1, source_target_pairs={{0,2},{2,0},{4,6},{6,4},{8,10},{10,8},{12,14},{14,12},{1,3},{3,1},... | collective-permute-start | bytes 73736 | tf_op jit(solution)/shard_map/ppermute | solution.py:195
  19.0 2.6 %shard_map.93 = (f32[16,3072]{1,0:T(8,128)S(1)}, f32[2,3072]{1,0:T(2,128)S(1)}, bf16[384,3072]{1,0:T(8,128)(2,1)S(1)}) custom-call(bf16[32,384]{1,0:T(8,128)(2,1)S(1)} %get-tuple-element.23.attended_ref, s32[2]{0:T(128)} %plan_hbm.1, bf16[28,3072]{1,0:T(8,128)(2,1)} %table_hbm.2, bf16[16,1536]{1,0:T(8,128)(2,1)} %hidden_hbm.1, bf16[768,3072]{1,0:T(8,128)(2,1)} %weight_hbm.1), custom_call_target="tpu_custom_call" | custom-call | tf_op jit(solution)/shard_map/pallas_call | solution.py:218
  21.5 0.8 %collective-permute-done.7.attended_ref = bf16[32,384]{1,0:T(8,128)(2,1)S(1)} collective-permute-done((bf16[32,384]{1,0:T(8,128)(2,1)S(1)}, bf16[32,384]{1,0:T(8,128)(2,1)S(1)}, u32[]{:S(2)}, u32[]{:S(2)}) %collective-permute-start.7) | collective-permute-done | bytes 24608 | tf_op jit(solution)/shard_map/ppermute | solution.py:195
  22.4 0.5 %shard_map.94 = (f32[8,3072]{1,0:T(8,128)S(1)}, bf16[8,3072]{1,0:T(8,128)(2,1)S(1)}) custom-call(bf16[32,384]{1,0:T(8,128)(2,1)S(1)} %collective-permute-done.7.attended_ref, bf16[384,3072]{1,0:T(8,128)(2,1)S(1)} %get-tuple-element.24.weight_ref, f32[2,3072]{1,0:T(2,128)S(1)} %get-tuple-element.25.gates_ref, f32[16,3072]{1,0:T(8,128)S(1)} %get-tuple-element.26.sum_ref), custom_call_target="tpu_custom_call" | custom-call | tf_op jit(solution)/shard_map/pallas_call | solution.py:232
  22.9 0.1 collective-permute-start.8
  23.0 1.2 %collective-permute-done.8 = bf16[8,3072]{1,0:T(8,128)(2,1)S(1)} collective-permute-done((bf16[8,3072]{1,0:T(8,128)(2,1)S(1)}, bf16[8,3072]{1,0:T(8,128)(2,1)S(1)}, u32[]{:S(2)}, u32[]{:S(2)}) %collective-permute-start.8) | collective-permute-done | bytes 49184 | tf_op jit(solution)/shard_map/ppermute | solution.py:240
  24.2 0.6 %add_convert_fusion = bf16[8,3072]{1,0:T(8,128)(2,1)} fusion(f32[8,3072]{1,0:T(8,128)S(1)} %get-tuple-element.27, bf16[8,3072]{1,0:T(8,128)(2,1)S(1)} %collective-permute-done.8), kind=kLoop, calls=%fused_computation | loop fusion | flops 73728 | bytes 196608 | tf_op jit(solution)/shard_map/convert_element_type | solution.py:241
Async XLA Ops:
  1.7 8.9 %collective-permute-start.4 = (bf16[80,384]{1,0:T(8,128)(2,1)S(1)}, bf16[80,384]{1,0:T(8,128)(2,1)S(1)}, u32[]{:S(2)}, u32[]{:S(2)}) collective-permute-start(bf16[80,384]{1,0:T(8,128)(2,1)S(1)} %get-tuple-element.21), channel_id=1, source_target_pairs={{0,10},{2,8},{4,14},{6,12},{8,2},{10,0},{12,6},{14,4},{1,11},{3,9}... | collective-permute-start | bytes 184328 | tf_op jit(solution)/shard_map/ppermute | solution.py:195
  6.7 5.9 %collective-permute-start.3 = (bf16[80,384]{1,0:T(8,128)(2,1)S(1)}, bf16[80,384]{1,0:T(8,128)(2,1)S(1)}, u32[]{:S(2)}, u32[]{:S(2)}) collective-permute-start(bf16[80,384]{1,0:T(8,128)(2,1)S(1)} %get-tuple-element.18.own_ref), channel_id=1, source_target_pairs={{0,8},{2,10},{4,12},{6,14},{8,0},{10,2},{12,4},{14,6},{1,9},{3,11}... | collective-permute-start | bytes 184328 | tf_op jit(solution)/shard_map/ppermute | solution.py:195
  7.1 8.1 %collective-permute-start = (bf16[152,384]{1,0:T(8,128)(2,1)S(1)}, bf16[152,384]{1,0:T(8,128)(2,1)S(1)}, u32[]{:S(2)}, u32[]{:S(2)}) collective-permute-start(bf16[152,384]{1,0:T(8,128)(2,1)S(1)} %get-tuple-element.20), channel_id=1, source_target_pairs={{0,2},{2,0},{4,6},{6,4},{8,10},{10,8},{12,14},{14,12},{1,3},{3,1},... | collective-permute-start | bytes 350216 | tf_op jit(solution)/shard_map/ppermute | solution.py:195
  7.4 6.7 %collective-permute-start.2 = (bf16[80,384]{1,0:T(8,128)(2,1)S(1)}, bf16[80,384]{1,0:T(8,128)(2,1)S(1)}, u32[]{:S(2)}, u32[]{:S(2)}) collective-permute-start(bf16[80,384]{1,0:T(8,128)(2,1)S(1)} %get-tuple-element.21), channel_id=1, source_target_pairs={{0,6},{2,4},{4,2},{6,0},{8,14},{10,12},{12,10},{14,8},{1,7},{3,5},... | collective-permute-start | bytes 184328 | tf_op jit(solution)/shard_map/ppermute | solution.py:195
  10.1 5.1 %collective-permute-start.1 = (bf16[80,384]{1,0:T(8,128)(2,1)S(1)}, bf16[80,384]{1,0:T(8,128)(2,1)S(1)}, u32[]{:S(2)}, u32[]{:S(2)}) collective-permute-start(bf16[80,384]{1,0:T(8,128)(2,1)S(1)} %get-tuple-element.18.own_ref), channel_id=1, source_target_pairs={{0,4},{2,6},{4,0},{6,2},{8,12},{10,14},{12,8},{14,10},{1,5},{3,7},... | collective-permute-start | bytes 184328 | tf_op jit(solution)/shard_map/ppermute | solution.py:195
  10.6 5.7 %collective-permute-start.6 = (bf16[80,384]{1,0:T(8,128)(2,1)S(1)}, bf16[80,384]{1,0:T(8,128)(2,1)S(1)}, u32[]{:S(2)}, u32[]{:S(2)}) collective-permute-start(bf16[80,384]{1,0:T(8,128)(2,1)S(1)} %collective-permute-done.4.refs_3_), channel_id=1, source_target_pairs={{0,4},{2,6},{4,0},{6,2},{8,12},{10,14},{12,8},{14,10},{1,5},{3,7},... | collective-permute-start | bytes 184328 | tf_op jit(solution)/shard_map/ppermute | solution.py:195
  12.7 4.3 %collective-permute-start.5 = (bf16[80,384]{1,0:T(8,128)(2,1)S(1)}, bf16[80,384]{1,0:T(8,128)(2,1)S(1)}, u32[]{:S(2)}, u32[]{:S(2)}) collective-permute-start(bf16[80,384]{1,0:T(8,128)(2,1)S(1)} %collective-permute-done.3.refs_2_), channel_id=1, source_target_pairs={{0,4},{2,6},{4,0},{6,2},{8,12},{10,14},{12,8},{14,10},{1,5},{3,7},... | collective-permute-start | bytes 184328 | tf_op jit(solution)/shard_map/ppermute | solution.py:195
  18.5 3.9 %collective-permute-start.7 = (bf16[32,384]{1,0:T(8,128)(2,1)S(1)}, bf16[32,384]{1,0:T(8,128)(2,1)S(1)}, u32[]{:S(2)}, u32[]{:S(2)}) collective-permute-start(bf16[32,384]{1,0:T(8,128)(2,1)S(1)} %get-tuple-element.22), channel_id=1, source_target_pairs={{0,2},{2,0},{4,6},{6,4},{8,10},{10,8},{12,14},{14,12},{1,3},{3,1},... | collective-permute-start | bytes 73736 | tf_op jit(solution)/shard_map/ppermute | solution.py:195
  22.9 1.3 %collective-permute-start.8 = (bf16[8,3072]{1,0:T(8,128)(2,1)S(1)}, bf16[8,3072]{1,0:T(8,128)(2,1)S(1)}, u32[]{:S(2)}, u32[]{:S(2)}) collective-permute-start(bf16[8,3072]{1,0:T(8,128)(2,1)S(1)} %get-tuple-element.28), channel_id=1, source_target_pairs={{0,1},{1,0},{2,3},{3,2},{4,5},{5,4},{6,7},{7,6},{8,9},{9,8},{10,11... | collective-permute-start | bytes 147464 | tf_op jit(solution)/shard_map/ppermute | solution.py:240

commit v3 on v2

--- a/solution.py
+++ b/solution.py
@@ -18,15 +18,14 @@
     return (value + step - 1) // step * step
 
 
-def pack_kernel(sizes, text_hbm, table_hbm, stale_hbm, step_hbm, query_hbm, own_ref, other_ref, local_ref, pair_ref, bias_ref,
-                text_ref, table_ref, stale, step, query, sems):
-    strips, lat_rows, text_rows = sizes
+def pack_kernel(sizes, table_hbm, stale_hbm, step_hbm, query_hbm, own_ref, other_ref, local_ref, pair_ref, mask_ref,
+                table_ref, stale, step, query, sems):
+    text_rows = sizes
     copies = [
         pltpu.make_async_copy(stale_hbm, stale, sems.at[0]),
         pltpu.make_async_copy(step_hbm, step, sems.at[1]),
         pltpu.make_async_copy(query_hbm, query, sems.at[2]),
-        pltpu.make_async_copy(text_hbm, text_ref, sems.at[3]),
-        pltpu.make_async_copy(table_hbm, table_ref, sems.at[4]),
+        pltpu.make_async_copy(table_hbm, table_ref, sems.at[3]),
     ]
     for copy in copies:
         copy.start()
@@ -36,9 +35,8 @@
     for copy in copies:
         copy.wait()
     early = table_ref[5:6, :]
-    live = (early < 0) | ((strip ^ table_ref[4:5, :]) * text_rows + early < text_ref[0])
-    for c in range(4):
-        bias_ref[c : c + 1, :] = jnp.where((table_ref[c : c + 1, :] > 0) & live, 0.0, MASKED)
+    mask_ref[0:4, :] = table_ref[0:4, :]
+    mask_ref[4:5, :] = jnp.where(early < 0, -1, (strip ^ table_ref[4:5, :]) * text_rows + early)
 
     def pick(ref, lead, which):
         lanes = pl.ds(pl.multiple_of(which * half, LANES), half)
@@ -55,36 +53,43 @@
         rest_ref[...] = jnp.concatenate([rest, jnp.zeros((spare, half), rest.dtype)], axis=0) if spare else rest
 
 
-def attention_kernel(sizes, bias_ref, own_ref, local_ref, pair_ref, *refs):
-    set_rows, query_rows, columns = sizes
+def attention_kernel(sizes, text_ref, mask_ref, own_ref, local_ref, pair_ref, *refs):
+    set_rows, query_rows = sizes
     others, (mine_ref, back_ref) = refs[:-2], refs[-2:]
     pair_rows = 2 * set_rows
-    per_class = query_rows // 2
+    columns = mask_ref.shape[1]
     scale = 1.0 / HDIM**0.5
+    live = mask_ref[4:5, :] < text_ref[0]
     bias = jnp.concatenate(
-        [jnp.broadcast_to(bias_ref[c : c + 1, :], (per_class, columns)) for c in range(4)], axis=0
+        [
+            jnp.broadcast_to(jnp.where((mask_ref[c : c + 1, :] > 0) & live, 0.0, MASKED), (query_rows // 2, columns))
+            for c in range(4)
+        ],
+        axis=0,
     )
-    for head in range(own_ref.shape[1] // HDIM):
-        lanes = slice(head * HDIM, (head + 1) * HDIM)
+    lane_blocks = [slice(i, i + HDIM) for i in range(0, own_ref.shape[1], HDIM)]
+    keys, scores = [], []
+    for lanes in lane_blocks:
         rows = [own_ref[:, lanes], pair_ref[:pair_rows, lanes]]
         rows += [ref[:, lanes] for ref in others]
         rows += [local_ref[query_rows:, lanes], pair_ref[pair_rows + query_rows :, lanes]]
         filled = sum(r.shape[0] for r in rows)
         if filled < columns:
             rows.append(jnp.zeros((columns - filled, HDIM), jnp.bfloat16))
-        keys = jnp.concatenate(rows, axis=0)
+        keys.append(jnp.concatenate(rows, axis=0))
         queries = jnp.concatenate(
             [local_ref[:query_rows, lanes], pair_ref[pair_rows : pair_rows + query_rows, lanes]], axis=0
         )
-        scores = lax.dot_general(
-            queries, keys, (((1,), (1,)), ((), ())), preferred_element_type=jnp.float32
+        scores.append(
+            lax.dot_general(queries, keys[-1], (((1,), (1,)), ((), ())), preferred_element_type=jnp.float32)
+            * scale
+            + bias
         )
-        scores = scores * scale + bias
-        top = jnp.max(scores, axis=1, keepdims=True)
-        expo = jnp.exp(scores - top)
-        weights = expo / jnp.sum(expo, axis=1, keepdims=True)
-        weights = pltpu.roll(weights, 1, 1).astype(jnp.bfloat16)
-        mixed = jnp.dot(weights, keys, preferred_element_type=jnp.float32).astype(jnp.bfloat16)
+    expos = [jnp.exp(score - jnp.max(score, axis=1, keepdims=True)) for score in scores]
+    weights = [expo / jnp.sum(expo, axis=1, keepdims=True) for expo in expos]
+    for lanes, weight, key in zip(lane_blocks, weights, keys):
+        weight = pltpu.roll(weight, 1, 1).astype(jnp.bfloat16)
+        mixed = jnp.dot(weight, key, preferred_element_type=jnp.float32).astype(jnp.bfloat16)
         mine_ref[:, lanes] = mixed[:query_rows]
         back_ref[:, lanes] = mixed[query_rows:]
 
@@ -143,6 +148,7 @@
     set_rows = 2 * strip_rows
     query_rows = 2 * lat_rows
     block_rows = 2 * set_rows
+    smem = pl.BlockSpec(memory_space=pltpu.SMEM)
     vmem = pl.BlockSpec(memory_space=pltpu.VMEM)
     hbm = pl.BlockSpec(memory_space=pltpu.HBM)
     params = pltpu.CompilerParams(vmem_limit_bytes=VMEM_LIMIT)
@@ -169,27 +175,26 @@
     bf16 = functools.partial(jax.ShapeDtypeStruct, dtype=jnp.bfloat16)
     f32 = functools.partial(jax.ShapeDtypeStruct, dtype=jnp.float32)
     local_rows = query_rows + set_rows
-    own, other, local, pair, bias = pl.pallas_call(
-        functools.partial(pack_kernel, (strips, lat_rows, text_rows)),
+    own, other, local, pair, mask = pl.pallas_call(
+        functools.partial(pack_kernel, text_rows),
         out_shape=(
             bf16((block_rows, half)),
             bf16((block_rows, half)),
             bf16((local_rows, half)),
             bf16((block_rows + local_rows, half)),
-            f32((4, columns)),
+            jax.ShapeDtypeStruct((5, columns), jnp.int32),
         ),
-        in_specs=[hbm] * 5,
+        in_specs=[hbm] * 4,
         out_specs=(vmem,) * 5,
         scratch_shapes=[
-            pltpu.SMEM(text_len.shape, jnp.int32),
             pltpu.VMEM(table.shape, jnp.int32),
             pltpu.VMEM((strip_rows, 2, width), jnp.bfloat16),
             pltpu.VMEM((2, strip_rows, 2, width), jnp.bfloat16),
             pltpu.VMEM((2, lat_rows, width), jnp.bfloat16),
-            pltpu.SemaphoreType.DMA((5,)),
+            pltpu.SemaphoreType.DMA((4,)),
         ],
         compiler_params=params,
-    )(text_len, *in_hbm(jnp.asarray(table), stale_pairs.transpose(1, 0, 2), step_pairs.transpose(0, 2, 1, 3), queries))
+    )(*in_hbm(jnp.asarray(table), stale_pairs.transpose(1, 0, 2), step_pairs.transpose(0, 2, 1, 3), queries))
 
     def to(rows, flip):
         return lax.ppermute(rows, "patch", [(i, i ^ flip) for i in range(strips)])
@@ -208,10 +213,12 @@
         bit //= 2
 
     mine, back = pl.pallas_call(
-        functools.partial(attention_kernel, (set_rows, query_rows, columns)),
+        functools.partial(attention_kernel, (set_rows, query_rows)),
         out_shape=(bf16((query_rows, half)),) * 2,
-        compiler_params=params,
-    )(bias, own, local, pair_rows, *[held[flip] for flip in flips])
+        in_specs=[smem] + [vmem] * (4 + len(flips)),
+        out_specs=(vmem, vmem),
+        compiler_params=params,
+    )(text_len, mask, own, local, pair_rows, *[held[flip] for flip in flips])
     returned = to(back, 1)
 
     model = out_weight.shape[1]

time: 25 us -> 23.6 us (0.944)
  Pallas kernels: 5.71 us -> 4.93 us
  waiting for transfers between devices: 5.42 us -> 4.76 us
    pallas_call x2, Pallas kernels: 2.62 us -> 1.84 us  [the longest x1 1.02 us: per_device(): pl.pallas_call(functools.partial(pack_kernel, text_rows), out_shape=(bf16...]
    ppermute x8, waiting for transfers between devices: 4.2 us -> 3.54 us  [to(): return lax.ppermute(rows, 'patch', [(i, i ^ flip) for i in range(strips)])]
  transfers between devices with their start and end apart: 9 -> 9, of which waited for: 6 -> 6; matrix products, arithmetic and copies ran while one was open for 0% -> 0% of each run, Pallas kernels for 10% -> 11%
where the time goes in v3:
time: 23.6 us; the launch traced here: 23.4 us
  starting transfers between devices  12.4 us (53%)
  Pallas kernels  4.93 us (21%)
  waiting for transfers between devices  4.76 us (20%)
  between operations  0.7 us (3%)
  other arithmetic  0.63 us (3%)
    ppermute x8, starting transfers between devices, to(): return lax.ppermute(rows, 'patch', [(i, i ^ flip) for i in range(strips)])  12.3 us
    ppermute x8, waiting for transfers between devices, to(): return lax.ppermute(rows, 'patch', [(i, i ^ flip) for i in range(strips)])  3.54 us
    pallas_call x1, Pallas kernels, per_device(): pl.pallas_call(first_half_kernel, out_shape=(f32((lat_rows, model)), f32(...  2.56 us
    ppermute x1, waiting for transfers between devices, per_device(): received = lax.ppermute(send, 'head', [(0, 1), (1, 0)])  1.22 us
    pallas_call x1, Pallas kernels, per_device(): pl.pallas_call(functools.partial(pack_kernel, text_rows), out_shape=(bf16...  1.02 us
    pallas_call x1, Pallas kernels, per_device(): pl.pallas_call(functools.partial(attention_kernel, (set_rows, query_rows)...  0.82 us
    convert_element_type x1, other arithmetic, per_device(): return (keep + received.astype(jnp.float32)).astype(jnp.bfloat16)  0.63 us
    pallas_call x1, Pallas kernels, per_device(): pl.pallas_call(second_half_kernel, out_shape=(f32((lat_rows // 2, model))...  0.52 us
  transfers between devices with their start and end apart: 9, of which 6 were waited for; matrix products, arithmetic and copies ran while one was open for 0% of the time, Pallas kernels for 11%

profile of v3, /device:TPU:0, one launch (start us, length us, event | category | flops | bytes accessed | tf_op | source)
XLA Modules:
  0.0 23.4 jit_solution(10312351901095762340)
XLA Ops:
  0.0 1.0 %shard_map.91 = (bf16[80,384]{1,0:T(8,128)(2,1)S(1)}, bf16[80,384]{1,0:T(8,128)(2,1)S(1)}, bf16[72,384]{1,0:T(8,128)(2,1)S(1)}, bf16[152,384]{1,0:T(8,128)(2,1)S(1)}, s32[5,768]{1,0:T(8,128)S(1)}) custom-call(s32[8,768]{1,0:T(8,128)} %constant.2.clone.table_hbm, bf16[20,2,768]{2,1,0:T(2,128)(2,1)} %bitcast.3, bf16[2,20,2,768]{3,2,1,0:T(2,128)(2,1)} %bitcast.2, ...), custom_call_target="tpu_custom_call" | custom-call | tf_op jit(solution)/shard_map/pallas_call | solution.py:178
  1.0 5.0 %collective-permute-start.4 = (bf16[80,384]{1,0:T(8,128)(2,1)S(1)}, bf16[80,384]{1,0:T(8,128)(2,1)S(1)}, u32[]{:S(2)}, u32[]{:S(2)}) collective-permute-start(bf16[80,384]{1,0:T(8,128)(2,1)S(1)} %get-tuple-element.21), channel_id=1, source_target_pairs={{0,10},{2,8},{4,14},{6,12},{8,2},{10,0},{12,6},{14,4},{1,11},{3,9}... | collective-permute-start | bytes 184328 | tf_op jit(solution)/shard_map/ppermute | solution.py:200
  6.1 0.3 %collective-permute-start.3 = (bf16[80,384]{1,0:T(8,128)(2,1)S(1)}, bf16[80,384]{1,0:T(8,128)(2,1)S(1)}, u32[]{:S(2)}, u32[]{:S(2)}) collective-permute-start(bf16[80,384]{1,0:T(8,128)(2,1)S(1)} %get-tuple-element.18.own_ref), channel_id=1, source_target_pairs={{0,8},{2,10},{4,12},{6,14},{8,0},{10,2},{12,4},{14,6},{1,9},{3,11}... | collective-permute-start | bytes 184328 | tf_op jit(solution)/shard_map/ppermute | solution.py:200
  6.4 0.3 %collective-permute-start = (bf16[152,384]{1,0:T(8,128)(2,1)S(1)}, bf16[152,384]{1,0:T(8,128)(2,1)S(1)}, u32[]{:S(2)}, u32[]{:S(2)}) collective-permute-start(bf16[152,384]{1,0:T(8,128)(2,1)S(1)} %get-tuple-element.20), channel_id=1, source_target_pairs={{0,2},{2,0},{4,6},{6,4},{8,10},{10,8},{12,14},{14,12},{1,3},{3,1},... | collective-permute-start | bytes 350216 | tf_op jit(solution)/shard_map/ppermute | solution.py:200
  6.7 2.7 %collective-permute-start.2 = (bf16[80,384]{1,0:T(8,128)(2,1)S(1)}, bf16[80,384]{1,0:T(8,128)(2,1)S(1)}, u32[]{:S(2)}, u32[]{:S(2)}) collective-permute-start(bf16[80,384]{1,0:T(8,128)(2,1)S(1)} %get-tuple-element.21), channel_id=1, source_target_pairs={{0,6},{2,4},{4,2},{6,0},{8,14},{10,12},{12,10},{14,8},{1,7},{3,5},... | collective-permute-start | bytes 184328 | tf_op jit(solution)/shard_map/ppermute | solution.py:200
  9.4 0.4 %collective-permute-start.1 = (bf16[80,384]{1,0:T(8,128)(2,1)S(1)}, bf16[80,384]{1,0:T(8,128)(2,1)S(1)}, u32[]{:S(2)}, u32[]{:S(2)}) collective-permute-start(bf16[80,384]{1,0:T(8,128)(2,1)S(1)} %get-tuple-element.18.own_ref), channel_id=1, source_target_pairs={{0,4},{2,6},{4,0},{6,2},{8,12},{10,14},{12,8},{14,10},{1,5},{3,7},... | collective-permute-start | bytes 184328 | tf_op jit(solution)/shard_map/ppermute | solution.py:200
  9.9 0.0 collective-permute-done.4.refs_3_
  9.9 1.6 %collective-permute-start.6 = (bf16[80,384]{1,0:T(8,128)(2,1)S(1)}, bf16[80,384]{1,0:T(8,128)(2,1)S(1)}, u32[]{:S(2)}, u32[]{:S(2)}) collective-permute-start(bf16[80,384]{1,0:T(8,128)(2,1)S(1)} %collective-permute-done.4.refs_3_), channel_id=1, source_target_pairs={{0,4},{2,6},{4,0},{6,2},{8,12},{10,14},{12,8},{14,10},{1,5},{3,7},... | collective-permute-start | bytes 184328 | tf_op jit(solution)/shard_map/ppermute | solution.py:200
  11.5 0.5 %collective-permute-done.3.refs_2_ = bf16[80,384]{1,0:T(8,128)(2,1)S(1)} collective-permute-done((bf16[80,384]{1,0:T(8,128)(2,1)S(1)}, bf16[80,384]{1,0:T(8,128)(2,1)S(1)}, u32[]{:S(2)}, u32[]{:S(2)}) %collective-permute-start.3) | collective-permute-done | bytes 61472 | tf_op jit(solution)/shard_map/ppermute | solution.py:200
  12.0 1.4 %collective-permute-start.5 = (bf16[80,384]{1,0:T(8,128)(2,1)S(1)}, bf16[80,384]{1,0:T(8,128)(2,1)S(1)}, u32[]{:S(2)}, u32[]{:S(2)}) collective-permute-start(bf16[80,384]{1,0:T(8,128)(2,1)S(1)} %collective-permute-done.3.refs_2_), channel_id=1, source_target_pairs={{0,4},{2,6},{4,0},{6,2},{8,12},{10,14},{12,8},{14,10},{1,5},{3,7},... | collective-permute-start | bytes 184328 | tf_op jit(solution)/shard_map/ppermute | solution.py:200
  14.0 0.0 collective-permute-done.2.refs_1_
  14.0 0.5 %collective-permute-done.1.refs_0_ = bf16[80,384]{1,0:T(8,128)(2,1)S(1)} collective-permute-done((bf16[80,384]{1,0:T(8,128)(2,1)S(1)}, bf16[80,384]{1,0:T(8,128)(2,1)S(1)}, u32[]{:S(2)}, u32[]{:S(2)}) %collective-permute-start.1) | collective-permute-done | bytes 61472 | tf_op jit(solution)/shard_map/ppermute | solution.py:200
  14.5 0.0 collective-permute-done.pair_ref
  14.5 1.1 %collective-permute-done.6.refs_5_ = bf16[80,384]{1,0:T(8,128)(2,1)S(1)} collective-permute-done((bf16[80,384]{1,0:T(8,128)(2,1)S(1)}, bf16[80,384]{1,0:T(8,128)(2,1)S(1)}, u32[]{:S(2)}, u32[]{:S(2)}) %collective-permute-start.6) | collective-permute-done | bytes 61472 | tf_op jit(solution)/shard_map/ppermute | solution.py:200
  15.6 0.7 %collective-permute-done.5.refs_4_ = bf16[80,384]{1,0:T(8,128)(2,1)S(1)} collective-permute-done((bf16[80,384]{1,0:T(8,128)(2,1)S(1)}, bf16[80,384]{1,0:T(8,128)(2,1)S(1)}, u32[]{:S(2)}, u32[]{:S(2)}) %collective-permute-start.5) | collective-permute-done | bytes 61472 | tf_op jit(solution)/shard_map/ppermute | solution.py:200
  16.2 0.8 %shard_map.92 = (bf16[32,384]{1,0:T(8,128)(2,1)S(1)}, bf16[32,384]{1,0:T(8,128)(2,1)S(1)}) custom-call(s32[1]{0:T(128)S(6)} %copy.10.text_ref, s32[5,768]{1,0:T(8,128)S(1)} %get-tuple-element.17.mask_ref, bf16[80,384]{1,0:T(8,128)(2,1)S(1)} %get-tuple-element.18.own_ref, bf16[72,384]{1,0:T(8,128)(2,1)S(1)} %get-tuple-element.19.local_ref, ...), custom_call_target="tpu_custom_call" | custom-call | tf_op jit(solution)/shard_map/pallas_call | solution.py:215
  17.1 0.5 %collective-permute-start.7 = (bf16[32,384]{1,0:T(8,128)(2,1)S(1)}, bf16[32,384]{1,0:T(8,128)(2,1)S(1)}, u32[]{:S(2)}, u32[]{:S(2)}) collective-permute-start(bf16[32,384]{1,0:T(8,128)(2,1)S(1)} %get-tuple-element.22), channel_id=1, source_target_pairs={{0,2},{2,0},{4,6},{6,4},{8,10},{10,8},{12,14},{14,12},{1,3},{3,1},... | collective-permute-start | bytes 73736 | tf_op jit(solution)/shard_map/ppermute | solution.py:200
  17.5 2.6 %shard_map.93 = (f32[16,3072]{1,0:T(8,128)S(1)}, f32[2,3072]{1,0:T(2,128)S(1)}, bf16[384,3072]{1,0:T(8,128)(2,1)S(1)}) custom-call(bf16[32,384]{1,0:T(8,128)(2,1)S(1)} %get-tuple-element.23.attended_ref, s32[2]{0:T(128)} %plan_hbm.1, bf16[28,3072]{1,0:T(8,128)(2,1)} %table_hbm.2, bf16[16,1536]{1,0:T(8,128)(2,1)} %hidden_hbm.1, bf16[768,3072]{1,0:T(8,128)(2,1)} %weight_hbm.1), custom_call_target="tpu_custom_call" | custom-call | tf_op jit(solution)/shard_map/pallas_call | solution.py:225
  20.1 0.8 %collective-permute-done.7.attended_ref = bf16[32,384]{1,0:T(8,128)(2,1)S(1)} collective-permute-done((bf16[32,384]{1,0:T(8,128)(2,1)S(1)}, bf16[32,384]{1,0:T(8,128)(2,1)S(1)}, u32[]{:S(2)}, u32[]{:S(2)}) %collective-permute-start.7) | collective-permute-done | bytes 24608 | tf_op jit(solution)/shard_map/ppermute | solution.py:200
  20.9 0.5 %shard_map.94 = (f32[8,3072]{1,0:T(8,128)S(1)}, bf16[8,3072]{1,0:T(8,128)(2,1)S(1)}) custom-call(bf16[32,384]{1,0:T(8,128)(2,1)S(1)} %collective-permute-done.7.attended_ref, bf16[384,3072]{1,0:T(8,128)(2,1)S(1)} %get-tuple-element.24.weight_ref, f32[2,3072]{1,0:T(2,128)S(1)} %get-tuple-element.25.gates_ref, f32[16,3072]{1,0:T(8,128)S(1)} %get-tuple-element.26.sum_ref), custom_call_target="tpu_custom_call" | custom-call | tf_op jit(solution)/shard_map/pallas_call | solution.py:239
  21.5 0.1 collective-permute-start.8
  21.6 1.2 %collective-permute-done.8 = bf16[8,3072]{1,0:T(8,128)(2,1)S(1)} collective-permute-done((bf16[8,3072]{1,0:T(8,128)(2,1)S(1)}, bf16[8,3072]{1,0:T(8,128)(2,1)S(1)}, u32[]{:S(2)}, u32[]{:S(2)}) %collective-permute-start.8) | collective-permute-done | bytes 49184 | tf_op jit(solution)/shard_map/ppermute | solution.py:247
  22.8 0.6 %add_convert_fusion = bf16[8,3072]{1,0:T(8,128)(2,1)} fusion(f32[8,3072]{1,0:T(8,128)S(1)} %get-tuple-element.27, bf16[8,3072]{1,0:T(8,128)(2,1)S(1)} %collective-permute-done.8), kind=kLoop, calls=%fused_computation | loop fusion | flops 73728 | bytes 196608 | tf_op jit(solution)/shard_map/convert_element_type | solution.py:248
Async XLA Ops:
  1.0 8.9 %collective-permute-start.4 = (bf16[80,384]{1,0:T(8,128)(2,1)S(1)}, bf16[80,384]{1,0:T(8,128)(2,1)S(1)}, u32[]{:S(2)}, u32[]{:S(2)}) collective-permute-start(bf16[80,384]{1,0:T(8,128)(2,1)S(1)} %get-tuple-element.21), channel_id=1, source_target_pairs={{0,10},{2,8},{4,14},{6,12},{8,2},{10,0},{12,6},{14,4},{1,11},{3,9}... | collective-permute-start | bytes 184328 | tf_op jit(solution)/shard_map/ppermute | solution.py:200
  6.1 5.9 %collective-permute-start.3 = (bf16[80,384]{1,0:T(8,128)(2,1)S(1)}, bf16[80,384]{1,0:T(8,128)(2,1)S(1)}, u32[]{:S(2)}, u32[]{:S(2)}) collective-permute-start(bf16[80,384]{1,0:T(8,128)(2,1)S(1)} %get-tuple-element.18.own_ref), channel_id=1, source_target_pairs={{0,8},{2,10},{4,12},{6,14},{8,0},{10,2},{12,4},{14,6},{1,9},{3,11}... | collective-permute-start | bytes 184328 | tf_op jit(solution)/shard_map/ppermute | solution.py:200
  6.4 8.1 %collective-permute-start = (bf16[152,384]{1,0:T(8,128)(2,1)S(1)}, bf16[152,384]{1,0:T(8,128)(2,1)S(1)}, u32[]{:S(2)}, u32[]{:S(2)}) collective-permute-start(bf16[152,384]{1,0:T(8,128)(2,1)S(1)} %get-tuple-element.20), channel_id=1, source_target_pairs={{0,2},{2,0},{4,6},{6,4},{8,10},{10,8},{12,14},{14,12},{1,3},{3,1},... | collective-permute-start | bytes 350216 | tf_op jit(solution)/shard_map/ppermute | solution.py:200
  6.7 7.3 %collective-permute-start.2 = (bf16[80,384]{1,0:T(8,128)(2,1)S(1)}, bf16[80,384]{1,0:T(8,128)(2,1)S(1)}, u32[]{:S(2)}, u32[]{:S(2)}) collective-permute-start(bf16[80,384]{1,0:T(8,128)(2,1)S(1)} %get-tuple-element.21), channel_id=1, source_target_pairs={{0,6},{2,4},{4,2},{6,0},{8,14},{10,12},{12,10},{14,8},{1,7},{3,5},... | collective-permute-start | bytes 184328 | tf_op jit(solution)/shard_map/ppermute | solution.py:200
  9.4 5.1 %collective-permute-start.1 = (bf16[80,384]{1,0:T(8,128)(2,1)S(1)}, bf16[80,384]{1,0:T(8,128)(2,1)S(1)}, u32[]{:S(2)}, u32[]{:S(2)}) collective-permute-start(bf16[80,384]{1,0:T(8,128)(2,1)S(1)} %get-tuple-element.18.own_ref), channel_id=1, source_target_pairs={{0,4},{2,6},{4,0},{6,2},{8,12},{10,14},{12,8},{14,10},{1,5},{3,7},... | collective-permute-start | bytes 184328 | tf_op jit(solution)/shard_map/ppermute | solution.py:200
  9.9 5.7 %collective-permute-start.6 = (bf16[80,384]{1,0:T(8,128)(2,1)S(1)}, bf16[80,384]{1,0:T(8,128)(2,1)S(1)}, u32[]{:S(2)}, u32[]{:S(2)}) collective-permute-start(bf16[80,384]{1,0:T(8,128)(2,1)S(1)} %collective-permute-done.4.refs_3_), channel_id=1, source_target_pairs={{0,4},{2,6},{4,0},{6,2},{8,12},{10,14},{12,8},{14,10},{1,5},{3,7},... | collective-permute-start | bytes 184328 | tf_op jit(solution)/shard_map/ppermute | solution.py:200
  12.0 4.3 %collective-permute-start.5 = (bf16[80,384]{1,0:T(8,128)(2,1)S(1)}, bf16[80,384]{1,0:T(8,128)(2,1)S(1)}, u32[]{:S(2)}, u32[]{:S(2)}) collective-permute-start(bf16[80,384]{1,0:T(8,128)(2,1)S(1)} %collective-permute-done.3.refs_2_), channel_id=1, source_target_pairs={{0,4},{2,6},{4,0},{6,2},{8,12},{10,14},{12,8},{14,10},{1,5},{3,7},... | collective-permute-start | bytes 184328 | tf_op jit(solution)/shard_map/ppermute | solution.py:200
  17.1 3.9 %collective-permute-start.7 = (bf16[32,384]{1,0:T(8,128)(2,1)S(1)}, bf16[32,384]{1,0:T(8,128)(2,1)S(1)}, u32[]{:S(2)}, u32[]{:S(2)}) collective-permute-start(bf16[32,384]{1,0:T(8,128)(2,1)S(1)} %get-tuple-element.22), channel_id=1, source_target_pairs={{0,2},{2,0},{4,6},{6,4},{8,10},{10,8},{12,14},{14,12},{1,3},{3,1},... | collective-permute-start | bytes 73736 | tf_op jit(solution)/shard_map/ppermute | solution.py:200
  21.5 1.3 %collective-permute-start.8 = (bf16[8,3072]{1,0:T(8,128)(2,1)S(1)}, bf16[8,3072]{1,0:T(8,128)(2,1)S(1)}, u32[]{:S(2)}, u32[]{:S(2)}) collective-permute-start(bf16[8,3072]{1,0:T(8,128)(2,1)S(1)} %get-tuple-element.28), channel_id=1, source_target_pairs={{0,1},{1,0},{2,3},{3,2},{4,5},{5,4},{6,7},{7,6},{8,9},{9,8},{10,11... | collective-permute-start | bytes 147464 | tf_op jit(solution)/shard_map/ppermute | solution.py:247

commit v4 on v3

--- a/solution.py
+++ b/solution.py
@@ -11,6 +11,7 @@
 HDIM = 128
 LANES = 128
 MASKED = -1e30
+PAIR = 2
 VMEM_LIMIT = 24 * 1024 * 1024
 
 
@@ -18,9 +19,12 @@
     return (value + step - 1) // step * step
 
 
-def pack_kernel(sizes, table_hbm, stale_hbm, step_hbm, query_hbm, own_ref, other_ref, local_ref, pair_ref, mask_ref,
+def side_of(strip):
+    return lax.rem(lax.div(strip, PAIR), 2)
+
+
+def pack_kernel(text_rows, table_hbm, stale_hbm, step_hbm, query_hbm, own_ref, send_ref, other_ref, local_ref, pair_ref, mask_ref,
                 table_ref, stale, step, query, sems):
-    text_rows = sizes
     copies = [
         pltpu.make_async_copy(stale_hbm, stale, sems.at[0]),
         pltpu.make_async_copy(step_hbm, step, sems.at[1]),
@@ -30,7 +34,7 @@
     for copy in copies:
         copy.start()
     strip = lax.axis_index("patch")
-    side = lax.rem(strip, 2)
+    side = side_of(strip)
     half = own_ref.shape[1]
     for copy in copies:
         copy.wait()
@@ -47,49 +51,83 @@
         block = jnp.concatenate([pick(stale, (), which), pick(step, (0,), which)], axis=0)
         rest = jnp.concatenate([pick(query, (), which), pick(step, (1,), which)], axis=0)
         block_ref[...] = block
+        if block_ref is own_ref:
+            send_ref[...] = block
         if rest_ref is pair_ref:
             rest = jnp.concatenate([block, rest], axis=0)
         spare = rest_ref.shape[0] - rest.shape[0]
         rest_ref[...] = jnp.concatenate([rest, jnp.zeros((spare, half), rest.dtype)], axis=0) if spare else rest
 
 
-def attention_kernel(sizes, text_ref, mask_ref, own_ref, local_ref, pair_ref, *refs):
-    set_rows, query_rows = sizes
+def blocks_of(ref):
+    return [slice(i, i + HDIM) for i in range(0, ref.shape[-1], HDIM)]
+
+
+def queries_of(local_ref, pair_ref, query_rows, lanes):
+    block_rows = pair_ref.shape[0] - local_ref.shape[0]
+    return jnp.concatenate(
+        [local_ref[:query_rows, lanes], pair_ref[block_rows : block_rows + query_rows, lanes]], axis=0
+    )
+
+
+def scored(queries, parts, bias):
+    filled = sum(part.shape[0] for part in parts)
+    if filled < bias.shape[1]:
+        parts = parts + [jnp.zeros((bias.shape[1] - filled, HDIM), jnp.bfloat16)]
+    rows = jnp.concatenate(parts, axis=0)
+    scores = lax.dot_general(queries, rows, (((1,), (1,)), ((), ())), preferred_element_type=jnp.float32)
+    return rows, scores * (1.0 / HDIM**0.5) + bias
+
+
+def weigh(expo, rows):
+    return jnp.dot(pltpu.roll(expo, 1, 1).astype(jnp.bfloat16), rows, preferred_element_type=jnp.float32)
+
+
+def spread(bias, count):
+    return jnp.concatenate(
+        [jnp.broadcast_to(bias[c : c + 1, :], (count, bias.shape[1])) for c in range(bias.shape[0])], axis=0
+    )
+
+
+def early_attention_kernel(sizes, text_ref, mask_ref, own_ref, local_ref, pair_ref, *refs):
+    query_rows, columns = sizes
+    others, (mixed_ref, top_ref, norm_ref, bias_ref) = refs[:-4], refs[-4:]
+    block_rows = own_ref.shape[0]
+    live = mask_ref[4:5, :] < text_ref[0]
+    bias = jnp.where((mask_ref[0:4, :] > 0) & live, 0.0, MASKED)
+    bias_ref[...] = bias[:, columns:]
+    bias = spread(bias[:, :columns], query_rows // 2)
+    work = []
+    for lanes in blocks_of(own_ref):
+        parts = [own_ref[:, lanes], pair_ref[:block_rows, lanes]] + [ref[:, lanes] for ref in others]
+        parts += [local_ref[query_rows:, lanes], pair_ref[block_rows + query_rows :, lanes]]
+        work.append(scored(queries_of(local_ref, pair_ref, query_rows, lanes), parts, bias))
+    tops = [jnp.max(scores, axis=1, keepdims=True) for _, scores in work]
+    expos = [jnp.exp(scores - top) for (_, scores), top in zip(work, tops)]
+    for lanes, (rows, _), top, expo in zip(blocks_of(own_ref), work, tops, expos):
+        shape = (2 * query_rows, HDIM)
+        mixed_ref[:, lanes] = weigh(expo, rows)
+        top_ref[:, lanes] = jnp.broadcast_to(top, shape)
+        norm_ref[:, lanes] = jnp.broadcast_to(jnp.sum(expo, axis=1, keepdims=True), shape)
+
+
+def late_attention_kernel(query_rows, bias_ref, local_ref, pair_ref, mixed_ref, top_ref, norm_ref, *refs):
     others, (mine_ref, back_ref) = refs[:-2], refs[-2:]
-    pair_rows = 2 * set_rows
-    columns = mask_ref.shape[1]
-    scale = 1.0 / HDIM**0.5
-    live = mask_ref[4:5, :] < text_ref[0]
-    bias = jnp.concatenate(
-        [
-            jnp.broadcast_to(jnp.where((mask_ref[c : c + 1, :] > 0) & live, 0.0, MASKED), (query_rows // 2, columns))
-            for c in range(4)
-        ],
-        axis=0,
-    )
-    lane_blocks = [slice(i, i + HDIM) for i in range(0, own_ref.shape[1], HDIM)]
-    keys, scores = [], []
-    for lanes in lane_blocks:
-        rows = [own_ref[:, lanes], pair_ref[:pair_rows, lanes]]
-        rows += [ref[:, lanes] for ref in others]
-        rows += [local_ref[query_rows:, lanes], pair_ref[pair_rows + query_rows :, lanes]]
-        filled = sum(r.shape[0] for r in rows)
-        if filled < columns:
-            rows.append(jnp.zeros((columns - filled, HDIM), jnp.bfloat16))
-        keys.append(jnp.concatenate(rows, axis=0))
-        queries = jnp.concatenate(
-            [local_ref[:query_rows, lanes], pair_ref[pair_rows : pair_rows + query_rows, lanes]], axis=0
-        )
-        scores.append(
-            lax.dot_general(queries, keys[-1], (((1,), (1,)), ((), ())), preferred_element_type=jnp.float32)
-            * scale
-            + bias
-        )
-    expos = [jnp.exp(score - jnp.max(score, axis=1, keepdims=True)) for score in scores]
-    weights = [expo / jnp.sum(expo, axis=1, keepdims=True) for expo in expos]
-    for lanes, weight, key in zip(lane_blocks, weights, keys):
-        weight = pltpu.roll(weight, 1, 1).astype(jnp.bfloat16)
-        mixed = jnp.dot(weight, key, preferred_element_type=jnp.float32).astype(jnp.bfloat16)
+    bias = spread(bias_ref[...], query_rows // 2)
+    lane_blocks = blocks_of(local_ref)
+    work = [
+        scored(queries_of(local_ref, pair_ref, query_rows, lanes), [ref[:, lanes] for ref in others], bias)
+        for lanes in lane_blocks
+    ]
+    tops = [
+        jnp.maximum(jnp.max(scores, axis=1, keepdims=True), top_ref[:, lanes])
+        for lanes, (_, scores) in zip(lane_blocks, work)
+    ]
+    expos = [jnp.exp(scores - top[:, :1]) for (_, scores), top in zip(work, tops)]
+    for lanes, (rows, _), top, expo in zip(lane_blocks, work, tops, expos):
+        shrink = jnp.exp(top_ref[:, lanes] - top)
+        norm = norm_ref[:, lanes] * shrink + jnp.sum(expo, axis=1, keepdims=True)
+        mixed = ((mixed_ref[:, lanes] * shrink + weigh(expo, rows)) / norm).astype(jnp.bfloat16)
         mine_ref[:, lanes] = mixed[:query_rows]
         back_ref[:, lanes] = mixed[query_rows:]
 
@@ -104,7 +142,7 @@
                       plan_ref, table_ref, hidden_ref, near, sems):
     depth = attended_ref.shape[1]
     width = hidden_ref.shape[1]
-    side = lax.rem(lax.axis_index("patch"), 2)
+    side = side_of(lax.axis_index("patch"))
     rows = pl.ds(pl.multiple_of(side * depth, depth), depth)
     far_rows = pl.ds(pl.multiple_of((1 - side) * depth, depth), depth)
     near_copy = pltpu.make_async_copy(weight_hbm.at[rows, :], near, sems.at[0])
@@ -156,28 +194,30 @@
     def in_hbm(*arrays):
         return [pltpu.with_memory_space_constraint(array, pltpu.HBM) for array in arrays]
 
-    flips = list(range(2, strips))
-    blocks = [0, 1] + flips
-    filled = block_rows * len(blocks) + 2 * set_rows
-    columns = round_up(filled, LANES)
-    column = np.arange(columns)
-    in_blocks = column < block_rows * len(blocks)
-    block = np.minimum(column // block_rows, len(blocks) - 1)
-    within = column % block_rows
-    flip = np.where(in_blocks, np.asarray(blocks)[block], within // set_rows)
-    kind = np.where(in_blocks, within // set_rows, np.where(column < filled, 2, 3))
-    token = (within % set_rows) // 2
-    whose, step = np.asarray([0, 0, 1, 1])[:, None], np.asarray([0, 1, 0, 1])[:, None]
-    chosen = (within % 2 == 0) & (kind == np.where(flip == whose, step + 1, step))
-    unused = np.zeros((2, columns))
-    table = np.concatenate([chosen, flip[None], (token - lat_rows)[None], unused], axis=0).astype(np.int32)
+    late = [flip for flip in range(4, strips) if flip % 2]
+    early = [0, PAIR] + [flip for flip in range(1, strips) if flip != PAIR and flip not in late]
+    pieces = [[(flip, kind) for flip in early for kind in (0, 1)] + [(0, 2), (PAIR, 2)]]
+    pieces.append([(flip, kind) for flip in late for kind in (0, 1)])
+    whose, step = np.asarray([0, 0, PAIR, PAIR])[:, None], np.asarray([0, 1, 0, 1])[:, None]
+    tables = []
+    for part in pieces:
+        column = np.arange(round_up(set_rows * len(part), LANES))
+        within = column % set_rows
+        filled = column < set_rows * len(part)
+        flip, kind = np.asarray(part)[np.minimum(column // set_rows, len(part) - 1)].T
+        chosen = filled & (within % 2 == 0) & (kind == np.where(flip == whose, step + 1, step))
+        tables.append(np.concatenate([chosen, flip[None], (within // 2 - lat_rows)[None]], axis=0))
+    early_columns = tables[0].shape[1]
+    table = np.concatenate(tables, axis=1).astype(np.int32)
+    columns = table.shape[1]
 
     bf16 = functools.partial(jax.ShapeDtypeStruct, dtype=jnp.bfloat16)
     f32 = functools.partial(jax.ShapeDtypeStruct, dtype=jnp.float32)
     local_rows = query_rows + set_rows
-    own, other, local, pair, mask = pl.pallas_call(
+    own, sent, other, local, pair, mask = pl.pallas_call(
         functools.partial(pack_kernel, text_rows),
         out_shape=(
+            bf16((block_rows, half)),
             bf16((block_rows, half)),
             bf16((block_rows, half)),
             bf16((local_rows, half)),
@@ -185,7 +225,7 @@
             jax.ShapeDtypeStruct((5, columns), jnp.int32),
         ),
         in_specs=[hbm] * 4,
-        out_specs=(vmem,) * 5,
+        out_specs=(vmem,) * 6,
         scratch_shapes=[
             pltpu.VMEM(table.shape, jnp.int32),
             pltpu.VMEM((strip_rows, 2, width), jnp.bfloat16),
@@ -199,27 +239,34 @@
     def to(rows, flip):
         return lax.ppermute(rows, "patch", [(i, i ^ flip) for i in range(strips)])
 
-    held = {0: own}
+    held = {}
+    pair_rows = None
     bit = strips // 2
-    pair_rows = None
-    while bit > 1:
-        arrived = {bit: to(own, bit), bit + 1: to(other, bit + 1)}
-        if pair_rows is None:
-            pair_rows = to(pair, 1)
-        for flip, rows in held.items():
-            if flip > 1:
-                arrived[flip + bit] = to(rows, bit)
-        held.update(arrived)
+    while bit:
+        if bit != PAIR:
+            arrived = {bit ^ PAIR: to(other, bit ^ PAIR), bit: to(sent, bit)}
+            if pair_rows is None:
+                pair_rows = to(pair, PAIR)
+            for flip, rows in held.items():
+                arrived[flip ^ bit] = to(rows, bit)
+            held.update(arrived)
         bit //= 2
 
+    *first, late_bias = pl.pallas_call(
+        functools.partial(early_attention_kernel, (query_rows, early_columns)),
+        out_shape=(f32((2 * query_rows, half)),) * 3 + (f32((4, columns - early_columns)),),
+        in_specs=[smem] + [vmem] * (2 + len(early)),
+        out_specs=(vmem,) * 4,
+        compiler_params=params,
+    )(text_len, mask, own, local, pair_rows, *[held[flip] for flip in early[2:]])
     mine, back = pl.pallas_call(
-        functools.partial(attention_kernel, (set_rows, query_rows)),
+        functools.partial(late_attention_kernel, query_rows),
         out_shape=(bf16((query_rows, half)),) * 2,
-        in_specs=[smem] + [vmem] * (4 + len(flips)),
+        in_specs=[vmem] * (6 + len(late)),
         out_specs=(vmem, vmem),
         compiler_params=params,
-    )(text_len, mask, own, local, pair_rows, *[held[flip] for flip in flips])
-    returned = to(back, 1)
+    )(late_bias, local, pair_rows, *first, *[held[flip] for flip in late])
+    returned = to(back, PAIR)
 
     model = out_weight.shape[1]
     total, gates, far_weight = pl.pallas_call(

time: 23.6 us -> 23 us (0.975)
  waiting for transfers between devices: 4.76 us -> 2.91 us
  starting transfers between devices: 12.4 us -> 13.1 us
  Pallas kernels: 4.93 us -> 5.43 us
    ppermute x8, waiting for transfers between devices: 3.54 us -> 1.7 us  [to(): return lax.ppermute(rows, 'patch', [(i, i ^ flip) for i in range(strips)])]
    ppermute x8, starting transfers between devices: 12.3 us -> 13.1 us  [to(): return lax.ppermute(rows, 'patch', [(i, i ^ flip) for i in range(strips)])]
    pallas_call x1 -> x2, Pallas kernels: 0.82 us -> 1.32 us  [the longest x1 0.71 us: per_device(): pl.pallas_call(functools.partial(early_attention_kernel, (query_rows, ear...]
  transfers between devices with their start and end apart: 9 -> 9, of which waited for: 6 -> 5; matrix products, arithmetic and copies ran while one was open for 0% -> 0% of each run, Pallas kernels for 11% -> 14%
where the time goes in v4:
time: 23 us; the launch traced here: 22.9 us
  starting transfers between devices  13.1 us (57%)
  Pallas kernels  5.43 us (24%)
  waiting for transfers between devices  2.91 us (13%)
  between operations  0.72 us (3%)
  other arithmetic  0.63 us (3%)
    ppermute x8, starting transfers between devices, to(): return lax.ppermute(rows, 'patch', [(i, i ^ flip) for i in range(strips)])  13.1 us
    pallas_call x1, Pallas kernels, per_device(): pl.pallas_call(first_half_kernel, out_shape=(f32((lat_rows, model)), f32(...  2.56 us
    ppermute x8, waiting for transfers between devices, to(): return lax.ppermute(rows, 'patch', [(i, i ^ flip) for i in range(strips)])  1.7 us
    ppermute x1, waiting for transfers between devices, per_device(): received = lax.ppermute(send, 'head', [(0, 1), (1, 0)])  1.22 us
    pallas_call x1, Pallas kernels, per_device(): pl.pallas_call(functools.partial(pack_kernel, text_rows), out_shape=(bf16...  1.03 us
    pallas_call x1, Pallas kernels, per_device(): pl.pallas_call(functools.partial(early_attention_kernel, (query_rows, ear...  0.71 us
    convert_element_type x1, other arithmetic, per_device(): return (keep + received.astype(jnp.float32)).astype(jnp.bfloat16)  0.63 us
    pallas_call x1, Pallas kernels, per_device(): pl.pallas_call(functools.partial(late_attention_kernel, query_rows), out_...  0.61 us
  transfers between devices with their start and end apart: 9, of which 5 were waited for; matrix products, arithmetic and copies ran while one was open for 0% of the time, Pallas kernels for 14%

profile of v4, /device:TPU:0, one launch (start us, length us, event | category | flops | bytes accessed | tf_op | source)
XLA Modules:
  0.0 22.9 jit_solution(17599763249170320284)
XLA Ops:
  0.0 1.0 %shard_map.91 = (bf16[80,384]{1,0:T(8,128)(2,1)S(1)}, bf16[80,384]{1,0:T(8,128)(2,1)S(1)}, bf16[80,384]{1,0:T(8,128)(2,1)S(1)}, bf16[72,384]{1,0:T(8,128)(2,1)S(...) custom-call(s32[6,896]{1,0:T(8,128)} %constant.2.clone.table_hbm, bf16[20,2,768]{2,1,0:T(2,128)(2,1)} %bitcast.3, ...), custom_call_target="tpu_custom_call" | custom-call | tf_op jit(solution)/shard_map/pallas_call | solution.py:217
  1.0 4.1 %collective-permute-start.3 = (bf16[80,384]{1,0:T(8,128)(2,1)S(1)}, bf16[80,384]{1,0:T(8,128)(2,1)S(1)}, u32[]{:S(2)}, u32[]{:S(2)}) collective-permute-start(bf16[80,384]{1,0:T(8,128)(2,1)S(1)} %get-tuple-element.26), channel_id=1, source_target_pairs={{0,8},{2,10},{4,12},{6,14},{8,0},{10,2},{12,4},{14,6},{1,9},{3,11}... | collective-permute-start | bytes 184328 | tf_op jit(solution)/shard_map/ppermute | solution.py:240
  5.1 1.3 %collective-permute-start.4 = (bf16[80,384]{1,0:T(8,128)(2,1)S(1)}, bf16[80,384]{1,0:T(8,128)(2,1)S(1)}, u32[]{:S(2)}, u32[]{:S(2)}) collective-permute-start(bf16[80,384]{1,0:T(8,128)(2,1)S(1)} %get-tuple-element.27), channel_id=1, source_target_pairs={{0,12},{2,14},{4,8},{6,10},{8,4},{10,6},{12,0},{14,2},{1,13},{3,15... | collective-permute-start | bytes 184328 | tf_op jit(solution)/shard_map/ppermute | solution.py:240
  6.5 0.2 %collective-permute-start = (bf16[152,384]{1,0:T(8,128)(2,1)S(1)}, bf16[152,384]{1,0:T(8,128)(2,1)S(1)}, u32[]{:S(2)}, u32[]{:S(2)}) collective-permute-start(bf16[152,384]{1,0:T(8,128)(2,1)S(1)} %get-tuple-element.25), channel_id=1, source_target_pairs={{0,4},{2,6},{4,0},{6,2},{8,12},{10,14},{12,8},{14,10},{1,5},{3,7},... | collective-permute-start | bytes 350216 | tf_op jit(solution)/shard_map/ppermute | solution.py:240
  6.7 1.5 %collective-permute-start.1 = (bf16[80,384]{1,0:T(8,128)(2,1)S(1)}, bf16[80,384]{1,0:T(8,128)(2,1)S(1)}, u32[]{:S(2)}, u32[]{:S(2)}) collective-permute-start(bf16[80,384]{1,0:T(8,128)(2,1)S(1)} %get-tuple-element.26), channel_id=1, source_target_pairs={{0,2},{2,0},{4,6},{6,4},{8,10},{10,8},{12,14},{14,12},{1,3},{3,1},... | collective-permute-start | bytes 184328 | tf_op jit(solution)/shard_map/ppermute | solution.py:240
  8.2 1.8 %collective-permute-start.2 = (bf16[80,384]{1,0:T(8,128)(2,1)S(1)}, bf16[80,384]{1,0:T(8,128)(2,1)S(1)}, u32[]{:S(2)}, u32[]{:S(2)}) collective-permute-start(bf16[80,384]{1,0:T(8,128)(2,1)S(1)} %get-tuple-element.27), channel_id=1, source_target_pairs={{0,6},{2,4},{4,2},{6,0},{8,14},{10,12},{12,10},{14,8},{1,7},{3,5},... | collective-permute-start | bytes 184328 | tf_op jit(solution)/shard_map/ppermute | solution.py:240
  10.0 0.0 collective-permute-done.3.refs_2_
  10.0 1.5 %collective-permute-start.5 = (bf16[80,384]{1,0:T(8,128)(2,1)S(1)}, bf16[80,384]{1,0:T(8,128)(2,1)S(1)}, u32[]{:S(2)}, u32[]{:S(2)}) collective-permute-start(bf16[80,384]{1,0:T(8,128)(2,1)S(1)} %collective-permute-done.3.refs_2_), channel_id=1, source_target_pairs={{0,2},{2,0},{4,6},{6,4},{8,10},{10,8},{12,14},{14,12},{1,3},{3,1},... | collective-permute-start | bytes 184328 | tf_op jit(solution)/shard_map/ppermute | solution.py:240
  11.5 0.2 collective-permute-done.4.refs_3_
  11.7 1.5 %collective-permute-start.6 = (bf16[80,384]{1,0:T(8,128)(2,1)S(1)}, bf16[80,384]{1,0:T(8,128)(2,1)S(1)}, u32[]{:S(2)}, u32[]{:S(2)}) collective-permute-start(bf16[80,384]{1,0:T(8,128)(2,1)S(1)} %collective-permute-done.4.refs_3_), channel_id=1, source_target_pairs={{0,2},{2,0},{4,6},{6,4},{8,10},{10,8},{12,14},{14,12},{1,3},{3,1},... | collective-permute-start | bytes 184328 | tf_op jit(solution)/shard_map/ppermute | solution.py:240
  13.8 0.0 collective-permute-done.1.refs_0_
  13.8 0.9 %collective-permute-done.2.refs_1_ = bf16[80,384]{1,0:T(8,128)(2,1)S(1)} collective-permute-done((bf16[80,384]{1,0:T(8,128)(2,1)S(1)}, bf16[80,384]{1,0:T(8,128)(2,1)S(1)}, u32[]{:S(2)}, u32[]{:S(2)}) %collective-permute-start.2) | collective-permute-done | bytes 61472 | tf_op jit(solution)/shard_map/ppermute | solution.py:240
  14.7 0.0 collective-permute-done.pair_ref
  14.7 0.7 %shard_map.92 = (f32[64,384]{1,0:T(8,128)S(1)}, f32[64,384]{1,0:T(8,128)S(1)}, f32[64,384]{1,0:T(8,128)S(1)}, f32[4,256]{1,0:T(4,128)S(1)}) custom-call(s32[1]{0:T(128)S(6)} %copy.10.text_ref, s32[5,896]{1,0:T(8,128)S(1)} %get-tuple-element.22.mask_ref, bf16[80,384]{1,0:T(8,128)(2,1)S(1)} %get-tuple-element.23.own_ref, ...), custom_call_target="tpu_custom_call" | custom-call | tf_op jit(solution)/shard_map/pallas_call | solution.py:255
  15.4 0.0 collective-permute-done.5.refs_0_
  15.5 0.4 %collective-permute-done.6.refs_1_ = bf16[80,384]{1,0:T(8,128)(2,1)S(1)} collective-permute-done((bf16[80,384]{1,0:T(8,128)(2,1)S(1)}, bf16[80,384]{1,0:T(8,128)(2,1)S(1)}, u32[]{:S(2)}, u32[]{:S(2)}) %collective-permute-start.6) | collective-permute-done | bytes 61472 | tf_op jit(solution)/shard_map/ppermute | solution.py:240
  15.9 0.6 %shard_map.93 = (bf16[32,384]{1,0:T(8,128)(2,1)S(1)}, bf16[32,384]{1,0:T(8,128)(2,1)S(1)}) custom-call(f32[4,256]{1,0:T(4,128)S(1)} %get-tuple-element.28.bias_ref, bf16[72,384]{1,0:T(8,128)(2,1)S(1)} %get-tuple-element.24.local_ref, bf16[152,384]{1,0:T(8,128)(2,1)S(1)} %collective-permute-done.pair_ref, f32[64,384]{1,0:T(8,128)S(1)} %get-tuple-element.29.mixed_ref, ...), custom_call_target="tpu_custom_call" | custom-call | tf_op jit(solution)/shard_map/pallas_call | solution.py:262
  16.5 1.2 %collective-permute-start.7 = (bf16[32,384]{1,0:T(8,128)(2,1)S(1)}, bf16[32,384]{1,0:T(8,128)(2,1)S(1)}, u32[]{:S(2)}, u32[]{:S(2)}) collective-permute-start(bf16[32,384]{1,0:T(8,128)(2,1)S(1)} %get-tuple-element.32), channel_id=1, source_target_pairs={{0,4},{2,6},{4,0},{6,2},{8,12},{10,14},{12,8},{14,10},{1,5},{3,7},... | collective-permute-start | bytes 73736 | tf_op jit(solution)/shard_map/ppermute | solution.py:240
  17.6 2.6 %shard_map.94 = (f32[16,3072]{1,0:T(8,128)S(1)}, f32[2,3072]{1,0:T(2,128)S(1)}, bf16[384,3072]{1,0:T(8,128)(2,1)S(1)}) custom-call(bf16[32,384]{1,0:T(8,128)(2,1)S(1)} %get-tuple-element.33.attended_ref, s32[2]{0:T(128)} %plan_hbm.1, bf16[28,3072]{1,0:T(8,128)(2,1)} %table_hbm.2, bf16[16,1536]{1,0:T(8,128)(2,1)} %hidden_hbm.1, bf16[768,3072]{1,0:T(8,128)(2,1)} %weight_hbm.1), custom_call_target="tpu_custom_call" | custom-call | tf_op jit(solution)/shard_map/pallas_call | solution.py:272
  20.2 0.2 collective-permute-done.7.attended_ref
  20.4 0.5 %shard_map.95 = (f32[8,3072]{1,0:T(8,128)S(1)}, bf16[8,3072]{1,0:T(8,128)(2,1)S(1)}) custom-call(bf16[32,384]{1,0:T(8,128)(2,1)S(1)} %collective-permute-done.7.attended_ref, bf16[384,3072]{1,0:T(8,128)(2,1)S(1)} %get-tuple-element.34.weight_ref, f32[2,3072]{1,0:T(2,128)S(1)} %get-tuple-element.35.gates_ref, f32[16,3072]{1,0:T(8,128)S(1)} %get-tuple-element.36.sum_ref), custom_call_target="tpu_custom_call" | custom-call | tf_op jit(solution)/shard_map/pallas_call | solution.py:286
  20.9 0.1 collective-permute-start.8
  21.0 1.2 %collective-permute-done.8 = bf16[8,3072]{1,0:T(8,128)(2,1)S(1)} collective-permute-done((bf16[8,3072]{1,0:T(8,128)(2,1)S(1)}, bf16[8,3072]{1,0:T(8,128)(2,1)S(1)}, u32[]{:S(2)}, u32[]{:S(2)}) %collective-permute-start.8) | collective-permute-done | bytes 49184 | tf_op jit(solution)/shard_map/ppermute | solution.py:294
  22.2 0.6 %add_convert_fusion = bf16[8,3072]{1,0:T(8,128)(2,1)} fusion(f32[8,3072]{1,0:T(8,128)S(1)} %get-tuple-element.37, bf16[8,3072]{1,0:T(8,128)(2,1)S(1)} %collective-permute-done.8), kind=kLoop, calls=%fused_computation | loop fusion | flops 73728 | bytes 196608 | tf_op jit(solution)/shard_map/convert_element_type | solution.py:295
Async XLA Ops:
  1.0 8.9 %collective-permute-start.3 = (bf16[80,384]{1,0:T(8,128)(2,1)S(1)}, bf16[80,384]{1,0:T(8,128)(2,1)S(1)}, u32[]{:S(2)}, u32[]{:S(2)}) collective-permute-start(bf16[80,384]{1,0:T(8,128)(2,1)S(1)} %get-tuple-element.26), channel_id=1, source_target_pairs={{0,8},{2,10},{4,12},{6,14},{8,0},{10,2},{12,4},{14,6},{1,9},{3,11}... | collective-permute-start | bytes 184328 | tf_op jit(solution)/shard_map/ppermute | solution.py:240
  5.1 6.5 %collective-permute-start.4 = (bf16[80,384]{1,0:T(8,128)(2,1)S(1)}, bf16[80,384]{1,0:T(8,128)(2,1)S(1)}, u32[]{:S(2)}, u32[]{:S(2)}) collective-permute-start(bf16[80,384]{1,0:T(8,128)(2,1)S(1)} %get-tuple-element.27), channel_id=1, source_target_pairs={{0,12},{2,14},{4,8},{6,10},{8,4},{10,6},{12,0},{14,2},{1,13},{3,15... | collective-permute-start | bytes 184328 | tf_op jit(solution)/shard_map/ppermute | solution.py:240
  6.5 8.2 %collective-permute-start = (bf16[152,384]{1,0:T(8,128)(2,1)S(1)}, bf16[152,384]{1,0:T(8,128)(2,1)S(1)}, u32[]{:S(2)}, u32[]{:S(2)}) collective-permute-start(bf16[152,384]{1,0:T(8,128)(2,1)S(1)} %get-tuple-element.25), channel_id=1, source_target_pairs={{0,4},{2,6},{4,0},{6,2},{8,12},{10,14},{12,8},{14,10},{1,5},{3,7},... | collective-permute-start | bytes 350216 | tf_op jit(solution)/shard_map/ppermute | solution.py:240
  6.7 7.1 %collective-permute-start.1 = (bf16[80,384]{1,0:T(8,128)(2,1)S(1)}, bf16[80,384]{1,0:T(8,128)(2,1)S(1)}, u32[]{:S(2)}, u32[]{:S(2)}) collective-permute-start(bf16[80,384]{1,0:T(8,128)(2,1)S(1)} %get-tuple-element.26), channel_id=1, source_target_pairs={{0,2},{2,0},{4,6},{6,4},{8,10},{10,8},{12,14},{14,12},{1,3},{3,1},... | collective-permute-start | bytes 184328 | tf_op jit(solution)/shard_map/ppermute | solution.py:240
  8.2 6.5 %collective-permute-start.2 = (bf16[80,384]{1,0:T(8,128)(2,1)S(1)}, bf16[80,384]{1,0:T(8,128)(2,1)S(1)}, u32[]{:S(2)}, u32[]{:S(2)}) collective-permute-start(bf16[80,384]{1,0:T(8,128)(2,1)S(1)} %get-tuple-element.27), channel_id=1, source_target_pairs={{0,6},{2,4},{4,2},{6,0},{8,14},{10,12},{12,10},{14,8},{1,7},{3,5},... | collective-permute-start | bytes 184328 | tf_op jit(solution)/shard_map/ppermute | solution.py:240
  10.0 5.5 %collective-permute-start.5 = (bf16[80,384]{1,0:T(8,128)(2,1)S(1)}, bf16[80,384]{1,0:T(8,128)(2,1)S(1)}, u32[]{:S(2)}, u32[]{:S(2)}) collective-permute-start(bf16[80,384]{1,0:T(8,128)(2,1)S(1)} %collective-permute-done.3.refs_2_), channel_id=1, source_target_pairs={{0,2},{2,0},{4,6},{6,4},{8,10},{10,8},{12,14},{14,12},{1,3},{3,1},... | collective-permute-start | bytes 184328 | tf_op jit(solution)/shard_map/ppermute | solution.py:240
  11.7 4.2 %collective-permute-start.6 = (bf16[80,384]{1,0:T(8,128)(2,1)S(1)}, bf16[80,384]{1,0:T(8,128)(2,1)S(1)}, u32[]{:S(2)}, u32[]{:S(2)}) collective-permute-start(bf16[80,384]{1,0:T(8,128)(2,1)S(1)} %collective-permute-done.4.refs_3_), channel_id=1, source_target_pairs={{0,2},{2,0},{4,6},{6,4},{8,10},{10,8},{12,14},{14,12},{1,3},{3,1},... | collective-permute-start | bytes 184328 | tf_op jit(solution)/shard_map/ppermute | solution.py:240
  16.5 3.9 %collective-permute-start.7 = (bf16[32,384]{1,0:T(8,128)(2,1)S(1)}, bf16[32,384]{1,0:T(8,128)(2,1)S(1)}, u32[]{:S(2)}, u32[]{:S(2)}) collective-permute-start(bf16[32,384]{1,0:T(8,128)(2,1)S(1)} %get-tuple-element.32), channel_id=1, source_target_pairs={{0,4},{2,6},{4,0},{6,2},{8,12},{10,14},{12,8},{14,10},{1,5},{3,7},... | collective-permute-start | bytes 73736 | tf_op jit(solution)/shard_map/ppermute | solution.py:240
  20.9 1.3 %collective-permute-start.8 = (bf16[8,3072]{1,0:T(8,128)(2,1)S(1)}, bf16[8,3072]{1,0:T(8,128)(2,1)S(1)}, u32[]{:S(2)}, u32[]{:S(2)}) collective-permute-start(bf16[8,3072]{1,0:T(8,128)(2,1)S(1)} %get-tuple-element.38), channel_id=1, source_target_pairs={{0,1},{1,0},{2,3},{3,2},{4,5},{5,4},{6,7},{7,6},{8,9},{9,8},{10,11... | collective-permute-start | bytes 147464 | tf_op jit(solution)/shard_map/ppermute | solution.py:294

commit v5 on v0

v5 whole, which is shorter than its diff:
```python
import functools

import jax
import jax.numpy as jnp
import numpy as np
from jax import lax
from jax.experimental import pallas as pl
from jax.experimental.pallas import tpu as pltpu
from jax.sharding import PartitionSpec as P

HDIM = 128
LANES = 128
MASKED = -1e30
VMEM_LIMIT = 24 * 1024 * 1024
TERMS, TERM_LANES = 3, 32
CHUNKS = 6


def round_up(value, step):
    return (value + step - 1) // step * step


def pack_kernel(text_rows, table_hbm, stale_hbm, step_hbm, query_hbm, block_ref, local_ref, query_ref, mask_ref,
                table_ref, stale, step, query, sems):
    copies = [
        pltpu.make_async_copy(stale_hbm, stale, sems.at[0]),
        pltpu.make_async_copy(step_hbm, step, sems.at[1]),
        pltpu.make_async_copy(query_hbm, query, sems.at[2]),
        pltpu.make_async_copy(table_hbm, table_ref, sems.at[3]),
    ]
    for copy in copies:
        copy.start()
    for copy in copies:
        copy.wait()
    strip = lax.axis_index("patch")
    classes = mask_ref.shape[0] - 1
    early = table_ref[classes + 1 : classes + 2, :]
    mask_ref[:classes, :] = table_ref[:classes, :]
    mask_ref[classes:, :] = jnp.where(early < 0, -1, (strip ^ table_ref[classes : classes + 1, :]) * text_rows + early)
    width = block_ref.shape[1]
    block_ref[...] = jnp.concatenate([stale[...].reshape(-1, width), step[0].reshape(-1, width)], axis=0)
    query_ref[...] = query[...].reshape(-1, width)
    local_ref[...] = jnp.concatenate([query[...].reshape(-1, width), step[1].reshape(-1, width)], axis=0)


def blocks_of(ref):
    return [slice(i, i + HDIM) for i in range(0, ref.shape[-1], HDIM)]


def attention(query_rows, bias_ref, own_ref, local_ref, query_ref, others, first_class):
    columns = bias_ref.shape[1]
    bias = jnp.concatenate(
        [jnp.broadcast_to(bias_ref[first_class + c : first_class + c + 1, :], (query_rows // 2, columns)) for c in range(2)],
        axis=0,
    )
    lane_blocks = blocks_of(own_ref)
    rows, scores = [], []
    for lanes in lane_blocks:
        parts = [own_ref[:, lanes]] + [ref[:, lanes] for ref in others] + [local_ref[query_rows:, lanes]]
        filled = sum(part.shape[0] for part in parts)
        if filled < columns:
            parts.append(jnp.zeros((columns - filled, HDIM), jnp.bfloat16))
        rows.append(jnp.concatenate(parts, axis=0))
        scores.append(
            lax.dot_general(
                query_ref[:query_rows, lanes], rows[-1], (((1,), (1,)), ((), ())), preferred_element_type=jnp.float32
            )
            * (1.0 / HDIM**0.5)
            + bias
        )
    tops = [jnp.max(score, axis=1, keepdims=True) for score in scores]
    expos = [jnp.exp(score - top) for score, top in zip(scores, tops)]
    norms = [jnp.sum(expo, axis=1, keepdims=True) for expo in expos]
    lane = lax.broadcasted_iota(jnp.int32, (query_rows, LANES), 1)
    logs = jnp.zeros((query_rows, LANES), jnp.float32)
    mixed = []
    for head, (expo, norm, top, row) in enumerate(zip(expos, norms, tops, rows)):
        weights = pltpu.roll(expo / norm, 1, 1).astype(jnp.bfloat16)
        mixed.append(jnp.dot(weights, row, preferred_element_type=jnp.float32))
        logs = jnp.where(lane == head, top + jnp.log(norm), logs)
    return mixed, logs


def own_kernel(query_rows, bias_ref, own_ref, local_ref, *refs):
    others, (mixed_ref, log_ref) = refs[:-2], refs[-2:]
    mixed, logs = attention(query_rows, bias_ref, own_ref, local_ref, local_ref, others, 0)
    for lanes, rows in zip(blocks_of(own_ref), mixed):
        mixed_ref[:, lanes] = rows
    log_ref[...] = logs


def partner_kernel(query_rows, bias_ref, own_ref, local_ref, query_ref, *refs):
    others, partner_ref = refs[:-1], refs[-1]
    mixed, rest = attention(query_rows, bias_ref, own_ref, local_ref, query_ref, others, 2)
    for lanes, rows in zip(blocks_of(own_ref), mixed):
        partner_ref[:, lanes] = rows.astype(jnp.bfloat16)
    coded = jnp.zeros_like(rest)
    for term in range(TERMS):
        part = rest.astype(jnp.bfloat16).astype(jnp.float32)
        coded = coded + (pltpu.roll(part, term * TERM_LANES, 1) if term else part)
        rest = rest - part
    partner_ref[:, own_ref.shape[1] :] = coded.astype(jnp.bfloat16)


def decoded(packed_ref, width):
    coded = packed_ref[:, width:].astype(jnp.float32)
    logs = pltpu.roll(coded, LANES - 2 * TERM_LANES, 1) + pltpu.roll(coded, LANES - TERM_LANES, 1) + coded
    return packed_ref[:, :width].astype(jnp.float32), logs


def joined(one, two, lane_blocks):
    (mixed, logs), (other_mixed, other_logs) = one, two
    parts = []
    for head, lanes in enumerate(lane_blocks):
        log, other_log = logs[:, head : head + 1], other_logs[:, head : head + 1]
        top = jnp.maximum(log, other_log)
        share, other_share = jnp.exp(log - top), jnp.exp(other_log - top)
        whole = share + other_share
        parts.append(mixed[:, lanes] * (share / whole) + other_mixed[:, lanes] * (other_share / whole))
    return jnp.concatenate(parts, axis=1).astype(jnp.bfloat16)


def fetch_kernel(text_ref, mask_ref, plan_hbm, table_hbm, hidden_hbm, weight_hbm, bias_ref, sum_ref, gates_ref, weight_ref,
                 plan_ref, table_ref, hidden_ref, sems):
    small = [
        pltpu.make_async_copy(plan_hbm, plan_ref, sems.at[0]),
        pltpu.make_async_copy(table_hbm, table_ref, sems.at[1]),
        pltpu.make_async_copy(hidden_hbm, hidden_ref, sems.at[2]),
    ]
    depth = weight_ref.shape[0] // CHUNKS
    large = [
        pltpu.make_async_copy(
            weight_hbm.at[pl.ds(chunk * depth, depth), :], weight_ref.at[pl.ds(chunk * depth, depth), :], sems.at[3 + chunk]
        )
        for chunk in range(CHUNKS)
    ]
    for copy in small + large:
        copy.start()
    classes = bias_ref.shape[0]
    live = mask_ref[classes:, :] < text_ref[0]
    bias_ref[...] = jnp.where((mask_ref[:classes, :] > 0) & live, 0.0, MASKED)
    for copy in small:
        copy.wait()
    table = table_ref[...].astype(jnp.float32)
    entry = lax.broadcasted_iota(jnp.int32, table.shape, 0)
    for step in range(2):
        row = jnp.sum(jnp.where(entry == plan_ref[step], table, 0.0), axis=0, keepdims=True)
        gates_ref[step : step + 1, :] = row
    width = hidden_ref.shape[1]
    lanes = pl.ds(pl.multiple_of(lax.axis_index("head") * width, LANES), width)
    sum_ref[...] = jnp.zeros_like(sum_ref)
    sum_ref[:, lanes] = hidden_ref[...].astype(jnp.float32)
    for copy in large:
        copy.wait()


def project_kernel(mixed_ref, log_ref, partner_ref, weight_ref, gates_ref, sum_ref, keep_ref, send_ref):
    strip = sum_ref.shape[0]
    half = keep_ref.shape[0]
    attended = joined((mixed_ref[...], log_ref[...]), decoded(partner_ref, mixed_ref.shape[1]), blocks_of(mixed_ref))
    projected = jnp.dot(attended, weight_ref[...], preferred_element_type=jnp.float32)
    total = sum_ref[...] + gates_ref[0:1, :] * projected[:strip] + gates_ref[1:2, :] * projected[strip:]
    first = lax.axis_index("head") == 0
    keep_ref[...] = jnp.where(first, total[:half], total[half:])
    send_ref[...] = jnp.where(first, total[half:], total[:half]).astype(jnp.bfloat16)


def per_device(queries, stale_pairs, step_pairs, hidden, out_weight, gate_table, t_index, text_len):
    strips = lax.axis_size("patch")
    strip_rows = stale_pairs.shape[1]
    lat_rows = queries.shape[1]
    text_rows = strip_rows - lat_rows
    width = queries.shape[2]
    model = out_weight.shape[1]
    set_rows = 2 * strip_rows
    query_rows = 2 * lat_rows
    block_rows = 2 * set_rows
    smem = pl.BlockSpec(memory_space=pltpu.SMEM)
    vmem = pl.BlockSpec(memory_space=pltpu.VMEM)
    hbm = pl.BlockSpec(memory_space=pltpu.HBM)
    params = pltpu.CompilerParams(vmem_limit_bytes=VMEM_LIMIT)

    def in_hbm(*arrays):
        return [pltpu.with_memory_space_constraint(array, pltpu.HBM) for array in arrays]

    across = strips // 2
    neighbours = sorted(range(1, across), key=lambda flip: (-bin(flip).count("1"), flip))
    pieces = [(flip, kind) for flip in [0] + neighbours for kind in (0, 1)] + [(0, 2)]
    whose, step = np.asarray([0, 0, across, across])[:, None], np.asarray([0, 1, 0, 1])[:, None]
    columns = round_up(set_rows * len(pieces), LANES)
    column = np.arange(columns)
    within = column % set_rows
    flip, kind = np.asarray(pieces)[np.minimum(column // set_rows, len(pieces) - 1)].T
    is_key = (column < set_rows * len(pieces)) & (within % 2 == 0)
    chosen = is_key & (kind == np.where(flip == whose, step + 1, step))
    table = np.concatenate([chosen, flip[None], (within // 2 - lat_rows)[None]], axis=0).astype(np.int32)

    bf16 = functools.partial(jax.ShapeDtypeStruct, dtype=jnp.bfloat16)
    f32 = functools.partial(jax.ShapeDtypeStruct, dtype=jnp.float32)
    block, local, query, mask = pl.pallas_call(
        functools.partial(pack_kernel, text_rows),
        out_shape=(
            bf16((block_rows, width)),
            bf16((query_rows + set_rows, width)),
            bf16((query_rows, width)),
            jax.ShapeDtypeStruct((len(whose) + 1, columns), jnp.int32),
        ),
        in_specs=[hbm] * 4,
        out_specs=(vmem,) * 4,
        scratch_shapes=[
            pltpu.VMEM(table.shape, jnp.int32),
            pltpu.VMEM((strip_rows, 2, width), jnp.bfloat16),
            pltpu.VMEM((2, strip_rows, 2, width), jnp.bfloat16),
            pltpu.VMEM((2, lat_rows, width), jnp.bfloat16),
            pltpu.SemaphoreType.DMA((4,)),
        ],
        compiler_params=params,
    )(*in_hbm(jnp.asarray(table), stale_pairs.transpose(1, 0, 2), step_pairs.transpose(0, 2, 1, 3), queries))

    def to(rows, flip):
        return lax.ppermute(rows, "patch", [(i, i ^ flip) for i in range(strips)])

    partner_query = to(query, across)
    others = [to(block, flip) for flip in neighbours]
    bias, total, gates, weight = pl.pallas_call(
        fetch_kernel,
        out_shape=(f32((len(whose), columns)), f32((lat_rows, model)), f32((2, model)), bf16(out_weight.shape)),
        in_specs=[smem, vmem] + [hbm] * 4,
        out_specs=(vmem,) * 4,
        scratch_shapes=[
            pltpu.SMEM(t_index.shape, jnp.int32),
            pltpu.VMEM(gate_table.shape, jnp.bfloat16),
            pltpu.VMEM(hidden.shape, jnp.bfloat16),
            pltpu.SemaphoreType.DMA((3 + CHUNKS,)),
        ],
        compiler_params=params,
    )(text_len, mask, *in_hbm(t_index, gate_table, hidden, out_weight))
    partial_rows = pl.pallas_call(
        functools.partial(partner_kernel, query_rows),
        out_shape=bf16((query_rows, width + LANES)),
        in_specs=[vmem] * (4 + len(others)),
        out_specs=vmem,
        compiler_params=params,
    )(bias, block, local, partner_query, *others)
    mixed, logs = pl.pallas_call(
        functools.partial(own_kernel, query_rows),
        out_shape=(f32((query_rows, width)), f32((query_rows, LANES))),
        in_specs=[vmem] * (3 + len(others)),
        out_specs=(vmem,) * 2,
        compiler_params=params,
    )(bias, block, local, *others)
    partner_rows = to(partial_rows, across)

    keep, send = pl.pallas_call(
        project_kernel,
        out_shape=(f32((lat_rows // 2, model)), bf16((lat_rows // 2, model))),
        in_specs=[vmem] * 6,
        out_specs=(vmem, vmem),
        compiler_params=params,
    )(mixed, logs, partner_rows, weight, gates, total)
    received = lax.ppermute(send, "head", [(0, 1), (1, 0)])
    return (keep + received.astype(jnp.float32)).astype(jnp.bfloat16)


def solution(mesh):
    return jax.shard_map(
        per_device,
        mesh=mesh,
        in_specs=(
            P(None, ("groups", "patch"), "head"),
            P(None, ("groups", "patch"), "head"),
            P(None, None, ("groups", "patch"), "head"),
            P(("groups", "patch"), "head"),
            P("head", None),
            P(),
            P("groups"),
            P("groups"),
        ),
        out_specs=P(("groups", "patch", "head"), None),
        check_vma=False,
    )
```

time: 113 us -> 21.2 us (0.19)
  blocking collectives: 68.2 us -> 0 us
  between operations: 17.8 us -> 0.72 us
  starting transfers between devices: 0.04 us -> 9.84 us
  matrix products: 8.77 us -> 0 us
  local copies, waits for them, and re-layouts: 8.44 us -> 0 us
  Pallas kernels: 0 us -> 5.98 us
  other arithmetic: 4.01 us -> 0.63 us
    all_gather x2 -> x0, blocking collectives: 64.4 us -> none  [the longest x1 32.9 us: per_device(): first_sets = lax.all_gather(step_pairs[0], 'patch', axis=1, tiled=True)]
    ppermute x0 -> x6, starting transfers between devices: none -> 9.84 us  [the longest x5 9.77 us: to(): return lax.ppermute(rows, 'patch', [(i, i ^ flip) for i in range(strips)])]
    dot_general x4 -> x0, matrix products: 7.96 us -> none  [the longest x2 7.5 us: project(): return jnp.dot(attended, out_weight, preferred_element_type=jnp.float32)]
    slice x4 -> x0, local copies, waits for them, and re-layouts: 7.37 us -> none  [the longest x2 5.91 us: project(): attended = attend(queries[section], pairs[0], pairs[1], usable)]
    pallas_call x0 -> x5, Pallas kernels: none -> 5.98 us  [the longest x1 2.54 us: per_device(): pl.pallas_call(fetch_kernel, out_shape=(f32((len(whose), columns)), f32((...]
    reduce_scatter x2 -> x0, waiting for transfers between devices: 4.8 us -> none  [the longest x1 4.78 us: per_device(): lax.psum_scatter(project(1), 'head', scatter_dimension=0, tiled=True)]
    ppermute x0 -> x6, waiting for transfers between devices: none -> 3.87 us  [the longest x5 2.65 us: to(): return lax.ppermute(rows, 'patch', [(i, i ^ flip) for i in range(strips)])]
    all_to_all x1 -> x0, blocking collectives: 3.79 us -> none  [per_device(): lax.all_to_all(state, 'head', split_axis=0, concat_axis=1, tiled=True)]
  transfers between devices with their start and end apart: 2 -> 6, of which waited for: 1 -> 3; matrix products, arithmetic and copies ran while one was open for 7% -> 0% of each run, Pallas kernels for 0% -> 15%
where the time goes in v5:
time: 21.2 us; the launch traced here: 21.1 us
  starting transfers between devices  9.84 us (46%)
  Pallas kernels  5.98 us (28%)
  waiting for transfers between devices  3.87 us (18%)
  between operations  0.72 us (3%)
  other arithmetic  0.63 us (3%)
    ppermute x5, starting transfers between devices, to(): return lax.ppermute(rows, 'patch', [(i, i ^ flip) for i in range(strips)])  9.77 us
    ppermute x5, waiting for transfers between devices, to(): return lax.ppermute(rows, 'patch', [(i, i ^ flip) for i in range(strips)])  2.65 us
    pallas_call x1, Pallas kernels, per_device(): pl.pallas_call(fetch_kernel, out_shape=(f32((len(whose), columns)), f32((...  2.54 us
    ppermute x1, waiting for transfers between devices, per_device(): received = lax.ppermute(send, 'head', [(0, 1), (1, 0)])  1.22 us
    pallas_call x1, Pallas kernels, per_device(): pl.pallas_call(project_kernel, out_shape=(f32((lat_rows // 2, model)), bf...  1.06 us
    pallas_call x1, Pallas kernels, per_device(): pl.pallas_call(functools.partial(pack_kernel, text_rows), out_shape=(bf16...  1.01 us
    pallas_call x1, Pallas kernels, per_device(): pl.pallas_call(functools.partial(partner_kernel, query_rows), out_shape=b...  0.68 us
    pallas_call x1, Pallas kernels, per_device(): pl.pallas_call(functools.partial(own_kernel, query_rows), out_shape=(f32(...  0.68 us
  transfers between devices with their start and end apart: 6, of which 3 were waited for; matrix products, arithmetic and copies ran while one was open for 0% of the time, Pallas kernels for 15%

profile of v5, /device:TPU:0, one launch (start us, length us, event | category | flops | bytes accessed | tf_op | source)
XLA Modules:
  0.0 21.1 jit_solution(15944726538177260088)
XLA Ops:
  0.0 1.0 %shard_map.91 = (bf16[80,768]{1,0:T(8,128)(2,1)S(1)}, bf16[72,768]{1,0:T(8,128)(2,1)S(1)}, bf16[32,768]{1,0:T(8,128)(2,1)S(1)}, s32[5,384]{1,0:T(8,128)S(1)}) custom-call(s32[6,384]{1,0:T(8,128)} %constant.2.clone.table_hbm, bf16[20,2,768]{2,1,0:T(2,128)(2,1)} %bitcast.3, bf16[2,20,2,768]{3,2,1,0:T(2,128)(2,1)} %bitcast.2, bf16[2,16,768]{2,1,0:T(8,128)(2,1)} %query_hbm.1), custom_call_target="tpu_custom_call" | custom-call | tf_op jit(solution)/shard_map/pallas_call | solution.py:200
  1.0 3.1 %collective-permute-start.2 = (bf16[80,768]{1,0:T(8,128)(2,1)S(1)}, bf16[80,768]{1,0:T(8,128)(2,1)S(1)}, u32[]{:S(2)}, u32[]{:S(2)}) collective-permute-start(bf16[80,768]{1,0:T(8,128)(2,1)S(1)} %get-tuple-element.19.own_ref), channel_id=1, source_target_pairs={{0,4},{2,6},{4,0},{6,2},{8,12},{10,14},{12,8},{14,10},{1,5},{3,7},... | collective-permute-start | bytes 368648 | tf_op jit(solution)/shard_map/ppermute | solution.py:221
  4.1 1.5 %collective-permute-start.1 = (bf16[80,768]{1,0:T(8,128)(2,1)S(1)}, bf16[80,768]{1,0:T(8,128)(2,1)S(1)}, u32[]{:S(2)}, u32[]{:S(2)}) collective-permute-start(bf16[80,768]{1,0:T(8,128)(2,1)S(1)} %get-tuple-element.19.own_ref), channel_id=1, source_target_pairs={{0,2},{2,0},{4,6},{6,4},{8,10},{10,8},{12,14},{14,12},{1,3},{3,1},... | collective-permute-start | bytes 368648 | tf_op jit(solution)/shard_map/ppermute | solution.py:221
  5.6 0.0 collective-permute-start
  5.7 3.0 %collective-permute-start.3 = (bf16[32,768]{1,0:T(8,128)(2,1)S(1)}, bf16[32,768]{1,0:T(8,128)(2,1)S(1)}, u32[]{:S(2)}, u32[]{:S(2)}) collective-permute-start(bf16[32,768]{1,0:T(8,128)(2,1)S(1)} %get-tuple-element.23), channel_id=1, source_target_pairs={{0,8},{2,10},{4,12},{6,14},{8,0},{10,2},{12,4},{14,6},{1,9},{3,11}... | collective-permute-start | bytes 147464 | tf_op jit(solution)/shard_map/ppermute | solution.py:221
  9.3 2.5 %shard_map.92 = (f32[4,384]{1,0:T(4,128)S(1)}, f32[16,3072]{1,0:T(8,128)S(1)}, f32[2,3072]{1,0:T(2,128)S(1)}, bf16[768,3072]{1,0:T(8,128)(2,1)S(1)}) custom-call(s32[1]{0:T(128)S(6)} %copy.10.text_ref, s32[5,384]{1,0:T(8,128)S(1)} %get-tuple-element.17.mask_ref, s32[2]{0:T(128)} %plan_hbm.1, bf16[28,3072]{1,0:T(8,128)(2,1)} %table_hbm.2, ...), custom_call_target="tpu_custom_call" | custom-call | tf_op jit(solution)/shard_map/pallas_call | solution.py:225
  11.8 0.0 collective-permute-done.3.query_ref
  11.8 0.0 collective-permute-done.2.refs_2_
  11.8 0.0 collective-permute-done.1.refs_1_
  11.8 0.4 %collective-permute-done.refs_0_ = bf16[80,768]{1,0:T(8,128)(2,1)S(1)} collective-permute-done((bf16[80,768]{1,0:T(8,128)(2,1)S(1)}, bf16[80,768]{1,0:T(8,128)(2,1)S(1)}, u32[]{:S(2)}, u32[]{:S(2)}) %collective-permute-start) | collective-permute-done | bytes 122912 | tf_op jit(solution)/shard_map/ppermute | solution.py:221
  12.2 0.7 %shard_map.94 = bf16[32,896]{1,0:T(8,128)(2,1)S(1)} custom-call(f32[4,384]{1,0:T(4,128)S(1)} %get-tuple-element.18.bias_ref, bf16[80,768]{1,0:T(8,128)(2,1)S(1)} %get-tuple-element.19.own_ref, bf16[72,768]{1,0:T(8,128)(2,1)S(1)} %get-tuple-element.20.local_ref, bf16[32,768]{1,0:T(8,128)(2,1)S(1)} %collective-permute-done.3.query_ref, ...), custom_call_target="tpu_custom_call" | custom-call | tf_op jit(solution)/shard_map/pallas_call | solution.py:238
  12.9 2.2 %collective-permute-start.4 = (bf16[32,896]{1,0:T(8,128)(2,1)S(1)}, bf16[32,896]{1,0:T(8,128)(2,1)S(1)}, u32[]{:S(2)}, u32[]{:S(2)}) collective-permute-start(bf16[32,896]{1,0:T(8,128)(2,1)S(1)} %shard_map.94), channel_id=1, source_target_pairs={{0,8},{2,10},{4,12},{6,14},{8,0},{10,2},{12,4},{14,6},{1,9},{3,11}... | collective-permute-start | bytes 172040 | tf_op jit(solution)/shard_map/ppermute | solution.py:221
  15.1 0.7 %shard_map.93 = (f32[32,768]{1,0:T(8,128)S(1)}, f32[32,128]{1,0:T(8,128)S(1)}) custom-call(f32[4,384]{1,0:T(4,128)S(1)} %get-tuple-element.18.bias_ref, bf16[80,768]{1,0:T(8,128)(2,1)S(1)} %get-tuple-element.19.own_ref, bf16[72,768]{1,0:T(8,128)(2,1)S(1)} %get-tuple-element.20.local_ref, bf16[80,768]{1,0:T(8,128)(2,1)S(1)} %collective-permute-done.refs_0_, ...), custom_call_target="tpu_custom_call" | custom-call | tf_op jit(solution)/shard_map/pallas_call | solution.py:245
  15.8 2.3 %collective-permute-done.4.partner_ref = bf16[32,896]{1,0:T(8,128)(2,1)S(1)} collective-permute-done((bf16[32,896]{1,0:T(8,128)(2,1)S(1)}, bf16[32,896]{1,0:T(8,128)(2,1)S(1)}, u32[]{:S(2)}, u32[]{:S(2)}) %collective-permute-start.4) | collective-permute-done | bytes 57376 | tf_op jit(solution)/shard_map/ppermute | solution.py:221
  18.0 1.1 %shard_map.95 = (f32[8,3072]{1,0:T(8,128)S(1)}, bf16[8,3072]{1,0:T(8,128)(2,1)S(1)}) custom-call(f32[32,768]{1,0:T(8,128)S(1)} %get-tuple-element.21.mixed_ref, f32[32,128]{1,0:T(8,128)S(1)} %get-tuple-element.22.log_ref, bf16[32,896]{1,0:T(8,128)(2,1)S(1)} %collective-permute-done.4.partner_ref, bf16[768,3072]{1,0:T(8,128)(2,1)S(1)} %get-tuple-element.24.weight_ref, ...), custom_call_target="tpu_custom_call" | custom-call | tf_op jit(solution)/shard_map/pallas_call | solution.py:254
  19.1 0.1 collective-permute-start.5
  19.2 1.2 %collective-permute-done.5 = bf16[8,3072]{1,0:T(8,128)(2,1)S(1)} collective-permute-done((bf16[8,3072]{1,0:T(8,128)(2,1)S(1)}, bf16[8,3072]{1,0:T(8,128)(2,1)S(1)}, u32[]{:S(2)}, u32[]{:S(2)}) %collective-permute-start.5) | collective-permute-done | bytes 49184 | tf_op jit(solution)/shard_map/ppermute | solution.py:261
  20.4 0.6 %add_convert_fusion = bf16[8,3072]{1,0:T(8,128)(2,1)} fusion(f32[8,3072]{1,0:T(8,128)S(1)} %get-tuple-element.27, bf16[8,3072]{1,0:T(8,128)(2,1)S(1)} %collective-permute-done.5), kind=kLoop, calls=%fused_computation | loop fusion | flops 73728 | bytes 196608 | tf_op jit(solution)/shard_map/convert_element_type | solution.py:262
Async XLA Ops:
  1.0 10.8 %collective-permute-start.2 = (bf16[80,768]{1,0:T(8,128)(2,1)S(1)}, bf16[80,768]{1,0:T(8,128)(2,1)S(1)}, u32[]{:S(2)}, u32[]{:S(2)}) collective-permute-start(bf16[80,768]{1,0:T(8,128)(2,1)S(1)} %get-tuple-element.19.own_ref), channel_id=1, source_target_pairs={{0,4},{2,6},{4,0},{6,2},{8,12},{10,14},{12,8},{14,10},{1,5},{3,7},... | collective-permute-start | bytes 368648 | tf_op jit(solution)/shard_map/ppermute | solution.py:221
  4.1 7.7 %collective-permute-start.1 = (bf16[80,768]{1,0:T(8,128)(2,1)S(1)}, bf16[80,768]{1,0:T(8,128)(2,1)S(1)}, u32[]{:S(2)}, u32[]{:S(2)}) collective-permute-start(bf16[80,768]{1,0:T(8,128)(2,1)S(1)} %get-tuple-element.19.own_ref), channel_id=1, source_target_pairs={{0,2},{2,0},{4,6},{6,4},{8,10},{10,8},{12,14},{14,12},{1,3},{3,1},... | collective-permute-start | bytes 368648 | tf_op jit(solution)/shard_map/ppermute | solution.py:221
  5.6 6.6 %collective-permute-start = (bf16[80,768]{1,0:T(8,128)(2,1)S(1)}, bf16[80,768]{1,0:T(8,128)(2,1)S(1)}, u32[]{:S(2)}, u32[]{:S(2)}) collective-permute-start(bf16[80,768]{1,0:T(8,128)(2,1)S(1)} %get-tuple-element.19.own_ref), channel_id=1, source_target_pairs={{0,6},{2,4},{4,2},{6,0},{8,14},{10,12},{12,10},{14,8},{1,7},{3,5},... | collective-permute-start | bytes 368648 | tf_op jit(solution)/shard_map/ppermute | solution.py:221
  5.7 6.2 %collective-permute-start.3 = (bf16[32,768]{1,0:T(8,128)(2,1)S(1)}, bf16[32,768]{1,0:T(8,128)(2,1)S(1)}, u32[]{:S(2)}, u32[]{:S(2)}) collective-permute-start(bf16[32,768]{1,0:T(8,128)(2,1)S(1)} %get-tuple-element.23), channel_id=1, source_target_pairs={{0,8},{2,10},{4,12},{6,14},{8,0},{10,2},{12,4},{14,6},{1,9},{3,11}... | collective-permute-start | bytes 147464 | tf_op jit(solution)/shard_map/ppermute | solution.py:221
  12.9 5.1 %collective-permute-start.4 = (bf16[32,896]{1,0:T(8,128)(2,1)S(1)}, bf16[32,896]{1,0:T(8,128)(2,1)S(1)}, u32[]{:S(2)}, u32[]{:S(2)}) collective-permute-start(bf16[32,896]{1,0:T(8,128)(2,1)S(1)} %shard_map.94), channel_id=1, source_target_pairs={{0,8},{2,10},{4,12},{6,14},{8,0},{10,2},{12,4},{14,6},{1,9},{3,11}... | collective-permute-start | bytes 172040 | tf_op jit(solution)/shard_map/ppermute | solution.py:221
  19.1 1.3 %collective-permute-start.5 = (bf16[8,3072]{1,0:T(8,128)(2,1)S(1)}, bf16[8,3072]{1,0:T(8,128)(2,1)S(1)}, u32[]{:S(2)}, u32[]{:S(2)}) collective-permute-start(bf16[8,3072]{1,0:T(8,128)(2,1)S(1)} %get-tuple-element.28), channel_id=1, source_target_pairs={{0,1},{1,0},{2,3},{3,2},{4,5},{5,4},{6,7},{7,6},{8,9},{9,8},{10,11... | collective-permute-start | bytes 147464 | tf_op jit(solution)/shard_map/ppermute | solution.py:261

commit v6 on v5

--- a/solution.py
+++ b/solution.py
@@ -71,13 +71,17 @@
     tops = [jnp.max(score, axis=1, keepdims=True) for score in scores]
     expos = [jnp.exp(score - top) for score, top in zip(scores, tops)]
     norms = [jnp.sum(expo, axis=1, keepdims=True) for expo in expos]
+    sums = [
+        jnp.dot(pltpu.roll(expo, 1, 1).astype(jnp.bfloat16), row, preferred_element_type=jnp.float32)
+        for expo, row in zip(expos, rows)
+    ]
+    mixed = [whole * (1.0 / norm) for whole, norm in zip(sums, norms)]
     lane = lax.broadcasted_iota(jnp.int32, (query_rows, LANES), 1)
-    logs = jnp.zeros((query_rows, LANES), jnp.float32)
-    mixed = []
-    for head, (expo, norm, top, row) in enumerate(zip(expos, norms, tops, rows)):
-        weights = pltpu.roll(expo / norm, 1, 1).astype(jnp.bfloat16)
-        mixed.append(jnp.dot(weights, row, preferred_element_type=jnp.float32))
-        logs = jnp.where(lane == head, top + jnp.log(norm), logs)
+    all_norms, all_tops = jnp.ones((query_rows, LANES), jnp.float32), jnp.zeros((query_rows, LANES), jnp.float32)
+    for head, (norm, top) in enumerate(zip(norms, tops)):
+        all_norms = jnp.where(lane == head, norm, all_norms)
+        all_tops = jnp.where(lane == head, top, all_tops)
+    logs = all_tops + jnp.log(all_norms)
     return mixed, logs
 
 
@@ -220,7 +224,14 @@
     def to(rows, flip):
         return lax.ppermute(rows, "patch", [(i, i ^ flip) for i in range(strips)])
 
-    partner_query = to(query, across)
+    cores = lax.axis_size("head")
+    partners = (across, across | across // 2)
+
+    def to_partner(rows):
+        pairs = [(i * cores + c, (i ^ partners[c % 2]) * cores + c) for i in range(strips) for c in range(cores)]
+        return lax.ppermute(rows, ("patch", "head"), pairs)
+
+    partner_query = to_partner(query)
     others = [to(block, flip) for flip in neighbours]
     bias, total, gates, weight = pl.pallas_call(
         fetch_kernel,
@@ -249,7 +260,7 @@
         out_specs=(vmem,) * 2,
         compiler_params=params,
     )(bias, block, local, *others)
-    partner_rows = to(partial_rows, across)
+    partner_rows = to_partner(partial_rows)
 
     keep, send = pl.pallas_call(
         project_kernel,

time: 21.2 us -> 21.1 us (level)
  waiting for transfers between devices: 3.87 us -> 3.51 us
  starting transfers between devices: 9.84 us -> 10.2 us
    ppermute x0 -> x2, starting transfers between devices: none -> 5.48 us  [to_partner(): return lax.ppermute(rows, ('patch', 'head'), pairs)]
    ppermute x5 -> x3, starting transfers between devices: 9.77 us -> 4.63 us  [to(): return lax.ppermute(rows, 'patch', [(i, i ^ flip) for i in range(strips)])]
    ppermute x5 -> x3, waiting for transfers between devices: 2.65 us -> 0.01 us  [to(): return lax.ppermute(rows, 'patch', [(i, i ^ flip) for i in range(strips)])]
    ppermute x0 -> x2, waiting for transfers between devices: none -> 2.28 us  [to_partner(): return lax.ppermute(rows, ('patch', 'head'), pairs)]
  transfers between devices with their start and end apart: 6 -> 6, of which waited for: 3 -> 2; matrix products, arithmetic and copies ran while one was open for 0% -> 0% of each run, Pallas kernels for 15% -> 15%
where the time goes in v6:
time: 21.1 us; the launch traced here: 20.9 us
  starting transfers between devices  10.2 us (48%)
  Pallas kernels  5.85 us (28%)
  waiting for transfers between devices  3.51 us (17%)
  between operations  0.73 us (3%)
  other arithmetic  0.63 us (3%)
    ppermute x2, starting transfers between devices, to_partner(): return lax.ppermute(rows, ('patch', 'head'), pairs)  5.48 us
    ppermute x3, starting transfers between devices, to(): return lax.ppermute(rows, 'patch', [(i, i ^ flip) for i in range(strips)])  4.63 us
    pallas_call x1, Pallas kernels, per_device(): pl.pallas_call(fetch_kernel, out_shape=(f32((len(whose), columns)), f32((...  2.54 us
    ppermute x2, waiting for transfers between devices, to_partner(): return lax.ppermute(rows, ('patch', 'head'), pairs)  2.28 us
    ppermute x1, waiting for transfers between devices, per_device(): received = lax.ppermute(send, 'head', [(0, 1), (1, 0)])  1.22 us
    pallas_call x1, Pallas kernels, per_device(): pl.pallas_call(project_kernel, out_shape=(f32((lat_rows // 2, model)), bf...  1.07 us
    pallas_call x1, Pallas kernels, per_device(): pl.pallas_call(functools.partial(pack_kernel, text_rows), out_shape=(bf16...  1.01 us
    convert_element_type x1, other arithmetic, per_device(): return (keep + received.astype(jnp.float32)).astype(jnp.bfloat16)  0.63 us
  transfers between devices with their start and end apart: 6, of which 2 were waited for; matrix products, arithmetic and copies ran while one was open for 0% of the time, Pallas kernels for 15%

profile of v6, /device:TPU:0, one launch (start us, length us, event | category | flops | bytes accessed | tf_op | source)
XLA Modules:
  0.0 20.9 jit_solution(14231045897056708291)
XLA Ops:
  0.0 1.0 %shard_map.91 = (bf16[80,768]{1,0:T(8,128)(2,1)S(1)}, bf16[72,768]{1,0:T(8,128)(2,1)S(1)}, bf16[32,768]{1,0:T(8,128)(2,1)S(1)}, s32[5,384]{1,0:T(8,128)S(1)}) custom-call(s32[6,384]{1,0:T(8,128)} %constant.2.clone.table_hbm, bf16[20,2,768]{2,1,0:T(2,128)(2,1)} %bitcast.3, bf16[2,20,2,768]{3,2,1,0:T(2,128)(2,1)} %bitcast.2, bf16[2,16,768]{2,1,0:T(8,128)(2,1)} %query_hbm.1), custom_call_target="tpu_custom_call" | custom-call | tf_op jit(solution)/shard_map/pallas_call | solution.py:204
  1.0 3.1 %collective-permute-start.2 = (bf16[80,768]{1,0:T(8,128)(2,1)S(1)}, bf16[80,768]{1,0:T(8,128)(2,1)S(1)}, u32[]{:S(2)}, u32[]{:S(2)}) collective-permute-start(bf16[80,768]{1,0:T(8,128)(2,1)S(1)} %get-tuple-element.19.own_ref), channel_id=1, source_target_pairs={{0,4},{2,6},{4,0},{6,2},{8,12},{10,14},{12,8},{14,10},{1,5},{3,7},... | collective-permute-start | bytes 368648 | tf_op jit(solution)/shard_map/ppermute | solution.py:225
  4.1 1.5 %collective-permute-start.1 = (bf16[80,768]{1,0:T(8,128)(2,1)S(1)}, bf16[80,768]{1,0:T(8,128)(2,1)S(1)}, u32[]{:S(2)}, u32[]{:S(2)}) collective-permute-start(bf16[80,768]{1,0:T(8,128)(2,1)S(1)} %get-tuple-element.19.own_ref), channel_id=1, source_target_pairs={{0,2},{2,0},{4,6},{6,4},{8,10},{10,8},{12,14},{14,12},{1,3},{3,1},... | collective-permute-start | bytes 368648 | tf_op jit(solution)/shard_map/ppermute | solution.py:225
  5.6 0.0 collective-permute-start
  5.7 3.0 %collective-permute-start.3 = (bf16[32,768]{1,0:T(8,128)(2,1)S(1)}, bf16[32,768]{1,0:T(8,128)(2,1)S(1)}, u32[]{:S(2)}, u32[]{:S(2)}) collective-permute-start(bf16[32,768]{1,0:T(8,128)(2,1)S(1)} %get-tuple-element.23), channel_id=1, source_target_pairs={{0,8},{1,13},{2,10},{3,15},{4,12},{5,9},{6,14},{7,11},{8,0},{9,5},... | collective-permute-start | bytes 147464 | tf_op jit(solution)/shard_map/ppermute | solution.py:232
  9.3 2.5 %shard_map.92 = (f32[4,384]{1,0:T(4,128)S(1)}, f32[16,3072]{1,0:T(8,128)S(1)}, f32[2,3072]{1,0:T(2,128)S(1)}, bf16[768,3072]{1,0:T(8,128)(2,1)S(1)}) custom-call(s32[1]{0:T(128)S(6)} %copy.10.text_ref, s32[5,384]{1,0:T(8,128)S(1)} %get-tuple-element.17.mask_ref, s32[2]{0:T(128)} %plan_hbm.1, bf16[28,3072]{1,0:T(8,128)(2,1)} %table_hbm.2, ...), custom_call_target="tpu_custom_call" | custom-call | tf_op jit(solution)/shard_map/pallas_call | solution.py:236
  11.8 0.0 collective-permute-done.3.query_ref
  11.8 0.0 collective-permute-done.2.refs_2_
  11.8 0.0 collective-permute-done.1.refs_1_
  11.8 0.0 collective-permute-done.refs_0_
  11.9 0.6 %shard_map.94 = bf16[32,896]{1,0:T(8,128)(2,1)S(1)} custom-call(f32[4,384]{1,0:T(4,128)S(1)} %get-tuple-element.18.bias_ref, bf16[80,768]{1,0:T(8,128)(2,1)S(1)} %get-tuple-element.19.own_ref, bf16[72,768]{1,0:T(8,128)(2,1)S(1)} %get-tuple-element.20.local_ref, bf16[32,768]{1,0:T(8,128)(2,1)S(1)} %collective-permute-done.3.query_ref, ...), custom_call_target="tpu_custom_call" | custom-call | tf_op jit(solution)/shard_map/pallas_call | solution.py:249
  12.5 2.5 %collective-permute-start.4 = (bf16[32,896]{1,0:T(8,128)(2,1)S(1)}, bf16[32,896]{1,0:T(8,128)(2,1)S(1)}, u32[]{:S(2)}, u32[]{:S(2)}) collective-permute-start(bf16[32,896]{1,0:T(8,128)(2,1)S(1)} %shard_map.94), channel_id=1, source_target_pairs={{0,8},{1,13},{2,10},{3,15},{4,12},{5,9},{6,14},{7,11},{8,0},{9,5},... | collective-permute-start | bytes 172040 | tf_op jit(solution)/shard_map/ppermute | solution.py:232
  15.0 0.6 %shard_map.93 = (f32[32,768]{1,0:T(8,128)S(1)}, f32[32,128]{1,0:T(8,128)S(1)}) custom-call(f32[4,384]{1,0:T(4,128)S(1)} %get-tuple-element.18.bias_ref, bf16[80,768]{1,0:T(8,128)(2,1)S(1)} %get-tuple-element.19.own_ref, bf16[72,768]{1,0:T(8,128)(2,1)S(1)} %get-tuple-element.20.local_ref, bf16[80,768]{1,0:T(8,128)(2,1)S(1)} %collective-permute-done.refs_0_, ...), custom_call_target="tpu_custom_call" | custom-call | tf_op jit(solution)/shard_map/pallas_call | solution.py:256
  15.6 2.3 %collective-permute-done.4.partner_ref = bf16[32,896]{1,0:T(8,128)(2,1)S(1)} collective-permute-done((bf16[32,896]{1,0:T(8,128)(2,1)S(1)}, bf16[32,896]{1,0:T(8,128)(2,1)S(1)}, u32[]{:S(2)}, u32[]{:S(2)}) %collective-permute-start.4) | collective-permute-done | bytes 57376 | tf_op jit(solution)/shard_map/ppermute | solution.py:232
  17.9 1.1 %shard_map.95 = (f32[8,3072]{1,0:T(8,128)S(1)}, bf16[8,3072]{1,0:T(8,128)(2,1)S(1)}) custom-call(f32[32,768]{1,0:T(8,128)S(1)} %get-tuple-element.21.mixed_ref, f32[32,128]{1,0:T(8,128)S(1)} %get-tuple-element.22.log_ref, bf16[32,896]{1,0:T(8,128)(2,1)S(1)} %collective-permute-done.4.partner_ref, bf16[768,3072]{1,0:T(8,128)(2,1)S(1)} %get-tuple-element.24.weight_ref, ...), custom_call_target="tpu_custom_call" | custom-call | tf_op jit(solution)/shard_map/pallas_call | solution.py:265
  19.0 0.1 collective-permute-start.5
  19.1 1.2 %collective-permute-done.5 = bf16[8,3072]{1,0:T(8,128)(2,1)S(1)} collective-permute-done((bf16[8,3072]{1,0:T(8,128)(2,1)S(1)}, bf16[8,3072]{1,0:T(8,128)(2,1)S(1)}, u32[]{:S(2)}, u32[]{:S(2)}) %collective-permute-start.5) | collective-permute-done | bytes 49184 | tf_op jit(solution)/shard_map/ppermute | solution.py:272
  20.3 0.6 %add_convert_fusion = bf16[8,3072]{1,0:T(8,128)(2,1)} fusion(f32[8,3072]{1,0:T(8,128)S(1)} %get-tuple-element.27, bf16[8,3072]{1,0:T(8,128)(2,1)S(1)} %collective-permute-done.5), kind=kLoop, calls=%fused_computation | loop fusion | flops 73728 | bytes 196608 | tf_op jit(solution)/shard_map/convert_element_type | solution.py:273
Async XLA Ops:
  1.0 10.8 %collective-permute-start.2 = (bf16[80,768]{1,0:T(8,128)(2,1)S(1)}, bf16[80,768]{1,0:T(8,128)(2,1)S(1)}, u32[]{:S(2)}, u32[]{:S(2)}) collective-permute-start(bf16[80,768]{1,0:T(8,128)(2,1)S(1)} %get-tuple-element.19.own_ref), channel_id=1, source_target_pairs={{0,4},{2,6},{4,0},{6,2},{8,12},{10,14},{12,8},{14,10},{1,5},{3,7},... | collective-permute-start | bytes 368648 | tf_op jit(solution)/shard_map/ppermute | solution.py:225
  4.1 7.7 %collective-permute-start.1 = (bf16[80,768]{1,0:T(8,128)(2,1)S(1)}, bf16[80,768]{1,0:T(8,128)(2,1)S(1)}, u32[]{:S(2)}, u32[]{:S(2)}) collective-permute-start(bf16[80,768]{1,0:T(8,128)(2,1)S(1)} %get-tuple-element.19.own_ref), channel_id=1, source_target_pairs={{0,2},{2,0},{4,6},{6,4},{8,10},{10,8},{12,14},{14,12},{1,3},{3,1},... | collective-permute-start | bytes 368648 | tf_op jit(solution)/shard_map/ppermute | solution.py:225
  5.6 6.2 %collective-permute-start = (bf16[80,768]{1,0:T(8,128)(2,1)S(1)}, bf16[80,768]{1,0:T(8,128)(2,1)S(1)}, u32[]{:S(2)}, u32[]{:S(2)}) collective-permute-start(bf16[80,768]{1,0:T(8,128)(2,1)S(1)} %get-tuple-element.19.own_ref), channel_id=1, source_target_pairs={{0,6},{2,4},{4,2},{6,0},{8,14},{10,12},{12,10},{14,8},{1,7},{3,5},... | collective-permute-start | bytes 368648 | tf_op jit(solution)/shard_map/ppermute | solution.py:225
  5.7 6.2 %collective-permute-start.3 = (bf16[32,768]{1,0:T(8,128)(2,1)S(1)}, bf16[32,768]{1,0:T(8,128)(2,1)S(1)}, u32[]{:S(2)}, u32[]{:S(2)}) collective-permute-start(bf16[32,768]{1,0:T(8,128)(2,1)S(1)} %get-tuple-element.23), channel_id=1, source_target_pairs={{0,8},{1,13},{2,10},{3,15},{4,12},{5,9},{6,14},{7,11},{8,0},{9,5},... | collective-permute-start | bytes 147464 | tf_op jit(solution)/shard_map/ppermute | solution.py:232
  12.5 5.4 %collective-permute-start.4 = (bf16[32,896]{1,0:T(8,128)(2,1)S(1)}, bf16[32,896]{1,0:T(8,128)(2,1)S(1)}, u32[]{:S(2)}, u32[]{:S(2)}) collective-permute-start(bf16[32,896]{1,0:T(8,128)(2,1)S(1)} %shard_map.94), channel_id=1, source_target_pairs={{0,8},{1,13},{2,10},{3,15},{4,12},{5,9},{6,14},{7,11},{8,0},{9,5},... | collective-permute-start | bytes 172040 | tf_op jit(solution)/shard_map/ppermute | solution.py:232
  19.0 1.3 %collective-permute-start.5 = (bf16[8,3072]{1,0:T(8,128)(2,1)S(1)}, bf16[8,3072]{1,0:T(8,128)(2,1)S(1)}, u32[]{:S(2)}, u32[]{:S(2)}) collective-permute-start(bf16[8,3072]{1,0:T(8,128)(2,1)S(1)} %get-tuple-element.28), channel_id=1, source_target_pairs={{0,1},{1,0},{2,3},{3,2},{4,5},{5,4},{6,7},{7,6},{8,9},{9,8},{10,11... | collective-permute-start | bytes 147464 | tf_op jit(solution)/shard_map/ppermute | solution.py:272

commit v7 on v6

--- a/solution.py
+++ b/solution.py
@@ -106,10 +106,10 @@
     partner_ref[:, own_ref.shape[1] :] = coded.astype(jnp.bfloat16)
 
 
-def decoded(packed_ref, width):
-    coded = packed_ref[:, width:].astype(jnp.float32)
+def decoded(packed, width):
+    coded = packed[:, width:]
     logs = pltpu.roll(coded, LANES - 2 * TERM_LANES, 1) + pltpu.roll(coded, LANES - TERM_LANES, 1) + coded
-    return packed_ref[:, :width].astype(jnp.float32), logs
+    return packed[:, :width], logs
 
 
 def joined(one, two, lane_blocks):
@@ -158,15 +158,22 @@
         copy.wait()
 
 
-def project_kernel(mixed_ref, log_ref, partner_ref, weight_ref, gates_ref, sum_ref, keep_ref, send_ref):
-    strip = sum_ref.shape[0]
-    half = keep_ref.shape[0]
-    attended = joined((mixed_ref[...], log_ref[...]), decoded(partner_ref, mixed_ref.shape[1]), blocks_of(mixed_ref))
+def rows_of(rows, mine):
+    part = rows.shape[0] // 4
+    low = jnp.concatenate([rows[:part], rows[2 * part : 3 * part]], axis=0)
+    high = jnp.concatenate([rows[part : 2 * part], rows[3 * part :]], axis=0)
+    return jnp.where((lax.axis_index("head") == 0) == mine, low, high)
+
+
+def project_kernel(mine, mixed_ref, log_ref, partner_ref, weight_ref, gates_ref, sum_ref, out_ref):
+    half = out_ref.shape[0]
+    own = rows_of(mixed_ref[...], mine), rows_of(log_ref[...], mine)
+    partner = rows_of(partner_ref[...].astype(jnp.float32), mine)
+    attended = joined(own, decoded(partner, mixed_ref.shape[1]), blocks_of(mixed_ref))
     projected = jnp.dot(attended, weight_ref[...], preferred_element_type=jnp.float32)
-    total = sum_ref[...] + gates_ref[0:1, :] * projected[:strip] + gates_ref[1:2, :] * projected[strip:]
-    first = lax.axis_index("head") == 0
-    keep_ref[...] = jnp.where(first, total[:half], total[half:])
-    send_ref[...] = jnp.where(first, total[half:], total[:half]).astype(jnp.bfloat16)
+    base = jnp.where((lax.axis_index("head") == 0) == mine, sum_ref[:half, :], sum_ref[half:, :])
+    total = base + gates_ref[0:1, :] * projected[:half] + gates_ref[1:2, :] * projected[half:]
+    out_ref[...] = total.astype(out_ref.dtype)
 
 
 def per_device(queries, stale_pairs, step_pairs, hidden, out_weight, gate_table, t_index, text_len):
@@ -262,13 +269,16 @@
     )(bias, block, local, *others)
     partner_rows = to_partner(partial_rows)
 
-    keep, send = pl.pallas_call(
-        project_kernel,
-        out_shape=(f32((lat_rows // 2, model)), bf16((lat_rows // 2, model))),
-        in_specs=[vmem] * 6,
-        out_specs=(vmem, vmem),
-        compiler_params=params,
-    )(mixed, logs, partner_rows, weight, gates, total)
+    def project(mine, dtype):
+        return pl.pallas_call(
+            functools.partial(project_kernel, mine),
+            out_shape=jax.ShapeDtypeStruct((lat_rows // 2, model), dtype),
+            in_specs=[vmem] * 6,
+            out_specs=vmem,
+            compiler_params=params,
+        )(mixed, logs, partner_rows, weight, gates, total)
+
+    send, keep = project(False, jnp.bfloat16), project(True, jnp.float32)
     received = lax.ppermute(send, "head", [(0, 1), (1, 0)])
     return (keep + received.astype(jnp.float32)).astype(jnp.bfloat16)
 

time: 21.1 us -> 20.8 us (0.986)
  waiting for transfers between devices: 3.51 us -> 2.64 us
  Pallas kernels: 5.85 us -> 6.55 us
    ppermute x1, waiting for transfers between devices: 1.22 us -> 0.35 us  [per_device(): received = lax.ppermute(send, 'head', [(0, 1), (1, 0)])]
    pallas_call x1 -> x2, Pallas kernels: 1.07 us -> 1.76 us  [project(): pl.pallas_call(functools.partial(project_kernel, mine), out_shape=jax.Sha...]
  transfers between devices with their start and end apart: 6 -> 6, of which waited for: 2 -> 2; matrix products, arithmetic and copies ran while one was open for 0% -> 0% of each run, Pallas kernels for 15% -> 19%
where the time goes in v7:
time: 20.8 us; the launch traced here: 20.7 us
  starting transfers between devices  10.1 us (49%)
  Pallas kernels  6.55 us (31%)
  waiting for transfers between devices  2.64 us (13%)
  between operations  0.72 us (3%)
  other arithmetic  0.63 us (3%)
    ppermute x2, starting transfers between devices, to_partner(): return lax.ppermute(rows, ('patch', 'head'), pairs)  5.48 us
    ppermute x3, starting transfers between devices, to(): return lax.ppermute(rows, 'patch', [(i, i ^ flip) for i in range(strips)])  4.63 us
    pallas_call x1, Pallas kernels, per_device(): pl.pallas_call(fetch_kernel, out_shape=(f32((len(whose), columns)), f32((...  2.54 us
    ppermute x2, waiting for transfers between devices, to_partner(): return lax.ppermute(rows, ('patch', 'head'), pairs)  2.28 us
    pallas_call x2, Pallas kernels, project(): pl.pallas_call(functools.partial(project_kernel, mine), out_shape=jax.Sha...  1.76 us
    pallas_call x1, Pallas kernels, per_device(): pl.pallas_call(functools.partial(pack_kernel, text_rows), out_shape=(bf16...  1.01 us
    convert_element_type x1, other arithmetic, per_device(): return (keep + received.astype(jnp.float32)).astype(jnp.bfloat16)  0.63 us
    pallas_call x1, Pallas kernels, per_device(): pl.pallas_call(functools.partial(partner_kernel, query_rows), out_shape=b...  0.63 us
  transfers between devices with their start and end apart: 6, of which 2 were waited for; matrix products, arithmetic and copies ran while one was open for 0% of the time, Pallas kernels for 19%

profile of v7, /device:TPU:0, one launch (start us, length us, event | category | flops | bytes accessed | tf_op | source)
XLA Modules:
  0.0 20.7 jit_solution(10296162557759468369)
XLA Ops:
  0.0 1.0 %shard_map.91 = (bf16[80,768]{1,0:T(8,128)(2,1)S(1)}, bf16[72,768]{1,0:T(8,128)(2,1)S(1)}, bf16[32,768]{1,0:T(8,128)(2,1)S(1)}, s32[5,384]{1,0:T(8,128)S(1)}) custom-call(s32[6,384]{1,0:T(8,128)} %constant.2.clone.table_hbm, bf16[20,2,768]{2,1,0:T(2,128)(2,1)} %bitcast.3, bf16[2,20,2,768]{3,2,1,0:T(2,128)(2,1)} %bitcast.2, bf16[2,16,768]{2,1,0:T(8,128)(2,1)} %query_hbm.1), custom_call_target="tpu_custom_call" | custom-call | tf_op jit(solution)/shard_map/pallas_call | solution.py:211
  1.0 3.1 %collective-permute-start.2 = (bf16[80,768]{1,0:T(8,128)(2,1)S(1)}, bf16[80,768]{1,0:T(8,128)(2,1)S(1)}, u32[]{:S(2)}, u32[]{:S(2)}) collective-permute-start(bf16[80,768]{1,0:T(8,128)(2,1)S(1)} %get-tuple-element.17.own_ref), channel_id=1, source_target_pairs={{0,4},{2,6},{4,0},{6,2},{8,12},{10,14},{12,8},{14,10},{1,5},{3,7},... | collective-permute-start | bytes 368648 | tf_op jit(solution)/shard_map/ppermute | solution.py:232
  4.1 1.5 %collective-permute-start.1 = (bf16[80,768]{1,0:T(8,128)(2,1)S(1)}, bf16[80,768]{1,0:T(8,128)(2,1)S(1)}, u32[]{:S(2)}, u32[]{:S(2)}) collective-permute-start(bf16[80,768]{1,0:T(8,128)(2,1)S(1)} %get-tuple-element.17.own_ref), channel_id=1, source_target_pairs={{0,2},{2,0},{4,6},{6,4},{8,10},{10,8},{12,14},{14,12},{1,3},{3,1},... | collective-permute-start | bytes 368648 | tf_op jit(solution)/shard_map/ppermute | solution.py:232
  5.6 0.0 collective-permute-start
  5.7 3.0 %collective-permute-start.3 = (bf16[32,768]{1,0:T(8,128)(2,1)S(1)}, bf16[32,768]{1,0:T(8,128)(2,1)S(1)}, u32[]{:S(2)}, u32[]{:S(2)}) collective-permute-start(bf16[32,768]{1,0:T(8,128)(2,1)S(1)} %get-tuple-element.21), channel_id=1, source_target_pairs={{0,8},{1,13},{2,10},{3,15},{4,12},{5,9},{6,14},{7,11},{8,0},{9,5},... | collective-permute-start | bytes 147464 | tf_op jit(solution)/shard_map/ppermute | solution.py:239
  9.3 2.5 %shard_map.92 = (f32[4,384]{1,0:T(4,128)S(1)}, f32[16,3072]{1,0:T(8,128)S(1)}, f32[2,3072]{1,0:T(2,128)S(1)}, bf16[768,3072]{1,0:T(8,128)(2,1)S(1)}) custom-call(s32[1]{0:T(128)S(6)} %copy.10.text_ref, s32[5,384]{1,0:T(8,128)S(1)} %get-tuple-element.15.mask_ref, s32[2]{0:T(128)} %plan_hbm.1, bf16[28,3072]{1,0:T(8,128)(2,1)} %table_hbm.2, ...), custom_call_target="tpu_custom_call" | custom-call | tf_op jit(solution)/shard_map/pallas_call | solution.py:243
  11.8 0.0 collective-permute-done.3.query_ref
  11.8 0.0 collective-permute-done.2.refs_2_
  11.8 0.0 collective-permute-done.1.refs_1_
  11.8 0.0 collective-permute-done.refs_0_
  11.9 0.6 %shard_map.94 = bf16[32,896]{1,0:T(8,128)(2,1)S(1)} custom-call(f32[4,384]{1,0:T(4,128)S(1)} %get-tuple-element.16.bias_ref, bf16[80,768]{1,0:T(8,128)(2,1)S(1)} %get-tuple-element.17.own_ref, bf16[72,768]{1,0:T(8,128)(2,1)S(1)} %get-tuple-element.18.local_ref, bf16[32,768]{1,0:T(8,128)(2,1)S(1)} %collective-permute-done.3.query_ref, ...), custom_call_target="tpu_custom_call" | custom-call | tf_op jit(solution)/shard_map/pallas_call | solution.py:256
  12.5 2.5 %collective-permute-start.4 = (bf16[32,896]{1,0:T(8,128)(2,1)S(1)}, bf16[32,896]{1,0:T(8,128)(2,1)S(1)}, u32[]{:S(2)}, u32[]{:S(2)}) collective-permute-start(bf16[32,896]{1,0:T(8,128)(2,1)S(1)} %shard_map.94), channel_id=1, source_target_pairs={{0,8},{1,13},{2,10},{3,15},{4,12},{5,9},{6,14},{7,11},{8,0},{9,5},... | collective-permute-start | bytes 172040 | tf_op jit(solution)/shard_map/ppermute | solution.py:239
  15.0 0.6 %shard_map.93 = (f32[32,768]{1,0:T(8,128)S(1)}, f32[32,128]{1,0:T(8,128)S(1)}) custom-call(f32[4,384]{1,0:T(4,128)S(1)} %get-tuple-element.16.bias_ref, bf16[80,768]{1,0:T(8,128)(2,1)S(1)} %get-tuple-element.17.own_ref, bf16[72,768]{1,0:T(8,128)(2,1)S(1)} %get-tuple-element.18.local_ref, bf16[80,768]{1,0:T(8,128)(2,1)S(1)} %collective-permute-done.refs_0_, ...), custom_call_target="tpu_custom_call" | custom-call | tf_op jit(solution)/shard_map/pallas_call | solution.py:263
  15.6 2.3 %collective-permute-done.4.partner_ref = bf16[32,896]{1,0:T(8,128)(2,1)S(1)} collective-permute-done((bf16[32,896]{1,0:T(8,128)(2,1)S(1)}, bf16[32,896]{1,0:T(8,128)(2,1)S(1)}, u32[]{:S(2)}, u32[]{:S(2)}) %collective-permute-start.4) | collective-permute-done | bytes 57376 | tf_op jit(solution)/shard_map/ppermute | solution.py:239
  17.9 0.9 %shard_map.96 = bf16[8,3072]{1,0:T(8,128)(2,1)S(1)} custom-call(f32[32,768]{1,0:T(8,128)S(1)} %get-tuple-element.19.mixed_ref, f32[32,128]{1,0:T(8,128)S(1)} %get-tuple-element.20.log_ref, bf16[32,896]{1,0:T(8,128)(2,1)S(1)} %collective-permute-done.4.partner_ref, bf16[768,3072]{1,0:T(8,128)(2,1)S(1)} %get-tuple-element.22.weight_ref, ...), custom_call_target="tpu_custom_call" | custom-call | tf_op jit(solution)/shard_map/pallas_call | solution.py:273
  18.8 0.0 collective-permute-start.5
  18.8 0.9 %shard_map.95 = f32[8,3072]{1,0:T(8,128)S(1)} custom-call(f32[32,768]{1,0:T(8,128)S(1)} %get-tuple-element.19.mixed_ref, f32[32,128]{1,0:T(8,128)S(1)} %get-tuple-element.20.log_ref, bf16[32,896]{1,0:T(8,128)(2,1)S(1)} %collective-permute-done.4.partner_ref, bf16[768,3072]{1,0:T(8,128)(2,1)S(1)} %get-tuple-element.22.weight_ref, ...), custom_call_target="tpu_custom_call" | custom-call | tf_op jit(solution)/shard_map/pallas_call | solution.py:273
  19.7 0.3 %collective-permute-done.5 = bf16[8,3072]{1,0:T(8,128)(2,1)S(1)} collective-permute-done((bf16[8,3072]{1,0:T(8,128)(2,1)S(1)}, bf16[8,3072]{1,0:T(8,128)(2,1)S(1)}, u32[]{:S(2)}, u32[]{:S(2)}) %collective-permute-start.5) | collective-permute-done | bytes 49184 | tf_op jit(solution)/shard_map/ppermute | solution.py:282
  20.0 0.6 %add_convert_fusion = bf16[8,3072]{1,0:T(8,128)(2,1)} fusion(f32[8,3072]{1,0:T(8,128)S(1)} %shard_map.95, bf16[8,3072]{1,0:T(8,128)(2,1)S(1)} %collective-permute-done.5), kind=kLoop, calls=%fused_computation | loop fusion | flops 73728 | bytes 196608 | tf_op jit(solution)/shard_map/convert_element_type | solution.py:283
Async XLA Ops:
  1.0 10.8 %collective-permute-start.2 = (bf16[80,768]{1,0:T(8,128)(2,1)S(1)}, bf16[80,768]{1,0:T(8,128)(2,1)S(1)}, u32[]{:S(2)}, u32[]{:S(2)}) collective-permute-start(bf16[80,768]{1,0:T(8,128)(2,1)S(1)} %get-tuple-element.17.own_ref), channel_id=1, source_target_pairs={{0,4},{2,6},{4,0},{6,2},{8,12},{10,14},{12,8},{14,10},{1,5},{3,7},... | collective-permute-start | bytes 368648 | tf_op jit(solution)/shard_map/ppermute | solution.py:232
  4.1 7.7 %collective-permute-start.1 = (bf16[80,768]{1,0:T(8,128)(2,1)S(1)}, bf16[80,768]{1,0:T(8,128)(2,1)S(1)}, u32[]{:S(2)}, u32[]{:S(2)}) collective-permute-start(bf16[80,768]{1,0:T(8,128)(2,1)S(1)} %get-tuple-element.17.own_ref), channel_id=1, source_target_pairs={{0,2},{2,0},{4,6},{6,4},{8,10},{10,8},{12,14},{14,12},{1,3},{3,1},... | collective-permute-start | bytes 368648 | tf_op jit(solution)/shard_map/ppermute | solution.py:232
  5.6 6.2 %collective-permute-start = (bf16[80,768]{1,0:T(8,128)(2,1)S(1)}, bf16[80,768]{1,0:T(8,128)(2,1)S(1)}, u32[]{:S(2)}, u32[]{:S(2)}) collective-permute-start(bf16[80,768]{1,0:T(8,128)(2,1)S(1)} %get-tuple-element.17.own_ref), channel_id=1, source_target_pairs={{0,6},{2,4},{4,2},{6,0},{8,14},{10,12},{12,10},{14,8},{1,7},{3,5},... | collective-permute-start | bytes 368648 | tf_op jit(solution)/shard_map/ppermute | solution.py:232
  5.7 6.2 %collective-permute-start.3 = (bf16[32,768]{1,0:T(8,128)(2,1)S(1)}, bf16[32,768]{1,0:T(8,128)(2,1)S(1)}, u32[]{:S(2)}, u32[]{:S(2)}) collective-permute-start(bf16[32,768]{1,0:T(8,128)(2,1)S(1)} %get-tuple-element.21), channel_id=1, source_target_pairs={{0,8},{1,13},{2,10},{3,15},{4,12},{5,9},{6,14},{7,11},{8,0},{9,5},... | collective-permute-start | bytes 147464 | tf_op jit(solution)/shard_map/ppermute | solution.py:239
  12.5 5.4 %collective-permute-start.4 = (bf16[32,896]{1,0:T(8,128)(2,1)S(1)}, bf16[32,896]{1,0:T(8,128)(2,1)S(1)}, u32[]{:S(2)}, u32[]{:S(2)}) collective-permute-start(bf16[32,896]{1,0:T(8,128)(2,1)S(1)} %shard_map.94), channel_id=1, source_target_pairs={{0,8},{1,13},{2,10},{3,15},{4,12},{5,9},{6,14},{7,11},{8,0},{9,5},... | collective-permute-start | bytes 172040 | tf_op jit(solution)/shard_map/ppermute | solution.py:239
  18.8 1.2 %collective-permute-start.5 = (bf16[8,3072]{1,0:T(8,128)(2,1)S(1)}, bf16[8,3072]{1,0:T(8,128)(2,1)S(1)}, u32[]{:S(2)}, u32[]{:S(2)}) collective-permute-start(bf16[8,3072]{1,0:T(8,128)(2,1)S(1)} %shard_map.96), channel_id=1, source_target_pairs={{0,1},{1,0},{2,3},{3,2},{4,5},{5,4},{6,7},{7,6},{8,9},{9,8},{10,11... | collective-permute-start | bytes 147464 | tf_op jit(solution)/shard_map/ppermute | solution.py:282

commit v8 on v7

--- a/solution.py
+++ b/solution.py
@@ -13,7 +13,7 @@
 MASKED = -1e30
 VMEM_LIMIT = 24 * 1024 * 1024
 TERMS, TERM_LANES = 3, 32
-CHUNKS = 6
+CHUNKS = 4
 
 
 def round_up(value, step):
@@ -165,12 +165,29 @@
     return jnp.where((lax.axis_index("head") == 0) == mine, low, high)
 
 
-def project_kernel(mine, mixed_ref, log_ref, partner_ref, weight_ref, gates_ref, sum_ref, out_ref):
+def fetch_rest_kernel(_, weight_hbm, weight_ref, sems):
+    rows = weight_ref.shape[0]
+    depth = rows // CHUNKS
+    copies = [
+        pltpu.make_async_copy(
+            weight_hbm.at[pl.ds(rows + chunk * depth, depth), :], weight_ref.at[pl.ds(chunk * depth, depth), :], sems.at[chunk]
+        )
+        for chunk in range(CHUNKS)
+    ]
+    for copy in copies:
+        copy.start()
+    for copy in copies:
+        copy.wait()
+
+
+def project_kernel(mine, mixed_ref, log_ref, partner_ref, weight_ref, rest_ref, gates_ref, sum_ref, out_ref):
     half = out_ref.shape[0]
     own = rows_of(mixed_ref[...], mine), rows_of(log_ref[...], mine)
     partner = rows_of(partner_ref[...].astype(jnp.float32), mine)
     attended = joined(own, decoded(partner, mixed_ref.shape[1]), blocks_of(mixed_ref))
-    projected = jnp.dot(attended, weight_ref[...], preferred_element_type=jnp.float32)
+    depth = weight_ref.shape[0]
+    projected = jnp.dot(attended[:, :depth], weight_ref[...], preferred_element_type=jnp.float32)
+    projected += jnp.dot(attended[:, depth:], rest_ref[...], preferred_element_type=jnp.float32)
     base = jnp.where((lax.axis_index("head") == 0) == mine, sum_ref[:half, :], sum_ref[half:, :])
     total = base + gates_ref[0:1, :] * projected[:half] + gates_ref[1:2, :] * projected[half:]
     out_ref[...] = total.astype(out_ref.dtype)
@@ -242,7 +259,7 @@
     others = [to(block, flip) for flip in neighbours]
     bias, total, gates, weight = pl.pallas_call(
         fetch_kernel,
-        out_shape=(f32((len(whose), columns)), f32((lat_rows, model)), f32((2, model)), bf16(out_weight.shape)),
+        out_shape=(f32((len(whose), columns)), f32((lat_rows, model)), f32((2, model)), bf16((width // 2, model))),
         in_specs=[smem, vmem] + [hbm] * 4,
         out_specs=(vmem,) * 4,
         scratch_shapes=[
@@ -269,14 +286,23 @@
     )(bias, block, local, *others)
     partner_rows = to_partner(partial_rows)
 
+    rest = pl.pallas_call(
+        fetch_rest_kernel,
+        out_shape=bf16((width // 2, model)),
+        in_specs=[vmem, hbm],
+        out_specs=vmem,
+        scratch_shapes=[pltpu.SemaphoreType.DMA((CHUNKS,))],
+        compiler_params=params,
+    )(logs, *in_hbm(out_weight))
+
     def project(mine, dtype):
         return pl.pallas_call(
             functools.partial(project_kernel, mine),
             out_shape=jax.ShapeDtypeStruct((lat_rows // 2, model), dtype),
-            in_specs=[vmem] * 6,
+            in_specs=[vmem] * 7,
             out_specs=vmem,
             compiler_params=params,
-        )(mixed, logs, partner_rows, weight, gates, total)
+        )(mixed, logs, partner_rows, weight, rest, gates, total)
 
     send, keep = project(False, jnp.bfloat16), project(True, jnp.float32)
     received = lax.ppermute(send, "head", [(0, 1), (1, 0)])

time: 20.8 us -> 20.8 us (level)
  waiting for transfers between devices: 2.64 us -> 1.45 us
  Pallas kernels: 6.55 us -> 7.46 us
  starting transfers between devices: 10.1 us -> 10.4 us
    ppermute x2, waiting for transfers between devices: 2.28 us -> 0.57 us  [to_partner(): return lax.ppermute(rows, ('patch', 'head'), pairs)]
    pallas_call x0 -> x1, Pallas kernels: none -> 1.65 us  [per_device(): pl.pallas_call(fetch_rest_kernel, out_shape=bf16((width // 2, model)), in...]
    pallas_call x1, Pallas kernels: 2.54 us -> 1.8 us  [per_device(): pl.pallas_call(fetch_kernel, out_shape=(f32((len(whose), columns)), f32((...]
    ppermute x3, waiting for transfers between devices: 0.01 us -> 0.53 us  [to(): return lax.ppermute(rows, 'patch', [(i, i ^ flip) for i in range(strips)])]
    ppermute x2, starting transfers between devices: 5.48 us -> 5.71 us  [to_partner(): return lax.ppermute(rows, ('patch', 'head'), pairs)]
  transfers between devices with their start and end apart: 6 -> 6, of which waited for: 2 -> 3; matrix products, arithmetic and copies ran while one was open for 0% -> 0% of each run, Pallas kernels for 19% -> 24%
where the time goes in v8:
time: 20.8 us; the launch traced here: 20.6 us
  starting transfers between devices  10.4 us (50%)
  Pallas kernels  7.46 us (36%)
  waiting for transfers between devices  1.45 us (7%)
  between operations  0.72 us (3%)
  other arithmetic  0.63 us (3%)
    ppermute x2, starting transfers between devices, to_partner(): return lax.ppermute(rows, ('patch', 'head'), pairs)  5.71 us
    ppermute x3, starting transfers between devices, to(): return lax.ppermute(rows, 'patch', [(i, i ^ flip) for i in range(strips)])  4.63 us
    pallas_call x1, Pallas kernels, per_device(): pl.pallas_call(fetch_kernel, out_shape=(f32((len(whose), columns)), f32((...  1.8 us
    pallas_call x2, Pallas kernels, project(): pl.pallas_call(functools.partial(project_kernel, mine), out_shape=jax.Sha...  1.76 us
    pallas_call x1, Pallas kernels, per_device(): pl.pallas_call(fetch_rest_kernel, out_shape=bf16((width // 2, model)), in...  1.65 us
    pallas_call x1, Pallas kernels, per_device(): pl.pallas_call(functools.partial(pack_kernel, text_rows), out_shape=(bf16...  1.01 us
    convert_element_type x1, other arithmetic, per_device(): return (keep + received.astype(jnp.float32)).astype(jnp.bfloat16)  0.63 us
    pallas_call x1, Pallas kernels, per_device(): pl.pallas_call(functools.partial(partner_kernel, query_rows), out_shape=b...  0.63 us
  transfers between devices with their start and end apart: 6, of which 3 were waited for; matrix products, arithmetic and copies ran while one was open for 0% of the time, Pallas kernels for 24%

profile of v8, /device:TPU:0, one launch (start us, length us, event | category | flops | bytes accessed | tf_op | source)
XLA Modules:
  0.0 20.6 jit_solution(11628713264575056801)
XLA Ops:
  0.0 1.0 %shard_map.91 = (bf16[80,768]{1,0:T(8,128)(2,1)S(1)}, bf16[72,768]{1,0:T(8,128)(2,1)S(1)}, bf16[32,768]{1,0:T(8,128)(2,1)S(1)}, s32[5,384]{1,0:T(8,128)S(1)}) custom-call(s32[6,384]{1,0:T(8,128)} %constant.2.clone.table_hbm, bf16[20,2,768]{2,1,0:T(2,128)(2,1)} %bitcast.3, bf16[2,20,2,768]{3,2,1,0:T(2,128)(2,1)} %bitcast.2, bf16[2,16,768]{2,1,0:T(8,128)(2,1)} %query_hbm.1), custom_call_target="tpu_custom_call" | custom-call | tf_op jit(solution)/shard_map/pallas_call | solution.py:228
  1.0 3.1 %collective-permute-start.2 = (bf16[80,768]{1,0:T(8,128)(2,1)S(1)}, bf16[80,768]{1,0:T(8,128)(2,1)S(1)}, u32[]{:S(2)}, u32[]{:S(2)}) collective-permute-start(bf16[80,768]{1,0:T(8,128)(2,1)S(1)} %get-tuple-element.17.own_ref), channel_id=1, source_target_pairs={{0,4},{2,6},{4,0},{6,2},{8,12},{10,14},{12,8},{14,10},{1,5},{3,7},... | collective-permute-start | bytes 368648 | tf_op jit(solution)/shard_map/ppermute | solution.py:249
  4.1 1.5 %collective-permute-start.1 = (bf16[80,768]{1,0:T(8,128)(2,1)S(1)}, bf16[80,768]{1,0:T(8,128)(2,1)S(1)}, u32[]{:S(2)}, u32[]{:S(2)}) collective-permute-start(bf16[80,768]{1,0:T(8,128)(2,1)S(1)} %get-tuple-element.17.own_ref), channel_id=1, source_target_pairs={{0,2},{2,0},{4,6},{6,4},{8,10},{10,8},{12,14},{14,12},{1,3},{3,1},... | collective-permute-start | bytes 368648 | tf_op jit(solution)/shard_map/ppermute | solution.py:249
  5.6 0.0 collective-permute-start
  5.7 3.0 %collective-permute-start.3 = (bf16[32,768]{1,0:T(8,128)(2,1)S(1)}, bf16[32,768]{1,0:T(8,128)(2,1)S(1)}, u32[]{:S(2)}, u32[]{:S(2)}) collective-permute-start(bf16[32,768]{1,0:T(8,128)(2,1)S(1)} %get-tuple-element.21), channel_id=1, source_target_pairs={{0,8},{1,13},{2,10},{3,15},{4,12},{5,9},{6,14},{7,11},{8,0},{9,5},... | collective-permute-start | bytes 147464 | tf_op jit(solution)/shard_map/ppermute | solution.py:256
  9.3 1.8 %shard_map.92 = (f32[4,384]{1,0:T(4,128)S(1)}, f32[16,3072]{1,0:T(8,128)S(1)}, f32[2,3072]{1,0:T(2,128)S(1)}, bf16[384,3072]{1,0:T(8,128)(2,1)S(1)}) custom-call(s32[1]{0:T(128)S(6)} %copy.10.text_ref, s32[5,384]{1,0:T(8,128)S(1)} %get-tuple-element.15.mask_ref, s32[2]{0:T(128)} %plan_hbm.1, bf16[28,3072]{1,0:T(8,128)(2,1)} %table_hbm.2, ...), custom_call_target="tpu_custom_call" | custom-call | tf_op jit(solution)/shard_map/pallas_call | solution.py:260
  11.1 0.0 collective-permute-done.3.query_ref
  11.1 0.0 collective-permute-done.2.refs_2_
  11.1 0.5 %collective-permute-done.1.refs_1_ = bf16[80,768]{1,0:T(8,128)(2,1)S(1)} collective-permute-done((bf16[80,768]{1,0:T(8,128)(2,1)S(1)}, bf16[80,768]{1,0:T(8,128)(2,1)S(1)}, u32[]{:S(2)}, u32[]{:S(2)}) %collective-permute-start.1) | collective-permute-done | bytes 122912 | tf_op jit(solution)/shard_map/ppermute | solution.py:249
  11.6 0.0 collective-permute-done.refs_0_
  11.6 0.6 %shard_map.94 = bf16[32,896]{1,0:T(8,128)(2,1)S(1)} custom-call(f32[4,384]{1,0:T(4,128)S(1)} %get-tuple-element.16.bias_ref, bf16[80,768]{1,0:T(8,128)(2,1)S(1)} %get-tuple-element.17.own_ref, bf16[72,768]{1,0:T(8,128)(2,1)S(1)} %get-tuple-element.18.local_ref, bf16[32,768]{1,0:T(8,128)(2,1)S(1)} %collective-permute-done.3.query_ref, ...), custom_call_target="tpu_custom_call" | custom-call | tf_op jit(solution)/shard_map/pallas_call | solution.py:273
  12.3 2.8 %collective-permute-start.4 = (bf16[32,896]{1,0:T(8,128)(2,1)S(1)}, bf16[32,896]{1,0:T(8,128)(2,1)S(1)}, u32[]{:S(2)}, u32[]{:S(2)}) collective-permute-start(bf16[32,896]{1,0:T(8,128)(2,1)S(1)} %shard_map.94), channel_id=1, source_target_pairs={{0,8},{1,13},{2,10},{3,15},{4,12},{5,9},{6,14},{7,11},{8,0},{9,5},... | collective-permute-start | bytes 172040 | tf_op jit(solution)/shard_map/ppermute | solution.py:256
  15.0 0.6 %shard_map.93 = (f32[32,768]{1,0:T(8,128)S(1)}, f32[32,128]{1,0:T(8,128)S(1)}) custom-call(f32[4,384]{1,0:T(4,128)S(1)} %get-tuple-element.16.bias_ref, bf16[80,768]{1,0:T(8,128)(2,1)S(1)} %get-tuple-element.17.own_ref, bf16[72,768]{1,0:T(8,128)(2,1)S(1)} %get-tuple-element.18.local_ref, bf16[80,768]{1,0:T(8,128)(2,1)S(1)} %collective-permute-done.refs_0_, ...), custom_call_target="tpu_custom_call" | custom-call | tf_op jit(solution)/shard_map/pallas_call | solution.py:280
  15.6 1.6 %shard_map.95.rest_ref = bf16[384,3072]{1,0:T(8,128)(2,1)S(1)} custom-call(f32[32,128]{1,0:T(8,128)S(1)} %get-tuple-element.20._.log_ref, bf16[768,3072]{1,0:T(8,128)(2,1)} %weight_hbm.3), custom_call_target="tpu_custom_call" | custom-call | tf_op jit(solution)/shard_map/pallas_call | solution.py:289
  17.3 0.6 %collective-permute-done.4.partner_ref = bf16[32,896]{1,0:T(8,128)(2,1)S(1)} collective-permute-done((bf16[32,896]{1,0:T(8,128)(2,1)S(1)}, bf16[32,896]{1,0:T(8,128)(2,1)S(1)}, u32[]{:S(2)}, u32[]{:S(2)}) %collective-permute-start.4) | collective-permute-done | bytes 57376 | tf_op jit(solution)/shard_map/ppermute | solution.py:256
  17.9 0.9 %shard_map.97 = bf16[8,3072]{1,0:T(8,128)(2,1)S(1)} custom-call(f32[32,768]{1,0:T(8,128)S(1)} %get-tuple-element.19.mixed_ref, f32[32,128]{1,0:T(8,128)S(1)} %get-tuple-element.20._.log_ref, bf16[32,896]{1,0:T(8,128)(2,1)S(1)} %collective-permute-done.4.partner_ref, bf16[384,3072]{1,0:T(8,128)(2,1)S(1)} %get-tuple-element.22.weight_ref, ...), custom_call_target="tpu_custom_call" | custom-call | tf_op jit(solution)/shard_map/pallas_call | solution.py:299
  18.7 0.0 collective-permute-start.5
  18.8 0.9 %shard_map.96 = f32[8,3072]{1,0:T(8,128)S(1)} custom-call(f32[32,768]{1,0:T(8,128)S(1)} %get-tuple-element.19.mixed_ref, f32[32,128]{1,0:T(8,128)S(1)} %get-tuple-element.20._.log_ref, bf16[32,896]{1,0:T(8,128)(2,1)S(1)} %collective-permute-done.4.partner_ref, bf16[384,3072]{1,0:T(8,128)(2,1)S(1)} %get-tuple-element.22.weight_ref, ...), custom_call_target="tpu_custom_call" | custom-call | tf_op jit(solution)/shard_map/pallas_call | solution.py:299
  19.7 0.3 %collective-permute-done.5 = bf16[8,3072]{1,0:T(8,128)(2,1)S(1)} collective-permute-done((bf16[8,3072]{1,0:T(8,128)(2,1)S(1)}, bf16[8,3072]{1,0:T(8,128)(2,1)S(1)}, u32[]{:S(2)}, u32[]{:S(2)}) %collective-permute-start.5) | collective-permute-done | bytes 49184 | tf_op jit(solution)/shard_map/ppermute | solution.py:308
  20.0 0.6 %add_convert_fusion = bf16[8,3072]{1,0:T(8,128)(2,1)} fusion(f32[8,3072]{1,0:T(8,128)S(1)} %shard_map.96, bf16[8,3072]{1,0:T(8,128)(2,1)S(1)} %collective-permute-done.5), kind=kLoop, calls=%fused_computation | loop fusion | flops 73728 | bytes 196608 | tf_op jit(solution)/shard_map/convert_element_type | solution.py:309
Async XLA Ops:
  1.0 10.1 %collective-permute-start.2 = (bf16[80,768]{1,0:T(8,128)(2,1)S(1)}, bf16[80,768]{1,0:T(8,128)(2,1)S(1)}, u32[]{:S(2)}, u32[]{:S(2)}) collective-permute-start(bf16[80,768]{1,0:T(8,128)(2,1)S(1)} %get-tuple-element.17.own_ref), channel_id=1, source_target_pairs={{0,4},{2,6},{4,0},{6,2},{8,12},{10,14},{12,8},{14,10},{1,5},{3,7},... | collective-permute-start | bytes 368648 | tf_op jit(solution)/shard_map/ppermute | solution.py:249
  4.1 7.5 %collective-permute-start.1 = (bf16[80,768]{1,0:T(8,128)(2,1)S(1)}, bf16[80,768]{1,0:T(8,128)(2,1)S(1)}, u32[]{:S(2)}, u32[]{:S(2)}) collective-permute-start(bf16[80,768]{1,0:T(8,128)(2,1)S(1)} %get-tuple-element.17.own_ref), channel_id=1, source_target_pairs={{0,2},{2,0},{4,6},{6,4},{8,10},{10,8},{12,14},{14,12},{1,3},{3,1},... | collective-permute-start | bytes 368648 | tf_op jit(solution)/shard_map/ppermute | solution.py:249
  5.6 6.0 %collective-permute-start = (bf16[80,768]{1,0:T(8,128)(2,1)S(1)}, bf16[80,768]{1,0:T(8,128)(2,1)S(1)}, u32[]{:S(2)}, u32[]{:S(2)}) collective-permute-start(bf16[80,768]{1,0:T(8,128)(2,1)S(1)} %get-tuple-element.17.own_ref), channel_id=1, source_target_pairs={{0,6},{2,4},{4,2},{6,0},{8,14},{10,12},{12,10},{14,8},{1,7},{3,5},... | collective-permute-start | bytes 368648 | tf_op jit(solution)/shard_map/ppermute | solution.py:249
  5.7 5.4 %collective-permute-start.3 = (bf16[32,768]{1,0:T(8,128)(2,1)S(1)}, bf16[32,768]{1,0:T(8,128)(2,1)S(1)}, u32[]{:S(2)}, u32[]{:S(2)}) collective-permute-start(bf16[32,768]{1,0:T(8,128)(2,1)S(1)} %get-tuple-element.21), channel_id=1, source_target_pairs={{0,8},{1,13},{2,10},{3,15},{4,12},{5,9},{6,14},{7,11},{8,0},{9,5},... | collective-permute-start | bytes 147464 | tf_op jit(solution)/shard_map/ppermute | solution.py:256
  12.3 5.6 %collective-permute-start.4 = (bf16[32,896]{1,0:T(8,128)(2,1)S(1)}, bf16[32,896]{1,0:T(8,128)(2,1)S(1)}, u32[]{:S(2)}, u32[]{:S(2)}) collective-permute-start(bf16[32,896]{1,0:T(8,128)(2,1)S(1)} %shard_map.94), channel_id=1, source_target_pairs={{0,8},{1,13},{2,10},{3,15},{4,12},{5,9},{6,14},{7,11},{8,0},{9,5},... | collective-permute-start | bytes 172040 | tf_op jit(solution)/shard_map/ppermute | solution.py:256
  18.7 1.3 %collective-permute-start.5 = (bf16[8,3072]{1,0:T(8,128)(2,1)S(1)}, bf16[8,3072]{1,0:T(8,128)(2,1)S(1)}, u32[]{:S(2)}, u32[]{:S(2)}) collective-permute-start(bf16[8,3072]{1,0:T(8,128)(2,1)S(1)} %shard_map.97), channel_id=1, source_target_pairs={{0,1},{1,0},{2,3},{3,2},{4,5},{5,4},{6,7},{7,6},{8,9},{9,8},{10,11... | collective-permute-start | bytes 147464 | tf_op jit(solution)/shard_map/ppermute | solution.py:308
